TPU v7x, 256 devices: a whole 4x4x8 slice. The times are simulated.
256 devices in a mesh: terms: 8 (over x, z_lo), row: 4 (over y), col: 8 (over z_hi, core).
Axes of the slice: x: 4, y: 4, z: 8 (z_hi: 4, z_lo: 2; z = z_hi * 2 + z_lo), core: 2. Of those that a mesh axis runs over, the one named last changes fastest.
Arguments:
- psi: bfloat16 [2048, 2048], P('row', 'col'), may hold values from -6 to 6
- left_ops: bfloat16 [24, 2048, 2048], P('terms', 'row', 'col')
- right_ops_t: bfloat16 [24, 2048, 2048], P('terms', 'row', 'col')
- term_count: int32 [8], P('terms'), may hold values from 1 to 3, as said below
Outputs:
- sigma: bfloat16 [2048, 2048], P('row', 'col')
- residual: bfloat16 [2048, 2048], P('row', 'col')
- energy: float32 [], replicated
Inputs may be any that keep to these rules, and one draw needn't show every extreme that they name: Group g uses its first term_count[g] slots and ignores the others; some group uses all 3, another uses one.
All inputs are finite; a program needn't handle non-finite values.
Results may differ from a plain program's by a relative error of at most 0.0056.
Values may be sent and summed in bfloat16 or wider, within the bound.
No kernel may reach another device: no remote copies, remote signals or barrier semaphores. Data moves between devices by JAX's collectives and lax.ppermute only.
A program may use at most 64 MiB of HBM per device.

v0:
```python
import jax
import jax.numpy as jnp
from jax import lax
from jax.sharding import PartitionSpec as P


def per_device(psi, left_ops, right_ops_t, term_count):
    live_count = term_count[0]
    slots = left_ops.shape[0]
    tile_rows = psi.shape[0]
    tile_cols = psi.shape[1]
    psi_cols = lax.all_gather(psi, "row", axis=0, tiled=True)
    partial_sum = jnp.zeros((tile_rows, tile_cols), jnp.float32)
    for slot in range(slots):
        left = lax.dynamic_index_in_dim(left_ops, slot, 0, keepdims=False)
        right = lax.dynamic_index_in_dim(right_ops_t, slot, 0, keepdims=False)
        right_cols = lax.all_gather(right, "row", axis=0, tiled=True)
        mixed = jnp.dot(
            lax.all_gather(left, "col", axis=1, tiled=True),
            psi_cols,
            preferred_element_type=jnp.float32,
        ).astype(jnp.bfloat16)
        term = jnp.dot(
            lax.all_gather(mixed, "col", axis=1, tiled=True),
            right_cols,
            preferred_element_type=jnp.float32,
        )
        partial_sum = partial_sum + jnp.where(slot < live_count, term, jnp.float32(0.0))
    sigma_full = lax.psum(partial_sum, "terms")
    psi_wide = psi.astype(jnp.float32)
    above, below = lax.psum(
        (jnp.sum(psi_wide * sigma_full), jnp.sum(psi_wide * psi_wide)), ("row", "col")
    )
    energy = above / below
    sigma = sigma_full.astype(jnp.bfloat16)
    residual = (sigma_full - energy * psi_wide).astype(jnp.bfloat16)
    return (sigma, residual, energy)


def solution(mesh):
    in_specs = (P("row", "col"), P("terms", "row", "col"), P("terms", "row", "col"), P("terms"))
    out_specs = (P("row", "col"), P("row", "col"), P())
    return jax.shard_map(
        per_device, mesh=mesh, in_specs=in_specs, out_specs=out_specs, check_vma=False
    )
```

profile of v0, /device:TPU:2, one launch (start us, length us, event | category | flops | bytes accessed | tf_op | source)
XLA Modules:
  0.0 532.9 jit_solution(3331261424070907159)
XLA Ops:
  7.2 0.0 copy-start.1
  7.2 0.0 all-gather.17.cloned.1.call-start
  7.2 0.7 all-gather.17.cloned.1.call-update
  7.9 0.0 all-gather.29.cloned.1.call-start
  8.0 2.0 fusion.25
  10.0 0.0 all-gather.29.cloned.1.call-update
  10.0 0.0 all-gather.25.cloned.1.call-start
  10.1 0.7 all-gather.25.cloned.1.call-update
  10.7 0.0 all-gather.33.cloned.1.call-start
  10.8 0.5 all-gather.33.cloned.1.call-update
  11.3 0.0 all-gather.31.cloned.1.call-start
  11.4 0.0 copy-done.1
  11.4 0.9 fusion.24
  12.3 0.0 all-gather.31.cloned.1.call-update
  12.3 0.0 all-gather.21.cloned.1.call-start
  12.3 27.0 %all-gather.17.cloned.1.call-done = bf16[2048,256]{1,0:T(8,128)(2,1)} async-done(((bf16[512,256]{1,0:T(8,128)(2,1)}), bf16[2048,256]{1,0:T(8,128)(2,1)}) %all-gather.17.cloned.1.call-update) | async-done | bytes 1048592 | tf_op jit(solution)/shard_map/all_gather | solution.py:12
  39.3 42.9 %all-gather.29.cloned.1.call-done = bf16[1,512,2048]{2,1,0:T(8,128)(2,1)} async-done(((bf16[1,512,256]{2,1,0:T(8,128)(2,1)}), bf16[1,512,2048]{2,1,0:T(8,128)(2,1)}) %all-gather.29.cloned.1.call-update) | async-done | bytes 2097168 | tf_op jit(solution)/shard_map/all_gather | solution.py:19
  82.3 3.3 fusion.11
  85.5 0.0 all-gather.21.cloned.1.call-update
  85.6 0.0 all-gather.27.cloned.1.call-start
  85.6 0.7 all-gather.27.cloned.1.call-update
  86.3 0.0 all-gather.19.cloned.1.call-start
  86.4 36.3 %all-gather.25.cloned.1.call-done = bf16[1,512,2048]{2,1,0:T(8,128)(2,1)} async-done(((bf16[1,512,256]{2,1,0:T(8,128)(2,1)}), bf16[1,512,2048]{2,1,0:T(8,128)(2,1)}) %all-gather.25.cloned.1.call-update) | async-done | bytes 2097168 | tf_op jit(solution)/shard_map/all_gather | solution.py:19
  122.7 0.0 copy-done.2
  122.7 3.0 fusion.8
  125.7 0.0 all-gather.19.cloned.1.call-update
  125.7 0.0 all-gather.35.cloned.1.call-start
  125.8 0.7 all-gather.35.cloned.1.call-update
  126.5 0.0 all-gather.23.cloned.1.call-start
  126.5 36.5 %all-gather.33.cloned.1.call-done = bf16[1,512,2048]{2,1,0:T(8,128)(2,1)} async-done(((bf16[1,512,256]{2,1,0:T(8,128)(2,1)}), bf16[1,512,2048]{2,1,0:T(8,128)(2,1)}) %all-gather.33.cloned.1.call-update) | async-done | bytes 2097168 | tf_op jit(solution)/shard_map/all_gather | solution.py:19
  163.0 3.0 fusion.14
  166.0 0.0 all-gather.23.cloned.1.call-update
  166.0 0.0 all-reduce.3.cloned.1.call-start
  166.7 21.8 %all-gather.31.cloned.1.call-done = bf16[1,2048,256]{2,1,0:T(8,128)(2,1)} async-done(((bf16[1,512,256]{2,1,0:T(8,128)(2,1)}), bf16[1,2048,256]{2,1,0:T(8,128)(2,1)}) %all-gather.31.cloned.1.call-update) | async-done | bytes 1048592 | tf_op jit(solution)/shard_map/all_gather | solution.py:17
  188.5 42.8 %all-gather.21.cloned.1.call-done = bf16[512,2048]{1,0:T(8,128)(2,1)} async-done(((bf16[512,256]{1,0:T(8,128)(2,1)}), bf16[512,2048]{1,0:T(8,128)(2,1)}) %all-gather.21.cloned.1.call-update) | async-done | bytes 2097168 | tf_op jit(solution)/shard_map/all_gather | solution.py:24
  231.3 2.6 convolution_select_fusion.1
  233.9 23.1 %all-gather.27.cloned.1.call-done = bf16[1,2048,256]{2,1,0:T(8,128)(2,1)} async-done(((bf16[1,512,256]{2,1,0:T(8,128)(2,1)}), bf16[1,2048,256]{2,1,0:T(8,128)(2,1)}) %all-gather.27.cloned.1.call-update) | async-done | bytes 1048592 | tf_op jit(solution)/shard_map/all_gather | solution.py:17
  257.0 43.5 %all-gather.19.cloned.1.call-done = bf16[512,2048]{1,0:T(8,128)(2,1)} async-done(((bf16[512,256]{1,0:T(8,128)(2,1)}), bf16[512,2048]{1,0:T(8,128)(2,1)}) %all-gather.19.cloned.1.call-update) | async-done | bytes 2097168 | tf_op jit(solution)/shard_map/all_gather | solution.py:24
  300.5 2.6 fusion.6
  303.0 23.1 %all-gather.35.cloned.1.call-done = bf16[1,2048,256]{2,1,0:T(8,128)(2,1)} async-done(((bf16[1,512,256]{2,1,0:T(8,128)(2,1)}), bf16[1,2048,256]{2,1,0:T(8,128)(2,1)}) %all-gather.35.cloned.1.call-update) | async-done | bytes 1048592 | tf_op jit(solution)/shard_map/all_gather | solution.py:17
  326.1 43.3 %all-gather.23.cloned.1.call-done = bf16[512,2048]{1,0:T(8,128)(2,1)} async-done(((bf16[512,256]{1,0:T(8,128)(2,1)}), bf16[512,2048]{1,0:T(8,128)(2,1)}) %all-gather.23.cloned.1.call-update) | async-done | bytes 2097168 | tf_op jit(solution)/shard_map/all_gather | solution.py:24
  369.5 3.4 fusion.7
  372.9 0.0 all-reduce.3.cloned.1.call-update
  372.9 76.3 %all-reduce.3.cloned.1.call-done = f32[512,256]{1,0:T(8,128)} async-done(((f32[512,256]{1,0:T(8,128)}), f32[512,256]{1,0:T(8,128)}) %all-reduce.3.cloned.1.call-update) | async-done | bytes 524304 | tf_op jit(solution)/shard_map/psum | solution.py:29
  449.2 0.0 copy-done
  449.2 1.8 fusion.21
  451.0 70.9 %all-reduce = (f32[]{:T(128)}, f32[]{:T(128)}) all-reduce(f32[]{:T(128)} %get-tuple-element.4, f32[]{:T(128)} %get-tuple-element.3), channel_id=1, replica_groups=mesh['terms'=8,'row'=4,'col'=8] {'row','col'}, use_global_device_ids=true, to_apply=%region_2.3 | all-reduce | flops 2 | bytes 16 | tf_op jit(solution)/shard_map/psum | solution.py:31
  523.2 2.1 fusion.23
  (2 shorter events, 0.0 us)
Async XLA Ops:
  7.2 4.2 copy-start.1
  7.2 32.2 %all-gather.17.cloned.1.call-start = ((), (), s32[]{:S(2)}) async-start(), calls=%async_computation | async-start | bytes 1310720 | tf_op jit(solution)/shard_map/all_gather | solution.py:12
  7.9 74.4 %all-gather.29.cloned.1.call-start = ((), (), s32[]{:S(2)}) async-start(), calls=%async_computation.7 | async-start | bytes 2359296 | tf_op jit(solution)/shard_map/all_gather | solution.py:19
  10.0 112.7 %all-gather.25.cloned.1.call-start = ((), (), s32[]{:S(2)}) async-start(), calls=%async_computation.5 | async-start | bytes 2359296 | tf_op jit(solution)/shard_map/all_gather | solution.py:19
  10.7 152.3 %all-gather.33.cloned.1.call-start = ((), (), s32[]{:S(2)}) async-start(), calls=%async_computation.9 | async-start | bytes 2359296 | tf_op jit(solution)/shard_map/all_gather | solution.py:19
  11.3 177.2 %all-gather.31.cloned.1.call-start = ((), (), s32[]{:S(2)}) async-start(), calls=%async_computation.8 | async-start | bytes 1310720 | tf_op jit(solution)/shard_map/all_gather | solution.py:17
  12.3 219.0 %all-gather.21.cloned.1.call-start = ((), (), s32[]{:S(2)}) async-start(), calls=%async_computation.2 | async-start | bytes 2359296 | tf_op jit(solution)/shard_map/all_gather | solution.py:24
  39.3 83.4 %copy-start.2 = (bf16[2048,256]{1,0:T(8,128)(2,1)S(1)}, bf16[2048,256]{1,0:T(8,128)(2,1)}, u32[]{:S(2)}) copy-start(bf16[2048,256]{1,0:T(8,128)(2,1)} %all-gather.17.cloned.1.call-done) | copy-start | bytes 3145732
  85.6 171.4 %all-gather.27.cloned.1.call-start = ((), (), s32[]{:S(2)}) async-start(), calls=%async_computation.6 | async-start | bytes 1310720 | tf_op jit(solution)/shard_map/all_gather | solution.py:17
  86.3 214.1 %all-gather.19.cloned.1.call-start = ((), (), s32[]{:S(2)}) async-start(), calls=%async_computation.1 | async-start | bytes 2359296 | tf_op jit(solution)/shard_map/all_gather | solution.py:24
  125.7 200.4 %all-gather.35.cloned.1.call-start = ((), (), s32[]{:S(2)}) async-start(), calls=%async_computation.10 | async-start | bytes 1310720 | tf_op jit(solution)/shard_map/all_gather | solution.py:17
  126.5 243.0 %all-gather.23.cloned.1.call-start = ((), (), s32[]{:S(2)}) async-start(), calls=%async_computation.3 | async-start | bytes 2359296 | tf_op jit(solution)/shard_map/all_gather | solution.py:24
  166.0 283.1 %all-reduce.3.cloned.1.call-start = ((), (), s32[]{:S(2)}) async-start(), calls=%async_computation.4 | async-start | bytes 1048576 | tf_op jit(solution)/shard_map/psum | solution.py:29
  369.5 79.7 %copy-start = (bf16[512,256]{1,0:T(8,128)(2,1)S(1)}, bf16[512,256]{1,0:T(8,128)(2,1)}, u32[]{:S(2)}) copy-start(bf16[512,256]{1,0:T(8,128)(2,1)} %param.4) | copy-start | bytes 786436
Sparse Core Ops, SparseCore 0:
  9.8 29.4 all-gather.16
  41.2 41.0 all-gather.28
  84.7 38.0 all-gather.24
  125.0 38.0 all-gather.32
  164.7 23.8 all-gather.30
  190.2 41.0 all-gather.20
  233.1 23.8 all-gather.26
  259.4 41.0 all-gather.18
  302.3 23.8 all-gather.34
  328.4 41.0 all-gather.22
  373.0 76.0 all-reduce.2
where the time goes:
time: 535 us; the launch traced here: 533 us
  waiting for transfers between devices  420 us (79%)
  blocking collectives  70.9 us (13%)
  matrix products  17.8 us (3%)
  between operations  17 us (3%)
    all_gather x3, waiting for transfers between devices, per_device(): lax.all_gather(mixed, 'col', axis=1, tiled=True)  130 us
    all_gather x3, waiting for transfers between devices, per_device(): lax.all_gather(left, 'col', axis=1, tiled=True)  116 us
    psum x1, waiting for transfers between devices, per_device(): sigma_full = lax.psum(partial_sum, 'terms')  76.3 us
    psum x1, blocking collectives, per_device(): lax.psum((jnp.sum(psi_wide * sigma_full), jnp.sum(psi_wide * psi_wide)),...  70.9 us
    all_gather x3, waiting for transfers between devices, per_device(): right_cols = lax.all_gather(right, 'row', axis=0, tiled=True)  68 us
    all_gather x1, waiting for transfers between devices, per_device(): psi_cols = lax.all_gather(psi, 'row', axis=0, tiled=True)  27 us
  transfers between devices with their start and end apart: 11, of which 11 were waited for; matrix products, arithmetic and copies ran while one was open for 3% of the time, Pallas kernels for 0%

commit v1 on v0

v1 whole, which is shorter than its diff:
```python
import jax
import jax.numpy as jnp
from jax import lax
from jax.experimental import pallas as pl
from jax.experimental.pallas import tpu as pltpu
from jax.sharding import Mesh, PartitionSpec as P

TERMS = ("x", "zlo")
BF16, F32 = jnp.bfloat16, jnp.float32
ANY = pl.BlockSpec(memory_space=pl.ANY)
SMEM = pl.BlockSpec(memory_space=pltpu.SMEM)
VMEM = pl.BlockSpec(memory_space=pltpu.VMEM)


def shift(x, axis, n, k):
    return lax.ppermute(x, axis, [(i, (i + k) % n) for i in range(n)])


def gather(x, axis, dim):
    half = x.shape[dim] // 2
    before = shift(x, axis, 4, 1)
    after = shift(x, axis, 4, 3)
    low = shift(lax.slice_in_dim(before, 0, half, axis=dim), axis, 4, 1)
    high = shift(lax.slice_in_dim(after, half, 2 * half, axis=dim), axis, 4, 3)
    return after, low, high, before


def first_kernel(place, own, sib, r0, r1, r2a, r2b, r3, keep, send, psi_buf, r_buf, sems):
    m, l, c = place[0], place[1], place[2]
    copies = [
        pltpu.make_async_copy(own, psi_buf.at[c], sems.at[0]),
        pltpu.make_async_copy(sib, psi_buf.at[1 - c], sems.at[1]),
        pltpu.make_async_copy(r0, r_buf.at[0], sems.at[2]),
        pltpu.make_async_copy(r1, r_buf.at[1], sems.at[3]),
        pltpu.make_async_copy(r2a, r_buf.at[2, :, pl.ds(0, 256)], sems.at[4]),
        pltpu.make_async_copy(r2b, r_buf.at[2, :, pl.ds(256, 256)], sems.at[5]),
        pltpu.make_async_copy(r3, r_buf.at[3], sems.at[6]),
    ]
    for copy in copies:
        copy.start()
    for copy in copies:
        copy.wait()
    for s in range(3):
        for out, half in ((keep, c), (send, 1 - c)):
            total = jnp.zeros((256, 256), F32)
            for d in range(4):
                e = lax.rem(m + d - l + 4, 4)
                rows = pl.ds(pl.multiple_of(e * 512 + half * 256, 256), 256)
                for h in range(2):
                    total += jnp.dot(
                        psi_buf[h, rows, :],
                        r_buf[d, s, h * 256 : (h + 1) * 256, :],
                        preferred_element_type=F32,
                    )
            out[s] = total.astype(BF16)


def second_kernel(place, l0, l1, l2a, l2b, l3, w0, w1, w2a, w2b, w3, own, sib, mine, theirs, dots, l_buf, w_buf, psi_buf, sems):
    m, l, live = place[0], place[1], place[3]
    copies = [
        pltpu.make_async_copy(l0, l_buf.at[0], sems.at[0]),
        pltpu.make_async_copy(l1, l_buf.at[1], sems.at[1]),
        pltpu.make_async_copy(l2a, l_buf.at[2, :, pl.ds(0, 256)], sems.at[2]),
        pltpu.make_async_copy(l2b, l_buf.at[2, :, pl.ds(256, 256)], sems.at[3]),
        pltpu.make_async_copy(l3, l_buf.at[3], sems.at[4]),
        pltpu.make_async_copy(w0, w_buf.at[0], sems.at[5]),
        pltpu.make_async_copy(w1, w_buf.at[1], sems.at[6]),
        pltpu.make_async_copy(w2a, w_buf.at[2, :, :, pl.ds(0, 128)], sems.at[7]),
        pltpu.make_async_copy(w2b, w_buf.at[2, :, :, pl.ds(128, 128)], sems.at[8]),
        pltpu.make_async_copy(w3, w_buf.at[3], sems.at[9]),
        pltpu.make_async_copy(own.at[pl.ds(0, 512)], psi_buf.at[0], sems.at[10]),
        pltpu.make_async_copy(sib.at[pl.ds(0, 512)], psi_buf.at[1], sems.at[11]),
    ]
    for copy in copies:
        copy.start()
    for copy in copies:
        copy.wait()
    above = jnp.zeros((8, 256), F32)
    for h, out in ((0, mine), (1, theirs)):
        for block in range(2):
            rows = slice(block * 256, (block + 1) * 256)
            out[rows] = jnp.zeros((256, 256), F32)
            for s in range(3):

                @pl.when(s < live)
                def _(s=s, h=h, rows=rows, out=out):
                    total = out[rows]
                    for e in range(4):
                        d = lax.rem(l + e - m + 4, 4)
                        total += jnp.dot(
                            l_buf[e, s, rows, :], w_buf[d, h, s], preferred_element_type=F32
                        )
                    out[rows] = total

            product = out[rows] * psi_buf[h, rows, :].astype(F32)
            above += product.reshape(32, 8, 256).sum(0)
    wide = psi_buf[0].astype(F32)
    below = (wide * wide).reshape(64, 8, 256).sum(0)
    dots[0:8] = above
    dots[8:16] = below


def per_device(psi, left_ops, right_ops_t, term_count):
    m, l, c = lax.axis_index("row"), lax.axis_index("zhi"), lax.axis_index("core")
    place = jnp.stack([m, l, c, term_count[0]]).astype(jnp.int32)

    p1, p2a, p2b, p3 = gather(psi, "zhi", 0)
    own = jnp.concatenate([psi, p1, p2a, p2b, p3], axis=0)
    sib = shift(own, "core", 2, 1)

    r1, r2a, r2b, r3 = gather(right_ops_t, "row", 1)
    left, _ = lax.optimization_barrier((left_ops, p3))
    l1, l2a, l2b, l3 = gather(left, "zhi", 1)

    keep, send = pl.pallas_call(
        first_kernel,
        out_shape=[jax.ShapeDtypeStruct((3, 256, 256), BF16)] * 2,
        in_specs=[SMEM] + [ANY] * 7,
        out_specs=[VMEM] * 2,
        scratch_shapes=[
            pltpu.VMEM((2, 2048, 256), BF16),
            pltpu.VMEM((4, 3, 512, 256), BF16),
            pltpu.SemaphoreType.DMA((7,)),
        ],
        compiler_params=pltpu.CompilerParams(vmem_limit_bytes=24 << 20),
        cost_estimate=pl.CostEstimate(flops=3 * 2 * 512 * 2048 * 256, bytes_accessed=6 << 20, transcendentals=0),
    )(place, own, sib, right_ops_t, r1, r2a, r2b, r3)

    w = jnp.stack([keep, shift(send, "core", 2, 1)])
    w1, w2a, w2b, w3 = gather(w, "row", 2)

    mine, theirs, dots = pl.pallas_call(
        second_kernel,
        out_shape=[jax.ShapeDtypeStruct((512, 256), F32)] * 2 + [jax.ShapeDtypeStruct((16, 256), F32)],
        in_specs=[SMEM] + [ANY] * 12,
        out_specs=[VMEM] * 3,
        scratch_shapes=[
            pltpu.VMEM((4, 3, 512, 256), BF16),
            pltpu.VMEM((4, 2, 3, 256, 256), BF16),
            pltpu.VMEM((2, 512, 256), BF16),
            pltpu.SemaphoreType.DMA((12,)),
        ],
        compiler_params=pltpu.CompilerParams(vmem_limit_bytes=24 << 20),
        cost_estimate=pl.CostEstimate(flops=3 * 2 * 512 * 1024 * 512, bytes_accessed=8 << 20, transcendentals=0),
    )(place, left_ops, l1, l2a, l2b, l3, w, w1, w2a, w2b, w3, own, sib)

    partial = mine + shift(theirs, "core", 2, 1)
    sums = jnp.stack([dots[:8].sum(), dots[8:].sum()])
    sums = jnp.broadcast_to(jnp.pad(sums, (0, 6))[:, None], (8, 256))
    payload = jnp.concatenate(
        [partial.reshape(8, 64, 256), jnp.broadcast_to(sums, (8, 8, 256))], axis=1
    )
    reduced = lax.all_to_all(payload, TERMS, 0, 0, tiled=True).sum(0)
    chunk, sums = reduced[:64], reduced[64:, :128]
    sums = sums + shift(sums, "row", 4, 1) + shift(sums, "row", 4, 2) + shift(sums, "row", 4, 3)
    sigma_full = lax.all_to_all(
        jnp.broadcast_to(chunk, (8, 64, 256)), TERMS, 0, 0, tiled=True
    ).reshape(512, 256)
    sums = sums + shift(sums, "zhi", 4, 1) + shift(sums, "zhi", 4, 2) + shift(sums, "zhi", 4, 3)
    sums = sums + shift(sums, "core", 2, 1)
    energy = sums[0, 0] / (sums[1, 0] * F32(0.125))
    residual = (sigma_full - energy * psi.astype(F32)).astype(BF16)
    return sigma_full.astype(BF16), residual, energy


def solution(mesh):
    fine = Mesh(mesh.devices.reshape(4, 2, 4, 4, 2), ("x", "zlo", "row", "zhi", "core"))
    col = ("zhi", "core")
    in_specs = (P("row", col), P(TERMS, "row", col), P(TERMS, "row", col), P(TERMS))
    out_specs = (P("row", col), P("row", col), P())
    return jax.shard_map(
        per_device, mesh=fine, in_specs=in_specs, out_specs=out_specs, check_vma=False
    )
```

time: 535 us -> 167 us (0.31)
  waiting for transfers between devices: 420 us -> 78 us
  blocking collectives: 70.9 us -> 17.2 us
  starting transfers between devices: 0.44 us -> 51.2 us
  matrix products: 17.8 us -> 0 us
  between operations: 17 us -> 3.92 us
  Pallas kernels: 0 us -> 6.32 us
    all_gather x10 -> x0, waiting for transfers between devices: 340 us -> none  [the longest x3 130 us: per_device(): lax.all_gather(mixed, 'col', axis=1, tiled=True)]
    ppermute x0 -> x26, waiting for transfers between devices: none -> 78 us  [shift(): return lax.ppermute(x, axis, [(i, (i + k) % n) for i in range(n)])]
    psum x1 -> x0, waiting for transfers between devices: 76.3 us -> none  [per_device(): sigma_full = lax.psum(partial_sum, 'terms')]
    psum x1 -> x0, blocking collectives: 70.9 us -> none  [per_device(): lax.psum((jnp.sum(psi_wide * sigma_full), jnp.sum(psi_wide * psi_wide)),...]
    ppermute x0 -> x26, starting transfers between devices: none -> 46.4 us  [shift(): return lax.ppermute(x, axis, [(i, (i + k) % n) for i in range(n)])]
    dot_general x6 -> x0, matrix products: 17.8 us -> none  [the longest x3 9.29 us: per_device(): jnp.dot(lax.all_gather(left, 'col', axis=1, tiled=True), psi_cols, prefer...]
    all_to_all x0 -> x1, blocking collectives: none -> 17.2 us  [per_device(): reduced = lax.all_to_all(payload, TERMS, 0, 0, tiled=True).sum(0)]
    pallas_call x0 -> x2, Pallas kernels: none -> 6.32 us  [the longest x1 3.64 us: per_device(): pl.pallas_call(first_kernel, out_shape=[jax.ShapeDtypeStruct((3, 256, 256...]
  transfers between devices with their start and end apart: 11 -> 27, of which waited for: 11 -> 14; matrix products, arithmetic and copies ran while one was open for 3% -> 3% of each run, Pallas kernels for 0% -> 0%
where the time goes in v1:
time: 167 us
  waiting for transfers between devices  78 us (47%)
  starting transfers between devices  51.2 us (31%)
  blocking collectives  17.2 us (10%)
  local copies, waits for them, and re-layouts  6.43 us (4%)
  Pallas kernels  6.32 us (4%)
  between operations  3.92 us (2%)
  other arithmetic  3.85 us (2%)
    ppermute x26, waiting for transfers between devices, shift(): return lax.ppermute(x, axis, [(i, (i + k) % n) for i in range(n)])  78 us
    ppermute x26, starting transfers between devices, shift(): return lax.ppermute(x, axis, [(i, (i + k) % n) for i in range(n)])  46.4 us
    all_to_all x1, blocking collectives, per_device(): reduced = lax.all_to_all(payload, TERMS, 0, 0, tiled=True).sum(0)  17.2 us
    all_to_all x1, starting transfers between devices, per_device(): lax.all_to_all(jnp.broadcast_to(chunk, (8, 64, 256)), TERMS, 0, 0, tiled=...  4.86 us
    pallas_call x1, Pallas kernels, per_device(): pl.pallas_call(first_kernel, out_shape=[jax.ShapeDtypeStruct((3, 256, 256...  3.64 us
  transfers between devices with their start and end apart: 27, of which 14 were waited for; matrix products, arithmetic and copies ran while one was open for 3% of the time, Pallas kernels for 0%

profile of v1, /device:TPU:2, one launch (start us, length us, event | category | flops | bytes accessed | tf_op | source)
XLA Modules:
  0.0 167.0 jit_solution(6581030833594477301)
XLA Ops:
  0.6 3.3 %collective-permute-start = (bf16[512,256]{1,0:T(8,128)(2,1)}, bf16[512,256]{1,0:T(8,128)(2,1)S(1)}, u32[]{:S(2)}, u32[]{:S(2)}) collective-permute-start(bf16[512,256]{1,0:T(8,128)(2,1)} %param.4), channel_id=1, source_target_pairs={{0,2},{2,4},{4,6},{6,0},{1,3},{3,5},{5,7},{7,1},{8,10},{10,12},{12... | collective-permute-start | bytes 786440 | tf_op jit(solution)/shard_map/ppermute | solution.py:16
  4.0 3.1 %collective-permute-start.5 = (bf16[512,256]{1,0:T(8,128)(2,1)}, bf16[512,256]{1,0:T(8,128)(2,1)S(1)}, u32[]{:S(2)}, u32[]{:S(2)}) collective-permute-start(bf16[512,256]{1,0:T(8,128)(2,1)} %param.4), channel_id=1, source_target_pairs={{0,6},{2,0},{4,2},{6,4},{1,7},{3,1},{5,3},{7,5},{8,14},{10,8},{12,... | collective-permute-start | bytes 786440 | tf_op jit(solution)/shard_map/ppermute | solution.py:16
  7.1 3.0 %collective-permute-start.9 = (bf16[3,512,256]{2,1,0:T(8,128)(2,1)}, bf16[3,512,256]{2,1,0:T(8,128)(2,1)S(1)}, u32[]{:S(2)}, u32[]{:S(2)}) collective-permute-start(bf16[3,512,256]{2,1,0:T(8,128)(2,1)} %r0.1), channel_id=1, source_target_pairs={{0,24},{8,0},{16,8},{24,16},{1,25},{9,1},{17,9},{25,17},{2,26},{10... | collective-permute-start | bytes 2359304 | tf_op jit(solution)/shard_map/ppermute | solution.py:16
  10.1 5.4 %collective-permute-done = bf16[512,256]{1,0:T(8,128)(2,1)S(1)} collective-permute-done((bf16[512,256]{1,0:T(8,128)(2,1)}, bf16[512,256]{1,0:T(8,128)(2,1)S(1)}, u32[]{:S(2)}, u32[]{:S(2)}) %collective-permute-start) | collective-permute-done | bytes 262176 | tf_op jit(solution)/shard_map/ppermute | solution.py:16
  15.5 4.4 %collective-permute-start.6 = (bf16[256,256]{1,0:T(8,128)(2,1)S(1)}, bf16[256,256]{1,0:T(8,128)(2,1)S(1)}, u32[]{:S(2)}, u32[]{:S(2)}) collective-permute-start(bf16[256,256]{1,0:T(8,128)(2,1)S(1)} %slice.58), channel_id=1, source_target_pairs={{0,2},{2,4},{4,6},{6,0},{1,3},{3,5},{5,7},{7,1},{8,10},{10,12},{12... | collective-permute-start | bytes 393224 | tf_op jit(solution)/shard_map/ppermute | solution.py:16
  20.0 0.4 collective-permute-done.5
  20.4 2.8 %collective-permute-start.7 = (bf16[256,256]{1,0:T(8,128)(2,1)S(1)}, bf16[256,256]{1,0:T(8,128)(2,1)S(1)}, u32[]{:S(2)}, u32[]{:S(2)}) collective-permute-start(bf16[256,256]{1,0:T(8,128)(2,1)S(1)} %slice.59), channel_id=1, source_target_pairs={{0,6},{2,0},{4,2},{6,4},{1,7},{3,1},{5,3},{7,5},{8,14},{10,8},{12,... | collective-permute-start | bytes 393224 | tf_op jit(solution)/shard_map/ppermute | solution.py:16
  23.2 4.5 %collective-permute-done.6 = bf16[256,256]{1,0:T(8,128)(2,1)S(1)} collective-permute-done((bf16[256,256]{1,0:T(8,128)(2,1)S(1)}, bf16[256,256]{1,0:T(8,128)(2,1)S(1)}, u32[]{:S(2)}, u32[]{:S(2)}) %collective-permute-start.6) | collective-permute-done | bytes 131104 | tf_op jit(solution)/shard_map/ppermute | solution.py:16
  27.7 1.5 collective-permute-done.7
  29.4 0.8 slice.61
  30.2 3.0 %collective-permute-start.12 = (bf16[3,256,256]{2,1,0:T(8,128)(2,1)}, bf16[3,256,256]{2,1,0:T(8,128)(2,1)S(1)}, u32[]{:S(2)}, u32[]{:S(2)}) collective-permute-start(bf16[3,256,256]{2,1,0:T(8,128)(2,1)} %slice.61), channel_id=1, source_target_pairs={{0,24},{8,0},{16,8},{24,16},{1,25},{9,1},{17,9},{25,17},{2,26},{10... | collective-permute-start | bytes 1179656 | tf_op jit(solution)/shard_map/ppermute | solution.py:16
  33.2 0.8 slice.60
  34.0 0.9 copy-done.1
  35.6 6.9 %collective-permute-done.12.r2b = bf16[3,256,256]{2,1,0:T(8,128)(2,1)S(1)} collective-permute-done((bf16[3,256,256]{2,1,0:T(8,128)(2,1)}, bf16[3,256,256]{2,1,0:T(8,128)(2,1)S(1)}, u32[]{:S(2)}, u32[]{:S(2)}) %collective-permute-start.12) | collective-permute-done | bytes 393248 | tf_op jit(solution)/shard_map/ppermute | solution.py:16
  42.6 5.1 %collective-permute-done.11.r2a = bf16[3,256,256]{2,1,0:T(8,128)(2,1)} collective-permute-done((bf16[3,256,256]{2,1,0:T(8,128)(2,1)}, bf16[3,256,256]{2,1,0:T(8,128)(2,1)}, u32[]{:S(2)}, u32[]{:S(2)}) %collective-permute-start.11) | collective-permute-done | bytes 393248 | tf_op jit(solution)/shard_map/ppermute | solution.py:16
  47.7 1.1 copy-done.2
  48.8 1.1 copy-done.3
  49.9 3.6 %shard_map.67 = (bf16[3,256,256]{2,1,0:T(8,128)(2,1)S(1)}, bf16[3,256,256]{2,1,0:T(8,128)(2,1)S(1)}) custom-call(s32[4]{0:T(128)S(1)} %pad_add_fusion.place, bf16[2048,256]{1,0:T(8,128)(2,1)S(1)} %constant_dynamic-update-slice_fusion.own, bf16[2048,256]{1,0:T(8,128)(2,1)S(1)} %collective-permute-done.8.sib, bf16[3,512,256]{2,1,0:T(8,128)(2,1)S(1)} %copy-done.3, ...), custom_call_target="tpu_custom_call" | custom-call | flops 1610612736 | bytes 6291456 | tf_op jit(solution)/shard_map/pallas_call | solution.py:115
  53.6 0.1 collective-permute-start.13
  53.7 3.5 %collective-permute-start.2 = (bf16[3,512,256]{2,1,0:T(8,128)(2,1)S(1)}, bf16[3,512,256]{2,1,0:T(8,128)(2,1)S(1)}, u32[]{:S(2)}, u32[]{:S(2)}) collective-permute-start(bf16[3,512,256]{2,1,0:T(8,128)(2,1)S(1)} %copy-done), channel_id=1, source_target_pairs={{0,2},{2,4},{4,6},{6,0},{1,3},{3,5},{5,7},{7,1},{8,10},{10,12},{12... | collective-permute-start | bytes 2359304 | tf_op jit(solution)/shard_map/ppermute | solution.py:16
  57.2 0.7 collective-permute-start.1
  58.1 3.2 %collective-permute-start.14 = (bf16[2,3,256,256]{3,2,1,0:T(8,128)(2,1)S(1)}, bf16[2,3,256,256]{3,2,1,0:T(8,128)(2,1)S(1)}, u32[]{:S(2)}, u32[]{:S(2)}) collective-permute-start(bf16[2,3,256,256]{3,2,1,0:T(8,128)(2,1)S(1)} %pad_maximum_fusion.w0), channel_id=1, source_target_pairs={{0,24},{8,0},{16,8},{24,16},{1,25},{9,1},{17,9},{25,17},{2,26},{10... | collective-permute-start | bytes 2359304 | tf_op jit(solution)/shard_map/ppermute | solution.py:16
  61.3 28.0 %collective-permute-done.2.l3 = bf16[3,512,256]{2,1,0:T(8,128)(2,1)S(1)} collective-permute-done((bf16[3,512,256]{2,1,0:T(8,128)(2,1)S(1)}, bf16[3,512,256]{2,1,0:T(8,128)(2,1)S(1)}, u32[]{:S(2)}, u32[]{:S(2)}) %collective-permute-start.2) | collective-permute-done | bytes 786464 | tf_op jit(solution)/shard_map/ppermute | solution.py:16
  89.3 5.8 %collective-permute-start.3 = (bf16[3,256,256]{2,1,0:T(8,128)(2,1)S(1)}, bf16[3,256,256]{2,1,0:T(8,128)(2,1)S(1)}, u32[]{:S(2)}, u32[]{:S(2)}) collective-permute-start(bf16[3,256,256]{2,1,0:T(8,128)(2,1)S(1)} %slice.56), channel_id=1, source_target_pairs={{0,2},{2,4},{4,6},{6,0},{1,3},{3,5},{5,7},{7,1},{8,10},{10,12},{12... | collective-permute-start | bytes 1179656 | tf_op jit(solution)/shard_map/ppermute | solution.py:16
  95.1 1.4 collective-permute-start.4
  96.7 3.3 %collective-permute-start.17 = (bf16[2,3,128,256]{3,2,1,0:T(8,128)(2,1)S(1)}, bf16[2,3,128,256]{3,2,1,0:T(8,128)(2,1)S(1)}, u32[]{:S(2)}, u32[]{:S(2)}) collective-permute-start(bf16[2,3,128,256]{3,2,1,0:T(8,128)(2,1)S(1)} %slice.63), channel_id=1, source_target_pairs={{0,24},{8,0},{16,8},{24,16},{1,25},{9,1},{17,9},{25,17},{2,26},{10... | collective-permute-start | bytes 1179656 | tf_op jit(solution)/shard_map/ppermute | solution.py:16
  100.0 2.5 %collective-permute-done.3.l2a = bf16[3,256,256]{2,1,0:T(8,128)(2,1)S(1)} collective-permute-done((bf16[3,256,256]{2,1,0:T(8,128)(2,1)S(1)}, bf16[3,256,256]{2,1,0:T(8,128)(2,1)S(1)}, u32[]{:S(2)}, u32[]{:S(2)}) %collective-permute-start.3) | collective-permute-done | bytes 393248 | tf_op jit(solution)/shard_map/ppermute | solution.py:16
  102.6 12.3 %collective-permute-done.4.l2b = bf16[3,256,256]{2,1,0:T(8,128)(2,1)S(1)} collective-permute-done((bf16[3,256,256]{2,1,0:T(8,128)(2,1)S(1)}, bf16[3,256,256]{2,1,0:T(8,128)(2,1)S(1)}, u32[]{:S(2)}, u32[]{:S(2)}) %collective-permute-start.4) | collective-permute-done | bytes 393248 | tf_op jit(solution)/shard_map/ppermute | solution.py:16
  114.9 2.7 %shard_map.68 = (f32[512,256]{1,0:T(8,128)S(1)}, f32[512,256]{1,0:T(8,128)S(1)}, f32[16,256]{1,0:T(8,128)S(1)}) custom-call(s32[4]{0:T(128)S(1)} %pad_add_fusion.place, bf16[3,512,256]{2,1,0:T(8,128)(2,1)S(1)} %copy-done, bf16[3,512,256]{2,1,0:T(8,128)(2,1)S(1)} %collective-permute-done.1.l1, bf16[3,256,256]{2,1,0:T(8,128)(2,1)S(1)} %collective-permute-done.3.l2a, ...), custom_call_target="tpu_custom_call" | custom-call | flops 1610612736 | bytes 8388608 | tf_op jit(solution)/shard_map/pallas_call | solution.py:132
  117.6 0.1 collective-permute-start.18
  117.7 0.6 slice_reduce_fusion.1
  118.3 1.4 fusion.1
  119.8 0.1 pad_maximum_fusion.1
  119.9 17.2 %all_to_all.10 = f32[8,72,256]{2,1,0:T(8,128)S(1)} all-to-all(f32[8,72,256]{2,1,0:T(8,128)S(1)} %pad_maximum_fusion.1), channel_id=1, replica_groups=mesh['x'=4,'zlo'=2,'row'=4,'zhi'=4,'core'=2] {'x','zlo'}, dimensions={0} | all-to-all | bytes 1179648 | tf_op jit(solution)/shard_map/all_to_all | solution.py:153
  137.1 0.9 broadcast_in_dim.4
  138.0 4.9 %all-to-all-start.1 = ((f32[8,64,256]{2,1,0:T(8,128)}), f32[8,64,256]{2,1,0:T(8,128)S(1)}, u32[]{:S(2)}, u32[]{:S(2)}) async-start(f32[8,64,256]{2,1,0:T(8,128)} %broadcast_in_dim.4), calls=%async_computation.1 | async-start | bytes 1048576 | tf_op jit(solution)/shard_map/all_to_all | solution.py:156
  142.9 1.7 %collective-permute-start.21 = (f32[8,128]{1,0:T(8,128)S(1)}, f32[8,128]{1,0:T(8,128)S(1)}, u32[]{:S(2)}, u32[]{:S(2)}) collective-permute-start(f32[8,128]{1,0:T(8,128)S(1)} %slice.65), channel_id=1, source_target_pairs={{0,24},{8,0},{16,8},{24,16},{1,25},{9,1},{17,9},{25,17},{2,26},{10... | collective-permute-start | bytes 12296 | tf_op jit(solution)/shard_map/ppermute | solution.py:16
  144.6 0.4 collective-permute-start.19
  145.0 3.0 %collective-permute-done.20 = f32[8,128]{1,0:T(8,128)S(1)} collective-permute-done((f32[8,128]{1,0:T(8,128)S(1)}, f32[8,128]{1,0:T(8,128)S(1)}, u32[]{:S(2)}, u32[]{:S(2)}) %collective-permute-start.20) | collective-permute-done | bytes 4128 | tf_op jit(solution)/shard_map/ppermute | solution.py:16
  148.0 1.5 collective-permute-done.19
  149.4 2.9 %collective-permute-start.24 = (f32[8,128]{1,0:T(8,128)S(1)}, f32[8,128]{1,0:T(8,128)S(1)}, u32[]{:S(2)}, u32[]{:S(2)}) collective-permute-start(f32[8,128]{1,0:T(8,128)S(1)} %add_add_fusion.1), channel_id=1, source_target_pairs={{0,6},{2,0},{4,2},{6,4},{1,7},{3,1},{5,3},{7,5},{8,14},{10,8},{12,... | collective-permute-start | bytes 12296 | tf_op jit(solution)/shard_map/ppermute | solution.py:16
  152.3 3.3 %collective-permute-start.23 = (f32[8,128]{1,0:T(8,128)S(1)}, f32[8,128]{1,0:T(8,128)S(1)}, u32[]{:S(2)}, u32[]{:S(2)}) collective-permute-start(f32[8,128]{1,0:T(8,128)S(1)} %add_add_fusion.1), channel_id=1, source_target_pairs={{0,4},{2,6},{4,0},{6,2},{1,5},{3,7},{5,1},{7,3},{8,12},{10,14},{12... | collective-permute-start | bytes 12296 | tf_op jit(solution)/shard_map/ppermute | solution.py:16
  155.6 4.3 %collective-permute-done.23 = f32[8,128]{1,0:T(8,128)S(1)} collective-permute-done((f32[8,128]{1,0:T(8,128)S(1)}, f32[8,128]{1,0:T(8,128)S(1)}, u32[]{:S(2)}, u32[]{:S(2)}) %collective-permute-start.23) | collective-permute-done | bytes 4128 | tf_op jit(solution)/shard_map/ppermute | solution.py:16
  159.9 1.5 collective-permute-done.22
  161.3 1.2 collective-permute-done.25
  162.5 0.5 fusion.2
  164.3 0.7 bitcast_convert_fusion
  165.1 0.8 fusion
  (49 shorter events, 0.9 us)
Async XLA Ops:
  0.6 19.3 %copy-start.4 = (bf16[512,256]{1,0:T(8,128)(2,1)S(1)}, bf16[512,256]{1,0:T(8,128)(2,1)}, u32[]{:S(2)}) copy-start(bf16[512,256]{1,0:T(8,128)(2,1)} %param.4) | copy-start | bytes 786436
  0.6 14.9 %collective-permute-start = (bf16[512,256]{1,0:T(8,128)(2,1)}, bf16[512,256]{1,0:T(8,128)(2,1)S(1)}, u32[]{:S(2)}, u32[]{:S(2)}) collective-permute-start(bf16[512,256]{1,0:T(8,128)(2,1)} %param.4), channel_id=1, source_target_pairs={{0,2},{2,4},{4,6},{6,0},{1,3},{3,5},{5,7},{7,1},{8,10},{10,12},{12... | collective-permute-start | bytes 786440 | tf_op jit(solution)/shard_map/ppermute | solution.py:16
  4.0 16.4 %collective-permute-start.5 = (bf16[512,256]{1,0:T(8,128)(2,1)}, bf16[512,256]{1,0:T(8,128)(2,1)S(1)}, u32[]{:S(2)}, u32[]{:S(2)}) collective-permute-start(bf16[512,256]{1,0:T(8,128)(2,1)} %param.4), channel_id=1, source_target_pairs={{0,6},{2,0},{4,2},{6,4},{1,7},{3,1},{5,3},{7,5},{8,14},{10,8},{12,... | collective-permute-start | bytes 786440 | tf_op jit(solution)/shard_map/ppermute | solution.py:16
  7.1 22.3 %collective-permute-start.9 = (bf16[3,512,256]{2,1,0:T(8,128)(2,1)}, bf16[3,512,256]{2,1,0:T(8,128)(2,1)S(1)}, u32[]{:S(2)}, u32[]{:S(2)}) collective-permute-start(bf16[3,512,256]{2,1,0:T(8,128)(2,1)} %r0.1), channel_id=1, source_target_pairs={{0,24},{8,0},{16,8},{24,16},{1,25},{9,1},{17,9},{25,17},{2,26},{10... | collective-permute-start | bytes 2359304 | tf_op jit(solution)/shard_map/ppermute | solution.py:16
  10.1 23.1 %collective-permute-start.10 = (bf16[3,512,256]{2,1,0:T(8,128)(2,1)}, bf16[3,512,256]{2,1,0:T(8,128)(2,1)S(1)}, u32[]{:S(2)}, u32[]{:S(2)}) collective-permute-start(bf16[3,512,256]{2,1,0:T(8,128)(2,1)} %r0.1), channel_id=1, source_target_pairs={{0,8},{8,16},{16,24},{24,0},{1,9},{9,17},{17,25},{25,1},{2,10},{10... | collective-permute-start | bytes 2359304 | tf_op jit(solution)/shard_map/ppermute | solution.py:16
  15.5 12.1 %collective-permute-start.6 = (bf16[256,256]{1,0:T(8,128)(2,1)S(1)}, bf16[256,256]{1,0:T(8,128)(2,1)S(1)}, u32[]{:S(2)}, u32[]{:S(2)}) collective-permute-start(bf16[256,256]{1,0:T(8,128)(2,1)S(1)} %slice.58), channel_id=1, source_target_pairs={{0,2},{2,4},{4,6},{6,0},{1,3},{3,5},{5,7},{7,1},{8,10},{10,12},{12... | collective-permute-start | bytes 393224 | tf_op jit(solution)/shard_map/ppermute | solution.py:16
  20.4 8.9 %collective-permute-start.7 = (bf16[256,256]{1,0:T(8,128)(2,1)S(1)}, bf16[256,256]{1,0:T(8,128)(2,1)S(1)}, u32[]{:S(2)}, u32[]{:S(2)}) collective-permute-start(bf16[256,256]{1,0:T(8,128)(2,1)S(1)} %slice.59), channel_id=1, source_target_pairs={{0,6},{2,0},{4,2},{6,4},{1,7},{3,1},{5,3},{7,5},{8,14},{10,8},{12,... | collective-permute-start | bytes 393224 | tf_op jit(solution)/shard_map/ppermute | solution.py:16
  29.3 18.4 %collective-permute-start.8 = (bf16[2048,256]{1,0:T(8,128)(2,1)S(1)}, bf16[2048,256]{1,0:T(8,128)(2,1)S(1)}, u32[]{:S(2)}, u32[]{:S(2)}) collective-permute-start(bf16[2048,256]{1,0:T(8,128)(2,1)S(1)} %constant_dynamic-update-slice_fusion.own), channel_id=1, source_target_pairs={{0,1},{1,0},{2,3},{3,2},{4,5},{5,4},{6,7},{7,6},{8,9},{9,8},{10,11... | collective-permute-start | bytes 3145736 | tf_op jit(solution)/shard_map/ppermute | solution.py:16
  30.2 12.4 %collective-permute-start.12 = (bf16[3,256,256]{2,1,0:T(8,128)(2,1)}, bf16[3,256,256]{2,1,0:T(8,128)(2,1)S(1)}, u32[]{:S(2)}, u32[]{:S(2)}) collective-permute-start(bf16[3,256,256]{2,1,0:T(8,128)(2,1)} %slice.61), channel_id=1, source_target_pairs={{0,24},{8,0},{16,8},{24,16},{1,25},{9,1},{17,9},{25,17},{2,26},{10... | collective-permute-start | bytes 1179656 | tf_op jit(solution)/shard_map/ppermute | solution.py:16
  34.0 0.9 copy-start.1
  34.9 12.8 %collective-permute-start.11 = (bf16[3,256,256]{2,1,0:T(8,128)(2,1)}, bf16[3,256,256]{2,1,0:T(8,128)(2,1)}, u32[]{:S(2)}, u32[]{:S(2)}) collective-permute-start(bf16[3,256,256]{2,1,0:T(8,128)(2,1)} %slice.60), channel_id=1, source_target_pairs={{0,8},{8,16},{16,24},{24,0},{1,9},{9,17},{17,25},{25,1},{2,10},{10... | collective-permute-start | bytes 1179656 | tf_op jit(solution)/shard_map/ppermute | solution.py:16
  35.6 18.0 %copy-start = (bf16[3,512,256]{2,1,0:T(8,128)(2,1)S(1)}, bf16[3,512,256]{2,1,0:T(8,128)(2,1)}, u32[]{:S(2)}) copy-start(bf16[3,512,256]{2,1,0:T(8,128)(2,1)} %l0.1) | copy-start | bytes 2359300
  47.7 1.1 copy-start.2
  48.8 1.1 copy-start.3
  53.6 4.3 %collective-permute-start.13 = (bf16[3,256,256]{2,1,0:T(8,128)(2,1)S(1)}, bf16[3,256,256]{2,1,0:T(8,128)(2,1)S(1)}, u32[]{:S(2)}, u32[]{:S(2)}) collective-permute-start(bf16[3,256,256]{2,1,0:T(8,128)(2,1)S(1)} %get-tuple-element.11), channel_id=1, source_target_pairs={{0,1},{1,0},{2,3},{3,2},{4,5},{5,4},{6,7},{7,6},{8,9},{9,8},{10,11... | collective-permute-start | bytes 1179656 | tf_op jit(solution)/shard_map/ppermute | solution.py:16
  53.7 35.6 %collective-permute-start.2 = (bf16[3,512,256]{2,1,0:T(8,128)(2,1)S(1)}, bf16[3,512,256]{2,1,0:T(8,128)(2,1)S(1)}, u32[]{:S(2)}, u32[]{:S(2)}) collective-permute-start(bf16[3,512,256]{2,1,0:T(8,128)(2,1)S(1)} %copy-done), channel_id=1, source_target_pairs={{0,2},{2,4},{4,6},{6,0},{1,3},{3,5},{5,7},{7,1},{8,10},{10,12},{12... | collective-permute-start | bytes 2359304 | tf_op jit(solution)/shard_map/ppermute | solution.py:16
  57.2 37.9 %collective-permute-start.1 = (bf16[3,512,256]{2,1,0:T(8,128)(2,1)S(1)}, bf16[3,512,256]{2,1,0:T(8,128)(2,1)S(1)}, u32[]{:S(2)}, u32[]{:S(2)}) collective-permute-start(bf16[3,512,256]{2,1,0:T(8,128)(2,1)S(1)} %copy-done), channel_id=1, source_target_pairs={{0,6},{2,0},{4,2},{6,4},{1,7},{3,1},{5,3},{7,5},{8,14},{10,8},{12,... | collective-permute-start | bytes 2359304 | tf_op jit(solution)/shard_map/ppermute | solution.py:16
  58.0 38.6 %collective-permute-start.15 = (bf16[2,3,256,256]{3,2,1,0:T(8,128)(2,1)S(1)}, bf16[2,3,256,256]{3,2,1,0:T(8,128)(2,1)S(1)}, u32[]{:S(2)}, u32[]{:S(2)}) collective-permute-start(bf16[2,3,256,256]{3,2,1,0:T(8,128)(2,1)S(1)} %pad_maximum_fusion.w0), channel_id=1, source_target_pairs={{0,8},{8,16},{16,24},{24,0},{1,9},{9,17},{17,25},{25,1},{2,10},{10... | collective-permute-start | bytes 2359304 | tf_op jit(solution)/shard_map/ppermute | solution.py:16
  58.1 38.6 %collective-permute-start.14 = (bf16[2,3,256,256]{3,2,1,0:T(8,128)(2,1)S(1)}, bf16[2,3,256,256]{3,2,1,0:T(8,128)(2,1)S(1)}, u32[]{:S(2)}, u32[]{:S(2)}) collective-permute-start(bf16[2,3,256,256]{3,2,1,0:T(8,128)(2,1)S(1)} %pad_maximum_fusion.w0), channel_id=1, source_target_pairs={{0,24},{8,0},{16,8},{24,16},{1,25},{9,1},{17,9},{25,17},{2,26},{10... | collective-permute-start | bytes 2359304 | tf_op jit(solution)/shard_map/ppermute | solution.py:16
  89.3 13.2 %collective-permute-start.3 = (bf16[3,256,256]{2,1,0:T(8,128)(2,1)S(1)}, bf16[3,256,256]{2,1,0:T(8,128)(2,1)S(1)}, u32[]{:S(2)}, u32[]{:S(2)}) collective-permute-start(bf16[3,256,256]{2,1,0:T(8,128)(2,1)S(1)} %slice.56), channel_id=1, source_target_pairs={{0,2},{2,4},{4,6},{6,0},{1,3},{3,5},{5,7},{7,1},{8,10},{10,12},{12... | collective-permute-start | bytes 1179656 | tf_op jit(solution)/shard_map/ppermute | solution.py:16
  95.1 19.7 %collective-permute-start.4 = (bf16[3,256,256]{2,1,0:T(8,128)(2,1)S(1)}, bf16[3,256,256]{2,1,0:T(8,128)(2,1)S(1)}, u32[]{:S(2)}, u32[]{:S(2)}) collective-permute-start(bf16[3,256,256]{2,1,0:T(8,128)(2,1)S(1)} %slice.57), channel_id=1, source_target_pairs={{0,6},{2,0},{4,2},{6,4},{1,7},{3,1},{5,3},{7,5},{8,14},{10,8},{12,... | collective-permute-start | bytes 1179656 | tf_op jit(solution)/shard_map/ppermute | solution.py:16
  96.6 18.3 %collective-permute-start.16 = (bf16[2,3,128,256]{3,2,1,0:T(8,128)(2,1)S(1)}, bf16[2,3,128,256]{3,2,1,0:T(8,128)(2,1)S(1)}, u32[]{:S(2)}, u32[]{:S(2)}) collective-permute-start(bf16[2,3,128,256]{3,2,1,0:T(8,128)(2,1)S(1)} %slice.62), channel_id=1, source_target_pairs={{0,8},{8,16},{16,24},{24,0},{1,9},{9,17},{17,25},{25,1},{2,10},{10... | collective-permute-start | bytes 1179656 | tf_op jit(solution)/shard_map/ppermute | solution.py:16
  96.7 18.1 %collective-permute-start.17 = (bf16[2,3,128,256]{3,2,1,0:T(8,128)(2,1)S(1)}, bf16[2,3,128,256]{3,2,1,0:T(8,128)(2,1)S(1)}, u32[]{:S(2)}, u32[]{:S(2)}) collective-permute-start(bf16[2,3,128,256]{3,2,1,0:T(8,128)(2,1)S(1)} %slice.63), channel_id=1, source_target_pairs={{0,24},{8,0},{16,8},{24,16},{1,25},{9,1},{17,9},{25,17},{2,26},{10... | collective-permute-start | bytes 1179656 | tf_op jit(solution)/shard_map/ppermute | solution.py:16
  117.6 2.2 %collective-permute-start.18 = (f32[512,256]{1,0:T(8,128)S(1)}, f32[512,256]{1,0:T(8,128)S(1)}, u32[]{:S(2)}, u32[]{:S(2)}) collective-permute-start(f32[512,256]{1,0:T(8,128)S(1)} %get-tuple-element.13), channel_id=1, source_target_pairs={{0,1},{1,0},{2,3},{3,2},{4,5},{5,4},{6,7},{7,6},{8,9},{9,8},{10,11... | collective-permute-start | bytes 1572872 | tf_op jit(solution)/shard_map/ppermute | solution.py:16
  138.0 26.3 %all-to-all-start.1 = ((f32[8,64,256]{2,1,0:T(8,128)}), f32[8,64,256]{2,1,0:T(8,128)S(1)}, u32[]{:S(2)}, u32[]{:S(2)}) async-start(f32[8,64,256]{2,1,0:T(8,128)} %broadcast_in_dim.4), calls=%async_computation.1 | async-start | bytes 1048576 | tf_op jit(solution)/shard_map/all_to_all | solution.py:156
  142.9 5.1 %collective-permute-start.20 = (f32[8,128]{1,0:T(8,128)S(1)}, f32[8,128]{1,0:T(8,128)S(1)}, u32[]{:S(2)}, u32[]{:S(2)}) collective-permute-start(f32[8,128]{1,0:T(8,128)S(1)} %slice.65), channel_id=1, source_target_pairs={{0,16},{8,24},{16,0},{24,8},{1,17},{9,25},{17,1},{25,9},{2,18},{10... | collective-permute-start | bytes 12296 | tf_op jit(solution)/shard_map/ppermute | solution.py:16
  142.9 5.1 %collective-permute-start.21 = (f32[8,128]{1,0:T(8,128)S(1)}, f32[8,128]{1,0:T(8,128)S(1)}, u32[]{:S(2)}, u32[]{:S(2)}) collective-permute-start(f32[8,128]{1,0:T(8,128)S(1)} %slice.65), channel_id=1, source_target_pairs={{0,24},{8,0},{16,8},{24,16},{1,25},{9,1},{17,9},{25,17},{2,26},{10... | collective-permute-start | bytes 12296 | tf_op jit(solution)/shard_map/ppermute | solution.py:16
  144.6 4.8 %collective-permute-start.19 = (f32[8,128]{1,0:T(8,128)S(1)}, f32[8,128]{1,0:T(8,128)S(1)}, u32[]{:S(2)}, u32[]{:S(2)}) collective-permute-start(f32[8,128]{1,0:T(8,128)S(1)} %slice.65), channel_id=1, source_target_pairs={{0,8},{8,16},{16,24},{24,0},{1,9},{9,17},{17,25},{25,1},{2,10},{10... | collective-permute-start | bytes 12296 | tf_op jit(solution)/shard_map/ppermute | solution.py:16
  149.4 6.2 %collective-permute-start.24 = (f32[8,128]{1,0:T(8,128)S(1)}, f32[8,128]{1,0:T(8,128)S(1)}, u32[]{:S(2)}, u32[]{:S(2)}) collective-permute-start(f32[8,128]{1,0:T(8,128)S(1)} %add_add_fusion.1), channel_id=1, source_target_pairs={{0,6},{2,0},{4,2},{6,4},{1,7},{3,1},{5,3},{7,5},{8,14},{10,8},{12,... | collective-permute-start | bytes 12296 | tf_op jit(solution)/shard_map/ppermute | solution.py:16
  152.3 7.5 %collective-permute-start.23 = (f32[8,128]{1,0:T(8,128)S(1)}, f32[8,128]{1,0:T(8,128)S(1)}, u32[]{:S(2)}, u32[]{:S(2)}) collective-permute-start(f32[8,128]{1,0:T(8,128)S(1)} %add_add_fusion.1), channel_id=1, source_target_pairs={{0,4},{2,6},{4,0},{6,2},{1,5},{3,7},{5,1},{7,3},{8,12},{10,14},{12... | collective-permute-start | bytes 12296 | tf_op jit(solution)/shard_map/ppermute | solution.py:16
  155.6 5.7 %collective-permute-start.22 = (f32[8,128]{1,0:T(8,128)S(1)}, f32[8,128]{1,0:T(8,128)S(1)}, u32[]{:S(2)}, u32[]{:S(2)}) collective-permute-start(f32[8,128]{1,0:T(8,128)S(1)} %add_add_fusion.1), channel_id=1, source_target_pairs={{0,2},{2,4},{4,6},{6,0},{1,3},{3,5},{5,7},{7,1},{8,10},{10,12},{12... | collective-permute-start | bytes 12296 | tf_op jit(solution)/shard_map/ppermute | solution.py:16
  161.3 1.2 collective-permute-start.25

commit v2 on v0

v2 whole, which is shorter than its diff:
```python
import jax
import jax.numpy as jnp
from jax import lax
from jax.experimental import pallas as pl
from jax.experimental.pallas import tpu as pltpu
from jax.sharding import Mesh, PartitionSpec as P

TERMS = ("x", "zlo")
BF16, F32 = jnp.bfloat16, jnp.float32
SMEM = pl.BlockSpec(memory_space=pltpu.SMEM)
VMEM = pl.BlockSpec(memory_space=pltpu.VMEM)
HBM = pl.BlockSpec(memory_space=pl.ANY)


def shift(x, axis, n, k):
    return lax.ppermute(x, axis, [(i, (i + k) % n) for i in range(n)])


def fetch(x):
    pairs = []
    for t in range(8):
        for at in range(16):
            for c in range(2):
                source = (at + 2 * t + c) % 16
                pairs.append((t * 32 + source * 2 + c, t * 32 + at * 2 + c))
    return lax.ppermute(x, (*TERMS, "row", "zhi", "core"), pairs)


def together(*xs):
    return lax.optimization_barrier(xs)


def far(after, before, axis, dim):
    half = after.shape[dim] // 2
    low = shift(lax.slice_in_dim(before, 0, half, axis=dim), axis, 4, 1)
    high = shift(lax.slice_in_dim(after, half, 2 * half, axis=dim), axis, 4, 3)
    return low, high


def spread_to(x, axis):
    n = 4
    return lax.all_to_all(jnp.broadcast_to(x[None], (n, *x.shape)), axis, 0, 0, tiled=True)


def start(moves, sems):
    copies = [pltpu.make_async_copy(a, b, sems.at[i]) for i, (a, b) in enumerate(moves)]
    for copy in copies:
        copy.start()
    return copies


def wait(copies):
    for copy in copies:
        copy.wait()


def first_kernel(place, own, sib, r0, r1, r2a, r2b, r3, keep, send, psi, right, sems):
    m, c = place[0], place[2]
    first = start([(own, psi.at[c]), (sib, psi.at[1 - c])], sems.at[3])
    slots = []
    for s in range(3):
        moves = [(r0.at[s], right.at[0, s]), (r1.at[s], right.at[1, s]), (r3.at[s], right.at[3, s])]
        moves += [(r2a.at[s], right.at[2, s, pl.ds(0, 256)]), (r2b.at[s], right.at[2, s, pl.ds(256, 256)])]
        slots.append(start(moves, sems.at[s]))
    wait(first)
    for s in range(3):
        wait(slots[s])
        for out, part in ((keep, c), (send, 1 - c)):
            total = jnp.zeros((256, 256), F32)
            for d in range(4):
                j = lax.rem(m + d, 4)
                for h in range(2):
                    rows = jnp.concatenate([psi[h, 2 * part, j], psi[h, 2 * part + 1, j]], axis=0)
                    total += jnp.dot(
                        rows, right[d, s, h * 256 : (h + 1) * 256], preferred_element_type=F32
                    )
            out[s] = total.astype(BF16)


def split(x):
    high = x.astype(BF16)
    return [high, (x - high.astype(F32)).astype(BF16)]


def second_kernel(place, left, w0, w1, w2a, w2b, w3, own, sib, out, total, l_buf, w_buf, psi, sems):
    m, l, c, live = place[0], place[1], place[2], place[4]
    slots = []
    for s in range(3):
        moves = [(left.at[:, s], l_buf.at[:, s]), (w0.at[:, s], w_buf.at[0, :, s]), (w1.at[:, s], w_buf.at[1, :, s])]
        moves += [(w2a.at[s], w_buf.at[2, 0, s]), (w2b.at[s], w_buf.at[2, 1, s]), (w3.at[:, s], w_buf.at[3, :, s])]
        slots.append(start(moves, sems.at[s]))
    last = start([(own.at[:, l], psi.at[0]), (sib.at[:, l], psi.at[1])], sems.at[3])
    for s in range(3):
        wait(slots[s])

        @pl.when(s < live)
        def _(s=s):
            for block in range(2):
                rows = slice(block * 256, (block + 1) * 256)
                for h in range(2):
                    term = jnp.zeros((256, 256), F32) if s == 0 else total[h, rows]
                    for d in range(4):
                        term += jnp.dot(
                            l_buf[lax.rem(m + d, 4), s, rows, :], w_buf[d, h, s], preferred_element_type=F32
                        )
                    total[h, rows] = term

    wait(last)
    above, below = jnp.zeros((8, 256), F32), jnp.zeros((8, 256), F32)
    for part in range(8):
        for h in range(2):
            wide = psi[h, part // 2, (part % 2) * 64 : (part % 2) * 64 + 64].astype(F32)
            term = total[h, part * 64 : (part + 1) * 64]
            above += (wide * term).reshape(8, 8, 256).sum(0)
            if h == 0:
                below += (wide * wide).reshape(8, 8, 256).sum(0)
            out[2 * part + (c if h == 0 else 1 - c), 0:64] = term.astype(BF16)
    sums = [y for x in (above, below) for y in split(x.reshape(4, 2, 256).sum(0).reshape(2, 256))]
    sums = jnp.concatenate(sums + [jnp.zeros((8, 256), BF16)], axis=0)
    for part in range(16):
        out[part, 64:80] = sums


def third_kernel(parts, out, sums):
    chunk = parts[0].astype(F32)
    for part in range(1, 16):
        chunk += parts[part].astype(F32)
    out[...] = chunk[0:64]
    for i in range(2):
        one = chunk[64 + 4 * i : 68 + 4 * i].sum(0, keepdims=True).sum(1, keepdims=True)
        sums[i : i + 1] = jnp.broadcast_to(one, (1, 128))
    sums[2:8] = jnp.zeros((6, 128), F32)


def spread_kernel(chunk, one, other, out):
    for part in range(8):
        out[part, 0:64] = chunk[...]
        out[part, 64:72, 0:128] = one[...]
        out[part, 64:72, 128:256] = other[...]


def last_kernel(parts, psi, sigma, residual, energy):
    tail = parts[0, 64:72]
    for part in range(1, 8):
        tail += parts[part, 64:72]
    tail = tail[:, 0:128] + tail[:, 128:256]
    ratio = jnp.broadcast_to(tail[0:1] / (tail[1:2] * 0.125), (8, 128))
    energy[...] = ratio
    row = jnp.concatenate([ratio[0:1], ratio[0:1]], axis=1)
    for part in range(8):
        rows = slice(part * 64, (part + 1) * 64)
        full = parts[part, 0:64]
        sigma[rows] = full.astype(BF16)
        residual[rows] = (full - row * psi[rows].astype(F32)).astype(BF16)


def call(kernel, outs, ins, *args, scratch=(), limit=8, flops=0, nbytes=1 << 10):
    return pl.pallas_call(
        kernel,
        out_shape=[jax.ShapeDtypeStruct(shape, dtype) for shape, dtype in outs],
        in_specs=ins,
        out_specs=[VMEM] * len(outs),
        scratch_shapes=scratch,
        compiler_params=pltpu.CompilerParams(vmem_limit_bytes=limit << 20),
        cost_estimate=pl.CostEstimate(flops=flops, bytes_accessed=nbytes, transcendentals=0),
    )(*args)


def per_device(psi, left_ops, right_ops_t, term_count):
    m, l, c = lax.axis_index("row"), lax.axis_index("zhi"), lax.axis_index("core")
    a = lax.axis_index("x")
    place = jnp.stack([m, l, c, a, term_count[0]]).astype(jnp.int32)

    left = lax.all_gather(left_ops, "zhi")

    quarter = lax.dynamic_slice_in_dim(psi, a * 128, 128, 0)
    r1, r3 = shift(right_ops_t, "row", 4, 3), shift(right_ops_t, "row", 4, 1)
    column = spread_to(quarter, "zhi")
    column, r1, r3 = together(column, r1, r3)
    r2a, r2b = far(r1, r3, "row", 1)
    own = spread_to(column, "x")
    own, r2a, r2b = together(own, r2a, r2b)
    sib = shift(own, "core", 2, 1)
    keep, send = call(
        first_kernel, [((3, 256, 256), BF16)] * 2, [SMEM] + [HBM] * 7,
        place, own, sib, right_ops_t, r1, r2a, r2b, r3,
        scratch=[pltpu.VMEM((2, 4, 4, 128, 256), BF16), pltpu.VMEM((4, 3, 512, 256), BF16), pltpu.SemaphoreType.DMA((4, 5))],
        limit=56,
    )
    w = jnp.stack([keep, shift(send, "core", 2, 1)])
    w1, w3 = shift(w, "row", 4, 3), shift(w, "row", 4, 1)
    w2a = shift(w3[0], "row", 4, 1)
    w2b = shift(w1[1], "row", 4, 3)

    (payload,) = call(
        second_kernel, [((16, 80, 256), BF16)], [SMEM] + [HBM] * 8,
        place, left, w, w1, w2a, w2b, w3, own, sib,
        scratch=[
            pltpu.VMEM((2, 512, 256), F32), pltpu.VMEM((4, 3, 512, 256), BF16), pltpu.VMEM((4, 2, 3, 256, 256), BF16),
            pltpu.VMEM((2, 4, 128, 256), BF16), pltpu.SemaphoreType.DMA((4, 6)),
        ],
        limit=56,
    )

    parts = lax.all_to_all(payload, (*TERMS, "core"), 0, 0, tiled=True)
    chunk, sums = call(third_kernel, [((64, 256), F32), ((8, 128), F32)], [VMEM], parts)
    one = fetch(sums)
    other = shift(one, "core", 2, 1)
    (spread,) = call(spread_kernel, [((8, 72, 256), F32)], [VMEM] * 3, chunk, one, other)
    full = lax.all_to_all(spread, TERMS, 0, 0, tiled=True)
    sigma, residual, energy = call(
        last_kernel, [((512, 256), BF16), ((512, 256), BF16), ((8, 128), F32)], [VMEM] * 2, full, psi
    )
    return sigma, residual, energy[0, 0]


def solution(mesh):
    fine = Mesh(mesh.devices.reshape(4, 2, 4, 4, 2), ("x", "zlo", "row", "zhi", "core"))
    col = ("zhi", "core")
    in_specs = (P("row", col), P(TERMS, "row", col), P(TERMS, "row", col), P(TERMS))
    out_specs = (P("row", col), P("row", col), P())
    return jax.shard_map(
        per_device, mesh=fine, in_specs=in_specs, out_specs=out_specs, check_vma=False
    )
```

time: 535 us -> 154 us (0.29)
  waiting for transfers between devices: 420 us -> 41.3 us
  starting transfers between devices: 0.44 us -> 25.8 us
  blocking collectives: 70.9 us -> 52.8 us
  matrix products: 17.8 us -> 0 us
  Pallas kernels: 0 us -> 11.7 us
    all_gather x10 -> x1, waiting for transfers between devices: 340 us -> 0.02 us  [per_device(): left = lax.all_gather(left_ops, 'zhi')]
    psum x1 -> x0, waiting for transfers between devices: 76.3 us -> none  [per_device(): sigma_full = lax.psum(partial_sum, 'terms')]
    psum x1 -> x0, blocking collectives: 70.9 us -> none  [per_device(): lax.psum((jnp.sum(psi_wide * sigma_full), jnp.sum(psi_wide * psi_wide)),...]
    all_to_all x0 -> x3, blocking collectives: none -> 52.8 us  [the longest x1 19.1 us: spread_to(): lax.all_to_all(jnp.broadcast_to(x[None], (n, *x.shape)), axis, 0, 0, tile...]
    ppermute x0 -> x12, waiting for transfers between devices: none -> 40.5 us  [the longest x11 39.2 us: shift(): return lax.ppermute(x, axis, [(i, (i + k) % n) for i in range(n)])]
    ppermute x0 -> x12, starting transfers between devices: none -> 21 us  [the longest x11 16.2 us: shift(): return lax.ppermute(x, axis, [(i, (i + k) % n) for i in range(n)])]
    dot_general x6 -> x0, matrix products: 17.8 us -> none  [the longest x3 9.29 us: per_device(): jnp.dot(lax.all_gather(left, 'col', axis=1, tiled=True), psi_cols, prefer...]
    pallas_call x0 -> x5, Pallas kernels: none -> 11.7 us  [call(): pl.pallas_call(kernel, out_shape=[jax.ShapeDtypeStruct(shape, dtype) for...]
  transfers between devices with their start and end apart: 11 -> 14, of which waited for: 11 -> 10; matrix products, arithmetic and copies ran while one was open for 3% -> 3% of each run, Pallas kernels for 0% -> 4%
where the time goes in v2:
time: 154 us; the launch traced here: 153 us
  blocking collectives  52.8 us (34%)
  waiting for transfers between devices  41.3 us (27%)
  starting transfers between devices  25.8 us (17%)
  between operations  14.9 us (10%)
  Pallas kernels  11.7 us (8%)
  local copies, waits for them, and re-layouts  5.3 us (3%)
    ppermute x11, waiting for transfers between devices, shift(): return lax.ppermute(x, axis, [(i, (i + k) % n) for i in range(n)])  39.2 us
    all_to_all x1, blocking collectives, spread_to(): lax.all_to_all(jnp.broadcast_to(x[None], (n, *x.shape)), axis, 0, 0, tile...  19.1 us
    all_to_all x1, blocking collectives, per_device(): full = lax.all_to_all(spread, TERMS, 0, 0, tiled=True)  17.2 us
    all_to_all x1, blocking collectives, per_device(): parts = lax.all_to_all(payload, (*TERMS, 'core'), 0, 0, tiled=True)  16.4 us
    ppermute x11, starting transfers between devices, shift(): return lax.ppermute(x, axis, [(i, (i + k) % n) for i in range(n)])  16.2 us
    pallas_call x5, Pallas kernels, call(): pl.pallas_call(kernel, out_shape=[jax.ShapeDtypeStruct(shape, dtype) for...  11.7 us
    all_to_all x1, starting transfers between devices, spread_to(): lax.all_to_all(jnp.broadcast_to(x[None], (n, *x.shape)), axis, 0, 0, tile...  4.82 us
    ppermute x1, starting transfers between devices, fetch(): return lax.ppermute(x, (*TERMS, 'row', 'zhi', 'core'), pairs)  4.78 us
  transfers between devices with their start and end apart: 14, of which 10 were waited for; matrix products, arithmetic and copies ran while one was open for 3% of the time, Pallas kernels for 4%

profile of v2, /device:TPU:2, one launch (start us, length us, event | category | flops | bytes accessed | tf_op | source)
XLA Modules:
  0.0 152.8 jit_solution(6355462247821417592)
XLA Ops:
  7.2 0.0 all-gather.3.cloned.1.call-start
  7.2 3.1 %collective-permute-start = (bf16[3,512,256]{2,1,0:T(8,128)(2,1)}, bf16[3,512,256]{2,1,0:T(8,128)(2,1)S(1)}, u32[]{:S(2)}, u32[]{:S(2)}) collective-permute-start(bf16[3,512,256]{2,1,0:T(8,128)(2,1)} %r0.1), channel_id=1, source_target_pairs={{0,24},{8,0},{16,8},{24,16},{1,25},{9,1},{17,9},{25,17},{2,26},{10... | collective-permute-start | bytes 2359304 | tf_op jit(solution)/shard_map/ppermute | solution.py:16
  10.3 0.0 collective-permute-start.1
  10.3 0.0 all-gather.3.cloned.1.call-update
  10.3 0.8 constant_dynamic-slice_fusion
  11.2 19.1 %all_to_all.20 = bf16[4,128,256]{2,1,0:T(8,128)(2,1)S(1)} all-to-all(bf16[4,128,256]{2,1,0:T(8,128)(2,1)S(1)} %broadcast_in_dim.4), channel_id=1, replica_groups=mesh['x'=4,'zlo'=2,'row'=4,'zhi'=4,'core'=2] {'zhi'}, dimensions={0} | all-to-all | bytes 524288 | tf_op jit(solution)/shard_map/all_to_all | solution.py:42
  30.3 0.0 collective-permute-done.r1
  30.3 0.4 collective-permute-done.1.r3
  30.7 1.2 broadcast_in_dim.5
  31.9 4.8 %all-to-all-start.1 = ((bf16[4,4,128,256]{3,2,1,0:T(8,128)(2,1)}), bf16[4,4,128,256]{3,2,1,0:T(8,128)(2,1)S(1)}, u32[]{:S(2)}, u32[]{:S(2)}) async-start(bf16[4,4,128,256]{3,2,1,0:T(8,128)(2,1)} %broadcast_in_dim.5), calls=%async_computation.1 | async-start | bytes 2097152 | tf_op jit(solution)/shard_map/all_to_all | solution.py:42
  36.8 2.6 %collective-permute-start.3 = (bf16[3,256,256]{2,1,0:T(8,128)(2,1)S(1)}, bf16[3,256,256]{2,1,0:T(8,128)(2,1)S(1)}, u32[]{:S(2)}, u32[]{:S(2)}) collective-permute-start(bf16[3,256,256]{2,1,0:T(8,128)(2,1)S(1)} %slice.16), channel_id=1, source_target_pairs={{0,24},{8,0},{16,8},{24,16},{1,25},{9,1},{17,9},{25,17},{2,26},{10... | collective-permute-start | bytes 1179656 | tf_op jit(solution)/shard_map/ppermute | solution.py:16
  39.4 0.0 collective-permute-start.2
  39.4 6.6 %collective-permute-done.3.r2b = bf16[3,256,256]{2,1,0:T(8,128)(2,1)S(1)} collective-permute-done((bf16[3,256,256]{2,1,0:T(8,128)(2,1)S(1)}, bf16[3,256,256]{2,1,0:T(8,128)(2,1)S(1)}, u32[]{:S(2)}, u32[]{:S(2)}) %collective-permute-start.3) | collective-permute-done | bytes 393248 | tf_op jit(solution)/shard_map/ppermute | solution.py:16
  46.0 2.5 %collective-permute-done.2.r2a = bf16[3,256,256]{2,1,0:T(8,128)(2,1)} collective-permute-done((bf16[3,256,256]{2,1,0:T(8,128)(2,1)S(1)}, bf16[3,256,256]{2,1,0:T(8,128)(2,1)}, u32[]{:S(2)}, u32[]{:S(2)}) %collective-permute-start.2) | collective-permute-done | bytes 393248 | tf_op jit(solution)/shard_map/ppermute | solution.py:16
  48.5 0.0 copy-done.7
  48.5 0.7 all-to-all-done.1.own
  49.2 0.0 collective-permute-start.4
  49.9 0.7 stack.28.place
  50.5 1.3 collective-permute-done.4.sib
  51.9 0.0 copy-done.1
  51.9 1.0 copy-done.2
  52.9 5.8 %shard_map.67 = (bf16[3,256,256]{2,1,0:T(8,128)(2,1)}, bf16[3,256,256]{2,1,0:T(8,128)(2,1)}) custom-call(s32[5]{0:T(128)} %stack.28.place, bf16[4,4,128,256]{3,2,1,0:T(8,128)(2,1)} %copy-done.1, bf16[4,4,128,256]{3,2,1,0:T(8,128)(2,1)} %copy-done.2, bf16[3,512,256]{2,1,0:T(8,128)(2,1)} %r0.1, bf16[3,512,256]{2,1,0:T(8,128)(2,1)} %copy-done.6, ...), custom_call_target="tpu_custom_call" | custom-call | bytes 1024 | tf_op jit(solution)/shard_map/pallas_call | solution.py:158
  58.6 0.2 collective-permute-start.5
  58.9 1.8 %collective-permute-done.5 = bf16[3,256,256]{2,1,0:T(8,128)(2,1)S(1)} collective-permute-done((bf16[3,256,256]{2,1,0:T(8,128)(2,1)}, bf16[3,256,256]{2,1,0:T(8,128)(2,1)S(1)}, u32[]{:S(2)}, u32[]{:S(2)}) %collective-permute-start.5) | collective-permute-done | bytes 393248 | tf_op jit(solution)/shard_map/ppermute | solution.py:16
  60.7 1.1 pad_maximum_fusion.w0
  61.7 0.0 copy-start.3
  61.7 0.1 collective-permute-start.7
  61.8 3.2 %collective-permute-start.6 = (bf16[2,3,256,256]{3,2,1,0:T(8,128)(2,1)S(1)}, bf16[2,3,256,256]{3,2,1,0:T(8,128)(2,1)S(1)}, u32[]{:S(2)}, u32[]{:S(2)}) collective-permute-start(bf16[2,3,256,256]{3,2,1,0:T(8,128)(2,1)S(1)} %pad_maximum_fusion.w0), channel_id=1, source_target_pairs={{0,24},{8,0},{16,8},{24,16},{1,25},{9,1},{17,9},{25,17},{2,26},{10... | collective-permute-start | bytes 2359304 | tf_op jit(solution)/shard_map/ppermute | solution.py:16
  65.1 17.6 %collective-permute-done.7.w3 = bf16[2,3,256,256]{3,2,1,0:T(8,128)(2,1)S(1)} collective-permute-done((bf16[2,3,256,256]{3,2,1,0:T(8,128)(2,1)S(1)}, bf16[2,3,256,256]{3,2,1,0:T(8,128)(2,1)S(1)}, u32[]{:S(2)}, u32[]{:S(2)}) %collective-permute-start.7) | collective-permute-done | bytes 786464 | tf_op jit(solution)/shard_map/ppermute | solution.py:16
  82.6 0.1 collective-permute-start.8
  82.7 0.0 collective-permute-done.6.w1
  82.8 3.3 %collective-permute-start.9 = (bf16[3,256,256]{2,1,0:T(8,128)(2,1)S(1)}, bf16[3,256,256]{2,1,0:T(8,128)(2,1)S(1)}, u32[]{:S(2)}, u32[]{:S(2)}) collective-permute-start(bf16[3,256,256]{2,1,0:T(8,128)(2,1)S(1)} %slice_bitcast_fusion), channel_id=1, source_target_pairs={{0,24},{8,0},{16,8},{24,16},{1,25},{9,1},{17,9},{25,17},{2,26},{10... | collective-permute-start | bytes 1179656 | tf_op jit(solution)/shard_map/ppermute | solution.py:16
  86.1 8.2 %collective-permute-done.8.w2a = bf16[3,256,256]{2,1,0:T(8,128)(2,1)S(1)} collective-permute-done((bf16[3,256,256]{2,1,0:T(8,128)(2,1)S(1)}, bf16[3,256,256]{2,1,0:T(8,128)(2,1)S(1)}, u32[]{:S(2)}, u32[]{:S(2)}) %collective-permute-start.8) | collective-permute-done | bytes 393248 | tf_op jit(solution)/shard_map/ppermute | solution.py:16
  94.3 0.0 collective-permute-done.9.w2b
  94.3 0.0 all-gather.3.cloned.1.call-done
  94.3 0.7 copy-done.8
  95.0 0.2 copy-done.9
  95.2 4.9 %shard_map.68 = bf16[16,80,256]{2,1,0:T(8,128)(2,1)} custom-call(s32[5]{0:T(128)} %stack.28.place, bf16[4,3,512,256]{3,2,1,0:T(8,128)(2,1)} %bitcast.12, bf16[2,3,256,256]{3,2,1,0:T(8,128)(2,1)} %copy-done.3, bf16[2,3,256,256]{3,2,1,0:T(8,128)(2,1)} %copy-done.5, bf16[3,256,256]{2,1,0:T(8,128)(2,1)} %copy-done.8, bf16[3,256,256]{2,1,0:T(8,128)(2,1)} %copy-done.9, ...), custom_call_target="tpu_custom_call" | custom-call | bytes 1024 | tf_op jit(solution)/shard_map/pallas_call | solution.py:158
  100.1 0.0 copy-start
  100.1 16.4 %all_to_all.21.parts = bf16[16,80,256]{2,1,0:T(8,128)(2,1)S(1)} all-to-all(bf16[16,80,256]{2,1,0:T(8,128)(2,1)} %shard_map.68), channel_id=1, replica_groups=mesh['x'=4,'zlo'=2,'row'=4,'zhi'=4,'core'=2] {'x','zlo','core'}, dimensions={0} | all-to-all | bytes 1310720 | tf_op jit(solution)/shard_map/all_to_all | solution.py:205
  116.6 0.1 shard_map.69
  116.7 4.8 %collective-permute-start.10 = (f32[8,128]{1,0:T(8,128)S(1)}, f32[8,128]{1,0:T(8,128)S(1)}, u32[]{:S(2)}, u32[]{:S(2)}) collective-permute-start(f32[8,128]{1,0:T(8,128)S(1)} %get-tuple-element.25), channel_id=1, source_target_pairs={{0,0},{3,1},{2,2},{5,3},{4,4},{7,5},{6,6},{9,7},{8,8},{11,9},{10,1... | collective-permute-start | bytes 12296 | tf_op jit(solution)/shard_map/ppermute | solution.py:26
  121.5 1.3 collective-permute-done.10.one
  122.8 3.6 %collective-permute-start.11 = (f32[8,128]{1,0:T(8,128)S(1)}, f32[8,128]{1,0:T(8,128)S(1)}, u32[]{:S(2)}, u32[]{:S(2)}) collective-permute-start(f32[8,128]{1,0:T(8,128)S(1)} %collective-permute-done.10.one), channel_id=1, source_target_pairs={{0,1},{1,0},{2,3},{3,2},{4,5},{5,4},{6,7},{7,6},{8,9},{9,8},{10,11... | collective-permute-start | bytes 12296 | tf_op jit(solution)/shard_map/ppermute | solution.py:16
  126.4 0.8 collective-permute-done.11.other
  127.3 17.2 %all_to_all.22.parts = f32[8,72,256]{2,1,0:T(8,128)S(1)} all-to-all(f32[8,72,256]{2,1,0:T(8,128)S(1)} %shard_map.70), channel_id=1, replica_groups=mesh['x'=4,'zlo'=2,'row'=4,'zhi'=4,'core'=2] {'x','zlo'}, dimensions={0} | all-to-all | bytes 1179648 | tf_op jit(solution)/shard_map/all_to_all | solution.py:210
  144.5 0.9 shard_map.71
  145.4 0.5 slice.19
  (21 shorter events, 0.2 us)
Async XLA Ops:
  7.2 87.1 %all-gather.3.cloned.1.call-start = ((), (), s32[]{:S(2)}) async-start(), calls=%async_computation.4 | async-start | bytes 3932160 | tf_op jit(solution)/shard_map/all_gather | solution.py:174
  7.2 23.1 %collective-permute-start = (bf16[3,512,256]{2,1,0:T(8,128)(2,1)}, bf16[3,512,256]{2,1,0:T(8,128)(2,1)S(1)}, u32[]{:S(2)}, u32[]{:S(2)}) collective-permute-start(bf16[3,512,256]{2,1,0:T(8,128)(2,1)} %r0.1), channel_id=1, source_target_pairs={{0,24},{8,0},{16,8},{24,16},{1,25},{9,1},{17,9},{25,17},{2,26},{10... | collective-permute-start | bytes 2359304 | tf_op jit(solution)/shard_map/ppermute | solution.py:16
  10.3 20.4 %collective-permute-start.1 = (bf16[3,512,256]{2,1,0:T(8,128)(2,1)}, bf16[3,512,256]{2,1,0:T(8,128)(2,1)S(1)}, u32[]{:S(2)}, u32[]{:S(2)}) collective-permute-start(bf16[3,512,256]{2,1,0:T(8,128)(2,1)} %r0.1), channel_id=1, source_target_pairs={{0,8},{8,16},{16,24},{24,0},{1,9},{9,17},{17,25},{25,1},{2,10},{10... | collective-permute-start | bytes 2359304 | tf_op jit(solution)/shard_map/ppermute | solution.py:16
  30.3 21.6 %copy-start.6 = (bf16[3,512,256]{2,1,0:T(8,128)(2,1)}, bf16[3,512,256]{2,1,0:T(8,128)(2,1)S(1)}, u32[]{:S(2)}) copy-start(bf16[3,512,256]{2,1,0:T(8,128)(2,1)S(1)} %collective-permute-done.r1) | copy-start | bytes 2359300
  30.7 17.7 %copy-start.7 = (bf16[3,512,256]{2,1,0:T(8,128)(2,1)}, bf16[3,512,256]{2,1,0:T(8,128)(2,1)S(1)}, u32[]{:S(2)}) copy-start(bf16[3,512,256]{2,1,0:T(8,128)(2,1)S(1)} %collective-permute-done.1.r3) | copy-start | bytes 2359300
  31.9 17.3 %all-to-all-start.1 = ((bf16[4,4,128,256]{3,2,1,0:T(8,128)(2,1)}), bf16[4,4,128,256]{3,2,1,0:T(8,128)(2,1)S(1)}, u32[]{:S(2)}, u32[]{:S(2)}) async-start(bf16[4,4,128,256]{3,2,1,0:T(8,128)(2,1)} %broadcast_in_dim.5), calls=%async_computation.1 | async-start | bytes 2097152 | tf_op jit(solution)/shard_map/all_to_all | solution.py:42
  36.8 9.2 %collective-permute-start.3 = (bf16[3,256,256]{2,1,0:T(8,128)(2,1)S(1)}, bf16[3,256,256]{2,1,0:T(8,128)(2,1)S(1)}, u32[]{:S(2)}, u32[]{:S(2)}) collective-permute-start(bf16[3,256,256]{2,1,0:T(8,128)(2,1)S(1)} %slice.16), channel_id=1, source_target_pairs={{0,24},{8,0},{16,8},{24,16},{1,25},{9,1},{17,9},{25,17},{2,26},{10... | collective-permute-start | bytes 1179656 | tf_op jit(solution)/shard_map/ppermute | solution.py:16
  39.4 9.1 %collective-permute-start.2 = (bf16[3,256,256]{2,1,0:T(8,128)(2,1)S(1)}, bf16[3,256,256]{2,1,0:T(8,128)(2,1)}, u32[]{:S(2)}, u32[]{:S(2)}) collective-permute-start(bf16[3,256,256]{2,1,0:T(8,128)(2,1)S(1)} %slice.15), channel_id=1, source_target_pairs={{0,8},{8,16},{16,24},{24,0},{1,9},{9,17},{17,25},{25,1},{2,10},{10... | collective-permute-start | bytes 1179656 | tf_op jit(solution)/shard_map/ppermute | solution.py:16
  46.0 5.9 %copy-start.10 = (bf16[3,256,256]{2,1,0:T(8,128)(2,1)}, bf16[3,256,256]{2,1,0:T(8,128)(2,1)S(1)}, u32[]{:S(2)}) copy-start(bf16[3,256,256]{2,1,0:T(8,128)(2,1)S(1)} %collective-permute-done.3.r2b) | copy-start | bytes 1179652
  49.2 2.7 %copy-start.1 = (bf16[4,4,128,256]{3,2,1,0:T(8,128)(2,1)}, bf16[4,4,128,256]{3,2,1,0:T(8,128)(2,1)S(1)}, u32[]{:S(2)}) copy-start(bf16[4,4,128,256]{3,2,1,0:T(8,128)(2,1)S(1)} %all-to-all-done.1.own) | copy-start | bytes 3145732
  49.2 2.7 %collective-permute-start.4 = (bf16[4,4,128,256]{3,2,1,0:T(8,128)(2,1)S(1)}, bf16[4,4,128,256]{3,2,1,0:T(8,128)(2,1)S(1)}, u32[]{:S(2)}, u32[]{:S(2)}) collective-permute-start(bf16[4,4,128,256]{3,2,1,0:T(8,128)(2,1)S(1)} %all-to-all-done.1.own), channel_id=1, source_target_pairs={{0,1},{1,0},{2,3},{3,2},{4,5},{5,4},{6,7},{7,6},{8,9},{9,8},{10,11... | collective-permute-start | bytes 3145736 | tf_op jit(solution)/shard_map/ppermute | solution.py:16
  51.9 1.0 copy-start.2
  58.6 2.0 %collective-permute-start.5 = (bf16[3,256,256]{2,1,0:T(8,128)(2,1)}, bf16[3,256,256]{2,1,0:T(8,128)(2,1)S(1)}, u32[]{:S(2)}, u32[]{:S(2)}) collective-permute-start(bf16[3,256,256]{2,1,0:T(8,128)(2,1)} %get-tuple-element.23), channel_id=1, source_target_pairs={{0,1},{1,0},{2,3},{3,2},{4,5},{5,4},{6,7},{7,6},{8,9},{9,8},{10,11... | collective-permute-start | bytes 1179656 | tf_op jit(solution)/shard_map/ppermute | solution.py:16
  61.7 32.6 %copy-start.3 = (bf16[2,3,256,256]{3,2,1,0:T(8,128)(2,1)}, bf16[2,3,256,256]{3,2,1,0:T(8,128)(2,1)S(1)}, u32[]{:S(2)}) copy-start(bf16[2,3,256,256]{3,2,1,0:T(8,128)(2,1)S(1)} %pad_maximum_fusion.w0) | copy-start | bytes 2359300
  61.7 20.9 %collective-permute-start.7 = (bf16[2,3,256,256]{3,2,1,0:T(8,128)(2,1)S(1)}, bf16[2,3,256,256]{3,2,1,0:T(8,128)(2,1)S(1)}, u32[]{:S(2)}, u32[]{:S(2)}) collective-permute-start(bf16[2,3,256,256]{3,2,1,0:T(8,128)(2,1)S(1)} %pad_maximum_fusion.w0), channel_id=1, source_target_pairs={{0,8},{8,16},{16,24},{24,0},{1,9},{9,17},{17,25},{25,1},{2,10},{10... | collective-permute-start | bytes 2359304 | tf_op jit(solution)/shard_map/ppermute | solution.py:16
  61.8 20.9 %collective-permute-start.6 = (bf16[2,3,256,256]{3,2,1,0:T(8,128)(2,1)S(1)}, bf16[2,3,256,256]{3,2,1,0:T(8,128)(2,1)S(1)}, u32[]{:S(2)}, u32[]{:S(2)}) collective-permute-start(bf16[2,3,256,256]{3,2,1,0:T(8,128)(2,1)S(1)} %pad_maximum_fusion.w0), channel_id=1, source_target_pairs={{0,24},{8,0},{16,8},{24,16},{1,25},{9,1},{17,9},{25,17},{2,26},{10... | collective-permute-start | bytes 2359304 | tf_op jit(solution)/shard_map/ppermute | solution.py:16
  82.6 11.7 %copy-start.4 = (bf16[2,3,256,256]{3,2,1,0:T(8,128)(2,1)}, bf16[2,3,256,256]{3,2,1,0:T(8,128)(2,1)S(1)}, u32[]{:S(2)}) copy-start(bf16[2,3,256,256]{3,2,1,0:T(8,128)(2,1)S(1)} %collective-permute-done.7.w3) | copy-start | bytes 2359300
  82.6 11.6 %collective-permute-start.8 = (bf16[3,256,256]{2,1,0:T(8,128)(2,1)S(1)}, bf16[3,256,256]{2,1,0:T(8,128)(2,1)S(1)}, u32[]{:S(2)}, u32[]{:S(2)}) collective-permute-start(bf16[3,256,256]{2,1,0:T(8,128)(2,1)S(1)} %slice_bitcast_fusion.1), channel_id=1, source_target_pairs={{0,8},{8,16},{16,24},{24,0},{1,9},{9,17},{17,25},{25,1},{2,10},{10... | collective-permute-start | bytes 1179656 | tf_op jit(solution)/shard_map/ppermute | solution.py:16
  82.8 11.6 %copy-start.5 = (bf16[2,3,256,256]{3,2,1,0:T(8,128)(2,1)}, bf16[2,3,256,256]{3,2,1,0:T(8,128)(2,1)S(1)}, u32[]{:S(2)}) copy-start(bf16[2,3,256,256]{3,2,1,0:T(8,128)(2,1)S(1)} %collective-permute-done.6.w1) | copy-start | bytes 2359300
  82.8 11.5 %collective-permute-start.9 = (bf16[3,256,256]{2,1,0:T(8,128)(2,1)S(1)}, bf16[3,256,256]{2,1,0:T(8,128)(2,1)S(1)}, u32[]{:S(2)}, u32[]{:S(2)}) collective-permute-start(bf16[3,256,256]{2,1,0:T(8,128)(2,1)S(1)} %slice_bitcast_fusion), channel_id=1, source_target_pairs={{0,24},{8,0},{16,8},{24,16},{1,25},{9,1},{17,9},{25,17},{2,26},{10... | collective-permute-start | bytes 1179656 | tf_op jit(solution)/shard_map/ppermute | solution.py:16
  94.3 0.8 copy-start.8
  94.3 1.0 copy-start.9
  100.1 44.4 %copy-start = (bf16[512,256]{1,0:T(8,128)(2,1)S(1)}, bf16[512,256]{1,0:T(8,128)(2,1)}, u32[]{:S(2)}) copy-start(bf16[512,256]{1,0:T(8,128)(2,1)} %psi.1) | copy-start | bytes 786436
  116.7 6.1 %collective-permute-start.10 = (f32[8,128]{1,0:T(8,128)S(1)}, f32[8,128]{1,0:T(8,128)S(1)}, u32[]{:S(2)}, u32[]{:S(2)}) collective-permute-start(f32[8,128]{1,0:T(8,128)S(1)} %get-tuple-element.25), channel_id=1, source_target_pairs={{0,0},{3,1},{2,2},{5,3},{4,4},{7,5},{6,6},{9,7},{8,8},{11,9},{10,1... | collective-permute-start | bytes 12296 | tf_op jit(solution)/shard_map/ppermute | solution.py:26
  122.8 4.5 %collective-permute-start.11 = (f32[8,128]{1,0:T(8,128)S(1)}, f32[8,128]{1,0:T(8,128)S(1)}, u32[]{:S(2)}, u32[]{:S(2)}) collective-permute-start(f32[8,128]{1,0:T(8,128)S(1)} %collective-permute-done.10.one), channel_id=1, source_target_pairs={{0,1},{1,0},{2,3},{3,2},{4,5},{5,4},{6,7},{7,6},{8,9},{9,8},{10,11... | collective-permute-start | bytes 12296 | tf_op jit(solution)/shard_map/ppermute | solution.py:16
Sparse Core Ops, SparseCore 0:
  10.4 70.9 all-gather.2

commit v3 on v2

--- a/solution.py
+++ b/solution.py
@@ -42,6 +42,21 @@
     return lax.all_to_all(jnp.broadcast_to(x[None], (n, *x.shape)), axis, 0, 0, tiled=True)
 
 
+def wide_kernel(x, out, held, sems):
+    wait(start([(x, held)], sems.at[pl.ds(4, 1)]))
+    wait(start([(held, out.at[i]) for i in range(4)], sems))
+
+
+def column_kernel(place, q0, q1, q2, q3, out):
+    for e, q in enumerate((q0, q1, q2, q3)):
+        out[lax.rem(place[1] + e, 4)] = q[...]
+
+
+def panel_kernel(place, x0, x1, x2, x3, out):
+    for g, x in enumerate((x0, x1, x2, x3)):
+        out[lax.rem(place[3] + g, 4)] = x[...]
+
+
 def start(moves, sems):
     copies = [pltpu.make_async_copy(a, b, sems.at[i]) for i, (a, b) in enumerate(moves)]
     for copy in copies:
@@ -54,13 +69,14 @@
         copy.wait()
 
 
-def first_kernel(place, own, sib, r0, r1, r2a, r2b, r3, keep, send, psi, right, sems):
+def first_kernel(place, own, sib, r0, r1, r2a, r2b, r3, v1, v2a, v2b, v3, keep, send, psi, right, sems):
     m, c = place[0], place[2]
     first = start([(own, psi.at[c]), (sib, psi.at[1 - c])], sems.at[3])
     slots = []
     for s in range(3):
-        moves = [(r0.at[s], right.at[0, s]), (r1.at[s], right.at[1, s]), (r3.at[s], right.at[3, s])]
-        moves += [(r2a.at[s], right.at[2, s, pl.ds(0, 256)]), (r2b.at[s], right.at[2, s, pl.ds(256, 256)])]
+        i, (one, low, high, three) = (s, (r1, r2a, r2b, r3)) if s < 2 else (0, (v1, v2a, v2b, v3))
+        moves = [(r0.at[s], right.at[0, s]), (one.at[i], right.at[1, s]), (three.at[i], right.at[3, s])]
+        moves += [(low.at[i], right.at[2, s, pl.ds(0, 256)]), (high.at[i], right.at[2, s, pl.ds(256, 256)])]
         slots.append(start(moves, sems.at[s]))
     wait(first)
     for s in range(3):
@@ -171,19 +187,33 @@
     a = lax.axis_index("x")
     place = jnp.stack([m, l, c, a, term_count[0]]).astype(jnp.int32)
 
-    left = lax.all_gather(left_ops, "zhi")
 
     quarter = lax.dynamic_slice_in_dim(psi, a * 128, 128, 0)
-    r1, r3 = shift(right_ops_t, "row", 4, 3), shift(right_ops_t, "row", 4, 1)
-    column = spread_to(quarter, "zhi")
-    column, r1, r3 = together(column, r1, r3)
+    most, last = right_ops_t[:2], right_ops_t[2:]
+    r1, r3 = shift(most, "row", 4, 3), shift(most, "row", 4, 1)
+    q1, q2, q3 = [shift(quarter, "zhi", 4, k) for k in (3, 2, 1)]
+    wide = pl.pallas_call(
+        wide_kernel,
+        out_shape=jax.ShapeDtypeStruct((4, 3, 512, 256), BF16),
+        in_specs=[HBM],
+        out_specs=HBM,
+        scratch_shapes=[pltpu.VMEM((3, 512, 256), BF16), pltpu.SemaphoreType.DMA((5,))],
+        compiler_params=pltpu.CompilerParams(vmem_limit_bytes=56 << 20),
+        cost_estimate=pl.CostEstimate(flops=0, bytes_accessed=1 << 10, transcendentals=0),
+    )(left_ops)
+    quarter, q1, q2, q3, r1, r3, last, left = together(quarter, q1, q2, q3, r1, r3, last, wide)
+    left = lax.all_to_all(left, "zhi", 0, 0, tiled=True)
+    v1, v3 = shift(last, "row", 4, 3), shift(last, "row", 4, 1)
+    (column,) = call(column_kernel, [((4, 128, 256), BF16)], [SMEM] + [VMEM] * 4, place, quarter, q1, q2, q3)
+    x1, x2, x3 = [shift(column, "x", 4, k) for k in (3, 2, 1)]
     r2a, r2b = far(r1, r3, "row", 1)
-    own = spread_to(column, "x")
-    own, r2a, r2b = together(own, r2a, r2b)
+    column, x1, x2, x3, r2a, r2b, v1, v3 = together(column, x1, x2, x3, r2a, r2b, v1, v3)
+    v2a, v2b = far(v1, v3, "row", 1)
+    (own,) = call(panel_kernel, [((4, 4, 128, 256), BF16)], [SMEM] + [VMEM] * 4, place, column, x1, x2, x3)
     sib = shift(own, "core", 2, 1)
     keep, send = call(
-        first_kernel, [((3, 256, 256), BF16)] * 2, [SMEM] + [HBM] * 7,
-        place, own, sib, right_ops_t, r1, r2a, r2b, r3,
+        first_kernel, [((3, 256, 256), BF16)] * 2, [SMEM] + [HBM] * 11,
+        place, own, sib, right_ops_t, r1, r2a, r2b, r3, v1, v2a, v2b, v3,
         scratch=[pltpu.VMEM((2, 4, 4, 128, 256), BF16), pltpu.VMEM((4, 3, 512, 256), BF16), pltpu.SemaphoreType.DMA((4, 5))],
         limit=56,
     )

time: 154 us -> 149 us (0.968)
  starting transfers between devices: 25.8 us -> 44.4 us
  blocking collectives: 52.8 us -> 35 us
  between operations: 14.9 us -> 1.58 us
  Pallas kernels: 11.7 us -> 16.3 us
  waiting for transfers between devices: 41.3 us -> 44 us
    all_to_all x1 -> x0, blocking collectives: 19.1 us -> none  [spread_to(): lax.all_to_all(jnp.broadcast_to(x[None], (n, *x.shape)), axis, 0, 0, tile...]
    ppermute x11 -> x21, starting transfers between devices: 16.2 us -> 34.6 us  [shift(): return lax.ppermute(x, axis, [(i, (i + k) % n) for i in range(n)])]
    pallas_call x0 -> x1, Pallas kernels: none -> 2.82 us  [per_device(): pl.pallas_call(wide_kernel, out_shape=jax.ShapeDtypeStruct((4, 3, 512, 25...]
    all_to_all x1, blocking collectives: 17.2 us -> 19.6 us  [per_device(): full = lax.all_to_all(spread, TERMS, 0, 0, tiled=True)]
    slice x0 -> x2, local copies, waits for them, and re-layouts: none -> 2.05 us  [per_device(): most, last = (right_ops_t[:2], right_ops_t[2:])]
    all_to_all x1, waiting for transfers between devices: 0.73 us -> 2.59 us  [per_device(): left = lax.all_to_all(left, 'zhi', 0, 0, tiled=True)]
    pallas_call x5 -> x7, Pallas kernels: 11.7 us -> 13.4 us  [call(): pl.pallas_call(kernel, out_shape=[jax.ShapeDtypeStruct(shape, dtype) for...]
    ppermute x11 -> x21, waiting for transfers between devices: 39.2 us -> 40.1 us  [shift(): return lax.ppermute(x, axis, [(i, (i + k) % n) for i in range(n)])]
  transfers between devices with their start and end apart: 14 -> 23, of which waited for: 10 -> 12; matrix products, arithmetic and copies ran while one was open for 3% -> 2% of each run, Pallas kernels for 4% -> 7%
where the time goes in v3:
time: 149 us; the launch traced here: 148 us
  starting transfers between devices  44.4 us (30%)
  waiting for transfers between devices  44 us (30%)
  blocking collectives  35 us (23%)
  Pallas kernels  16.3 us (11%)
  local copies, waits for them, and re-layouts  5.34 us (4%)
  between operations  1.58 us (1%)
    ppermute x21, waiting for transfers between devices, shift(): return lax.ppermute(x, axis, [(i, (i + k) % n) for i in range(n)])  40.1 us
    ppermute x21, starting transfers between devices, shift(): return lax.ppermute(x, axis, [(i, (i + k) % n) for i in range(n)])  34.6 us
    all_to_all x1, blocking collectives, per_device(): full = lax.all_to_all(spread, TERMS, 0, 0, tiled=True)  19.6 us
    all_to_all x1, blocking collectives, per_device(): parts = lax.all_to_all(payload, (*TERMS, 'core'), 0, 0, tiled=True)  15.5 us
    pallas_call x7, Pallas kernels, call(): pl.pallas_call(kernel, out_shape=[jax.ShapeDtypeStruct(shape, dtype) for...  13.4 us
    all_to_all x1, starting transfers between devices, per_device(): left = lax.all_to_all(left, 'zhi', 0, 0, tiled=True)  5.06 us
    ppermute x1, starting transfers between devices, fetch(): return lax.ppermute(x, (*TERMS, 'row', 'zhi', 'core'), pairs)  4.67 us
  transfers between devices with their start and end apart: 23, of which 12 were waited for; matrix products, arithmetic and copies ran while one was open for 2% of the time, Pallas kernels for 7%

profile of v3, /device:TPU:2, one launch (start us, length us, event | category | flops | bytes accessed | tf_op | source)
XLA Modules:
  0.0 147.6 jit_solution(5593949752304160027)
XLA Ops:
  0.6 1.1 slice.27
  1.7 1.7 %collective-permute-start.4 = (bf16[2,512,256]{2,1,0:T(8,128)(2,1)S(1)}, bf16[2,512,256]{2,1,0:T(8,128)(2,1)S(1)}, u32[]{:S(2)}, u32[]{:S(2)}) collective-permute-start(bf16[2,512,256]{2,1,0:T(8,128)(2,1)S(1)} %slice.27), channel_id=1, source_target_pairs={{0,8},{8,16},{16,24},{24,0},{1,9},{9,17},{17,25},{25,1},{2,10},{10... | collective-permute-start | bytes 1572872 | tf_op jit(solution)/shard_map/ppermute | solution.py:16
  3.4 1.7 %collective-permute-start.3 = (bf16[2,512,256]{2,1,0:T(8,128)(2,1)S(1)}, bf16[2,512,256]{2,1,0:T(8,128)(2,1)S(1)}, u32[]{:S(2)}, u32[]{:S(2)}) collective-permute-start(bf16[2,512,256]{2,1,0:T(8,128)(2,1)S(1)} %slice.27), channel_id=1, source_target_pairs={{0,24},{8,0},{16,8},{24,16},{1,25},{9,1},{17,9},{25,17},{2,26},{10... | collective-permute-start | bytes 1572872 | tf_op jit(solution)/shard_map/ppermute | solution.py:16
  5.0 0.8 constant_dynamic-slice_fusion.q0
  5.9 3.3 %collective-permute-start.2 = (bf16[128,256]{1,0:T(8,128)(2,1)S(1)}, bf16[128,256]{1,0:T(8,128)(2,1)S(1)}, u32[]{:S(2)}, u32[]{:S(2)}) collective-permute-start(bf16[128,256]{1,0:T(8,128)(2,1)S(1)} %constant_dynamic-slice_fusion.q0), channel_id=1, source_target_pairs={{0,2},{2,4},{4,6},{6,0},{1,3},{3,5},{5,7},{7,1},{8,10},{10,12},{12... | collective-permute-start | bytes 196616 | tf_op jit(solution)/shard_map/ppermute | solution.py:16
  9.1 5.4 %collective-permute-start.1 = (bf16[128,256]{1,0:T(8,128)(2,1)S(1)}, bf16[128,256]{1,0:T(8,128)(2,1)S(1)}, u32[]{:S(2)}, u32[]{:S(2)}) collective-permute-start(bf16[128,256]{1,0:T(8,128)(2,1)S(1)} %constant_dynamic-slice_fusion.q0), channel_id=1, source_target_pairs={{0,4},{2,6},{4,0},{6,2},{1,5},{3,7},{5,1},{7,3},{8,12},{10,14},{12... | collective-permute-start | bytes 196616 | tf_op jit(solution)/shard_map/ppermute | solution.py:16
  14.5 2.7 %collective-permute-start = (bf16[128,256]{1,0:T(8,128)(2,1)S(1)}, bf16[128,256]{1,0:T(8,128)(2,1)S(1)}, u32[]{:S(2)}, u32[]{:S(2)}) collective-permute-start(bf16[128,256]{1,0:T(8,128)(2,1)S(1)} %constant_dynamic-slice_fusion.q0), channel_id=1, source_target_pairs={{0,6},{2,0},{4,2},{6,4},{1,7},{3,1},{5,3},{7,5},{8,14},{10,8},{12,... | collective-permute-start | bytes 196616 | tf_op jit(solution)/shard_map/ppermute | solution.py:16
  17.2 1.0 slice.28
  18.2 2.8 %shard_map.67 = bf16[4,3,512,256]{3,2,1,0:T(8,128)(2,1)} custom-call(bf16[3,512,256]{2,1,0:T(8,128)(2,1)} %x.1), custom_call_target="tpu_custom_call" | custom-call | bytes 1024 | tf_op jit(solution)/shard_map/pallas_call | solution.py:195
  21.0 0.1 collective-permute-done.q1
  21.2 5.1 %all-to-all-start = ((bf16[4,3,512,256]{3,2,1,0:T(8,128)(2,1)}), bf16[4,3,512,256]{3,2,1,0:T(8,128)(2,1)}, u32[]{:S(2)}, u32[]{:S(2)}) async-start(bf16[4,3,512,256]{3,2,1,0:T(8,128)(2,1)} %shard_map.67), calls=%async_computation | async-start | bytes 6291456 | tf_op jit(solution)/shard_map/all_to_all | solution.py:205
  26.3 2.1 %collective-permute-start.9 = (bf16[2,256,256]{2,1,0:T(8,128)(2,1)S(1)}, bf16[2,256,256]{2,1,0:T(8,128)(2,1)S(1)}, u32[]{:S(2)}, u32[]{:S(2)}) collective-permute-start(bf16[2,256,256]{2,1,0:T(8,128)(2,1)S(1)} %slice.30), channel_id=1, source_target_pairs={{0,24},{8,0},{16,8},{24,16},{1,25},{9,1},{17,9},{25,17},{2,26},{10... | collective-permute-start | bytes 786440 | tf_op jit(solution)/shard_map/ppermute | solution.py:16
  28.4 0.1 collective-permute-start.8
  29.2 0.6 shard_map.68.x0
  29.8 1.6 %collective-permute-start.7 = (bf16[4,128,256]{2,1,0:T(8,128)(2,1)S(1)}, bf16[4,128,256]{2,1,0:T(8,128)(2,1)S(1)}, u32[]{:S(2)}, u32[]{:S(2)}) collective-permute-start(bf16[4,128,256]{2,1,0:T(8,128)(2,1)S(1)} %shard_map.68.x0), channel_id=1, source_target_pairs={{0,64},{64,128},{128,192},{192,0},{1,65},{65,129},{129,193},{193,1... | collective-permute-start | bytes 786440 | tf_op jit(solution)/shard_map/ppermute | solution.py:16
  31.3 1.1 collective-permute-start.6
  32.5 2.2 %collective-permute-start.5 = (bf16[4,128,256]{2,1,0:T(8,128)(2,1)S(1)}, bf16[4,128,256]{2,1,0:T(8,128)(2,1)S(1)}, u32[]{:S(2)}, u32[]{:S(2)}) collective-permute-start(bf16[4,128,256]{2,1,0:T(8,128)(2,1)S(1)} %shard_map.68.x0), channel_id=1, source_target_pairs={{0,192},{64,0},{128,64},{192,128},{1,193},{65,1},{129,65},{193,129... | collective-permute-start | bytes 786440 | tf_op jit(solution)/shard_map/ppermute | solution.py:16
  34.6 0.5 collective-permute-start.11
  35.2 0.9 collective-permute-done.8.r2a
  36.1 1.8 %collective-permute-start.10 = (bf16[1,512,256]{2,1,0:T(8,128)(2,1)S(1)}, bf16[1,512,256]{2,1,0:T(8,128)(2,1)S(1)}, u32[]{:S(2)}, u32[]{:S(2)}) collective-permute-start(bf16[1,512,256]{2,1,0:T(8,128)(2,1)S(1)} %slice.28), channel_id=1, source_target_pairs={{0,24},{8,0},{16,8},{24,16},{1,25},{9,1},{17,9},{25,17},{2,26},{10... | collective-permute-start | bytes 786440 | tf_op jit(solution)/shard_map/ppermute | solution.py:16
  37.9 1.2 collective-permute-done.7.x3
  39.1 3.0 %collective-permute-done.6.x2 = bf16[4,128,256]{2,1,0:T(8,128)(2,1)S(1)} collective-permute-done((bf16[4,128,256]{2,1,0:T(8,128)(2,1)S(1)}, bf16[4,128,256]{2,1,0:T(8,128)(2,1)S(1)}, u32[]{:S(2)}, u32[]{:S(2)}) %collective-permute-start.6) | collective-permute-done | bytes 262176 | tf_op jit(solution)/shard_map/ppermute | solution.py:16
  42.1 2.3 %collective-permute-done.5.x1 = bf16[4,128,256]{2,1,0:T(8,128)(2,1)S(1)} collective-permute-done((bf16[4,128,256]{2,1,0:T(8,128)(2,1)S(1)}, bf16[4,128,256]{2,1,0:T(8,128)(2,1)S(1)}, u32[]{:S(2)}, u32[]{:S(2)}) %collective-permute-start.5) | collective-permute-done | bytes 262176 | tf_op jit(solution)/shard_map/ppermute | solution.py:16
  44.5 0.6 shard_map.69.own
  45.2 0.4 collective-permute-start.13
  45.6 2.9 %collective-permute-start.14 = (bf16[1,256,256]{2,1,0:T(8,128)(2,1)S(1)}, bf16[1,256,256]{2,1,0:T(8,128)(2,1)S(1)}, u32[]{:S(2)}, u32[]{:S(2)}) collective-permute-start(bf16[1,256,256]{2,1,0:T(8,128)(2,1)S(1)} %slice.32), channel_id=1, source_target_pairs={{0,24},{8,0},{16,8},{24,16},{1,25},{9,1},{17,9},{25,17},{2,26},{10... | collective-permute-start | bytes 393224 | tf_op jit(solution)/shard_map/ppermute | solution.py:16
  48.6 3.9 %collective-permute-done.13.v2a = bf16[1,256,256]{2,1,0:T(8,128)(2,1)S(1)} collective-permute-done((bf16[1,256,256]{2,1,0:T(8,128)(2,1)S(1)}, bf16[1,256,256]{2,1,0:T(8,128)(2,1)S(1)}, u32[]{:S(2)}, u32[]{:S(2)}) %collective-permute-start.13) | collective-permute-done | bytes 131104 | tf_op jit(solution)/shard_map/ppermute | solution.py:16
  52.5 0.6 copy-done.15
  53.1 1.1 copy-done.3
  54.2 5.7 %shard_map.70 = (bf16[3,256,256]{2,1,0:T(8,128)(2,1)}, bf16[3,256,256]{2,1,0:T(8,128)(2,1)}) custom-call(s32[5]{0:T(128)} %copy-done.2, bf16[4,4,128,256]{3,2,1,0:T(8,128)(2,1)} %copy-done, bf16[4,4,128,256]{3,2,1,0:T(8,128)(2,1)} %copy-done.3, bf16[3,512,256]{2,1,0:T(8,128)(2,1)} %r0.1, bf16[2,512,256]{2,1,0:T(8,128)(2,1)} %copy-done.8, ...), custom_call_target="tpu_custom_call" | custom-call | bytes 1024 | tf_op jit(solution)/shard_map/pallas_call | solution.py:174
  60.0 1.9 %collective-permute-done.15 = bf16[3,256,256]{2,1,0:T(8,128)(2,1)S(1)} collective-permute-done((bf16[3,256,256]{2,1,0:T(8,128)(2,1)}, bf16[3,256,256]{2,1,0:T(8,128)(2,1)S(1)}, u32[]{:S(2)}, u32[]{:S(2)}) %collective-permute-start.15) | collective-permute-done | bytes 393248 | tf_op jit(solution)/shard_map/ppermute | solution.py:16
  61.9 1.1 pad_maximum_fusion.w0
  63.0 0.7 collective-permute-start.17
  63.7 2.6 %collective-permute-start.16 = (bf16[2,3,256,256]{3,2,1,0:T(8,128)(2,1)S(1)}, bf16[2,3,256,256]{3,2,1,0:T(8,128)(2,1)S(1)}, u32[]{:S(2)}, u32[]{:S(2)}) collective-permute-start(bf16[2,3,256,256]{3,2,1,0:T(8,128)(2,1)S(1)} %pad_maximum_fusion.w0), channel_id=1, source_target_pairs={{0,24},{8,0},{16,8},{24,16},{1,25},{9,1},{17,9},{25,17},{2,26},{10... | collective-permute-start | bytes 2359304 | tf_op jit(solution)/shard_map/ppermute | solution.py:16
  66.3 17.6 %collective-permute-done.17.w3 = bf16[2,3,256,256]{3,2,1,0:T(8,128)(2,1)S(1)} collective-permute-done((bf16[2,3,256,256]{3,2,1,0:T(8,128)(2,1)S(1)}, bf16[2,3,256,256]{3,2,1,0:T(8,128)(2,1)S(1)}, u32[]{:S(2)}, u32[]{:S(2)}) %collective-permute-start.17) | collective-permute-done | bytes 786464 | tf_op jit(solution)/shard_map/ppermute | solution.py:16
  84.0 3.3 %collective-permute-start.19 = (bf16[3,256,256]{2,1,0:T(8,128)(2,1)S(1)}, bf16[3,256,256]{2,1,0:T(8,128)(2,1)S(1)}, u32[]{:S(2)}, u32[]{:S(2)}) collective-permute-start(bf16[3,256,256]{2,1,0:T(8,128)(2,1)S(1)} %slice_bitcast_fusion), channel_id=1, source_target_pairs={{0,24},{8,0},{16,8},{24,16},{1,25},{9,1},{17,9},{25,17},{2,26},{10... | collective-permute-start | bytes 1179656 | tf_op jit(solution)/shard_map/ppermute | solution.py:16
  87.3 8.3 %collective-permute-done.18.w2a = bf16[3,256,256]{2,1,0:T(8,128)(2,1)S(1)} collective-permute-done((bf16[3,256,256]{2,1,0:T(8,128)(2,1)S(1)}, bf16[3,256,256]{2,1,0:T(8,128)(2,1)S(1)}, u32[]{:S(2)}, u32[]{:S(2)}) %collective-permute-start.18) | collective-permute-done | bytes 393248 | tf_op jit(solution)/shard_map/ppermute | solution.py:16
  95.6 2.6 %all-to-all-done.left = bf16[4,3,512,256]{3,2,1,0:T(8,128)(2,1)} async-done(((bf16[4,3,512,256]{3,2,1,0:T(8,128)(2,1)}), bf16[4,3,512,256]{3,2,1,0:T(8,128)(2,1)}, u32[]{:S(2)}, u32[]{:S(2)}) %all-to-all-start) | async-done | bytes 3145760 | tf_op jit(solution)/shard_map/all_to_all | solution.py:205
  98.2 5.5 %shard_map.71 = bf16[16,80,256]{2,1,0:T(8,128)(2,1)} custom-call(s32[5]{0:T(128)} %copy-done.2, bf16[4,3,512,256]{3,2,1,0:T(8,128)(2,1)} %all-to-all-done.left, bf16[2,3,256,256]{3,2,1,0:T(8,128)(2,1)} %copy-done.4, bf16[2,3,256,256]{3,2,1,0:T(8,128)(2,1)} %copy-done.6, bf16[3,256,256]{2,1,0:T(8,128)(2,1)} %copy-done.11, bf16[3,256,256]{2,1,0:T(8,128)(2,1)} %copy-done.12, ...), custom_call_target="tpu_custom_call" | custom-call | bytes 1024 | tf_op jit(solution)/shard_map/pallas_call | solution.py:174
  103.8 15.5 %all_to_all.15.parts = bf16[16,80,256]{2,1,0:T(8,128)(2,1)S(1)} all-to-all(bf16[16,80,256]{2,1,0:T(8,128)(2,1)} %shard_map.71), channel_id=1, replica_groups=mesh['x'=4,'zlo'=2,'row'=4,'zhi'=4,'core'=2] {'x','zlo','core'}, dimensions={0} | all-to-all | bytes 1310720 | tf_op jit(solution)/shard_map/all_to_all | solution.py:235
  119.3 0.1 shard_map.72
  119.4 4.7 %collective-permute-start.20 = (f32[8,128]{1,0:T(8,128)S(1)}, f32[8,128]{1,0:T(8,128)S(1)}, u32[]{:S(2)}, u32[]{:S(2)}) collective-permute-start(f32[8,128]{1,0:T(8,128)S(1)} %get-tuple-element.45), channel_id=1, source_target_pairs={{0,0},{3,1},{2,2},{5,3},{4,4},{7,5},{6,6},{9,7},{8,8},{11,9},{10,1... | collective-permute-start | bytes 12296 | tf_op jit(solution)/shard_map/ppermute | solution.py:26
  124.0 1.3 collective-permute-done.20.one
  125.3 0.4 collective-permute-start.21
  125.8 0.8 collective-permute-done.21.other
  126.7 19.6 %all_to_all.16.parts = f32[8,72,256]{2,1,0:T(8,128)S(1)} all-to-all(f32[8,72,256]{2,1,0:T(8,128)S(1)} %shard_map.73), channel_id=1, replica_groups=mesh['x'=4,'zlo'=2,'row'=4,'zhi'=4,'core'=2] {'x','zlo'}, dimensions={0} | all-to-all | bytes 1179648 | tf_op jit(solution)/shard_map/all_to_all | solution.py:240
  146.2 0.9 shard_map.74
  147.1 0.5 slice.35
  (54 shorter events, 0.6 us)
Async XLA Ops:
  1.7 19.4 %collective-permute-start.4 = (bf16[2,512,256]{2,1,0:T(8,128)(2,1)S(1)}, bf16[2,512,256]{2,1,0:T(8,128)(2,1)S(1)}, u32[]{:S(2)}, u32[]{:S(2)}) collective-permute-start(bf16[2,512,256]{2,1,0:T(8,128)(2,1)S(1)} %slice.27), channel_id=1, source_target_pairs={{0,8},{8,16},{16,24},{24,0},{1,9},{9,17},{17,25},{25,1},{2,10},{10... | collective-permute-start | bytes 1572872 | tf_op jit(solution)/shard_map/ppermute | solution.py:16
  3.4 17.8 %collective-permute-start.3 = (bf16[2,512,256]{2,1,0:T(8,128)(2,1)S(1)}, bf16[2,512,256]{2,1,0:T(8,128)(2,1)S(1)}, u32[]{:S(2)}, u32[]{:S(2)}) collective-permute-start(bf16[2,512,256]{2,1,0:T(8,128)(2,1)S(1)} %slice.27), channel_id=1, source_target_pairs={{0,24},{8,0},{16,8},{24,16},{1,25},{9,1},{17,9},{25,17},{2,26},{10... | collective-permute-start | bytes 1572872 | tf_op jit(solution)/shard_map/ppermute | solution.py:16
  5.9 15.1 %collective-permute-start.2 = (bf16[128,256]{1,0:T(8,128)(2,1)S(1)}, bf16[128,256]{1,0:T(8,128)(2,1)S(1)}, u32[]{:S(2)}, u32[]{:S(2)}) collective-permute-start(bf16[128,256]{1,0:T(8,128)(2,1)S(1)} %constant_dynamic-slice_fusion.q0), channel_id=1, source_target_pairs={{0,2},{2,4},{4,6},{6,0},{1,3},{3,5},{5,7},{7,1},{8,10},{10,12},{12... | collective-permute-start | bytes 196616 | tf_op jit(solution)/shard_map/ppermute | solution.py:16
  9.1 11.9 %collective-permute-start.1 = (bf16[128,256]{1,0:T(8,128)(2,1)S(1)}, bf16[128,256]{1,0:T(8,128)(2,1)S(1)}, u32[]{:S(2)}, u32[]{:S(2)}) collective-permute-start(bf16[128,256]{1,0:T(8,128)(2,1)S(1)} %constant_dynamic-slice_fusion.q0), channel_id=1, source_target_pairs={{0,4},{2,6},{4,0},{6,2},{1,5},{3,7},{5,1},{7,3},{8,12},{10,14},{12... | collective-permute-start | bytes 196616 | tf_op jit(solution)/shard_map/ppermute | solution.py:16
  14.5 6.6 %collective-permute-start = (bf16[128,256]{1,0:T(8,128)(2,1)S(1)}, bf16[128,256]{1,0:T(8,128)(2,1)S(1)}, u32[]{:S(2)}, u32[]{:S(2)}) collective-permute-start(bf16[128,256]{1,0:T(8,128)(2,1)S(1)} %constant_dynamic-slice_fusion.q0), channel_id=1, source_target_pairs={{0,6},{2,0},{4,2},{6,4},{1,7},{3,1},{5,3},{7,5},{8,14},{10,8},{12,... | collective-permute-start | bytes 196616 | tf_op jit(solution)/shard_map/ppermute | solution.py:16
  21.2 7.2 %copy-start.7 = (bf16[2,512,256]{2,1,0:T(8,128)(2,1)}, bf16[2,512,256]{2,1,0:T(8,128)(2,1)S(1)}, u32[]{:S(2)}) copy-start(bf16[2,512,256]{2,1,0:T(8,128)(2,1)S(1)} %collective-permute-done.4.r3) | copy-start | bytes 1572868
  21.2 5.1 %copy-start.8 = (bf16[2,512,256]{2,1,0:T(8,128)(2,1)}, bf16[2,512,256]{2,1,0:T(8,128)(2,1)S(1)}, u32[]{:S(2)}) copy-start(bf16[2,512,256]{2,1,0:T(8,128)(2,1)S(1)} %collective-permute-done.3.r1) | copy-start | bytes 1572868
  21.2 77.0 %all-to-all-start = ((bf16[4,3,512,256]{3,2,1,0:T(8,128)(2,1)}), bf16[4,3,512,256]{3,2,1,0:T(8,128)(2,1)}, u32[]{:S(2)}, u32[]{:S(2)}) async-start(bf16[4,3,512,256]{3,2,1,0:T(8,128)(2,1)} %shard_map.67), calls=%async_computation | async-start | bytes 6291456 | tf_op jit(solution)/shard_map/all_to_all | solution.py:205
  26.3 8.4 %collective-permute-start.9 = (bf16[2,256,256]{2,1,0:T(8,128)(2,1)S(1)}, bf16[2,256,256]{2,1,0:T(8,128)(2,1)S(1)}, u32[]{:S(2)}, u32[]{:S(2)}) collective-permute-start(bf16[2,256,256]{2,1,0:T(8,128)(2,1)S(1)} %slice.30), channel_id=1, source_target_pairs={{0,24},{8,0},{16,8},{24,16},{1,25},{9,1},{17,9},{25,17},{2,26},{10... | collective-permute-start | bytes 786440 | tf_op jit(solution)/shard_map/ppermute | solution.py:16
  28.4 7.7 %collective-permute-start.8 = (bf16[2,256,256]{2,1,0:T(8,128)(2,1)S(1)}, bf16[2,256,256]{2,1,0:T(8,128)(2,1)S(1)}, u32[]{:S(2)}, u32[]{:S(2)}) collective-permute-start(bf16[2,256,256]{2,1,0:T(8,128)(2,1)S(1)} %slice.29), channel_id=1, source_target_pairs={{0,8},{8,16},{16,24},{24,0},{1,9},{9,17},{17,25},{25,1},{2,10},{10... | collective-permute-start | bytes 786440 | tf_op jit(solution)/shard_map/ppermute | solution.py:16
  29.2 23.2 %copy-start.2 = (s32[5]{0:T(128)}, s32[5]{0:T(128)S(1)}, u32[]{:S(2)}) copy-start(s32[5]{0:T(128)S(1)} %stack.28.place) | copy-start | bytes 64
  29.8 9.3 %collective-permute-start.7 = (bf16[4,128,256]{2,1,0:T(8,128)(2,1)S(1)}, bf16[4,128,256]{2,1,0:T(8,128)(2,1)S(1)}, u32[]{:S(2)}, u32[]{:S(2)}) collective-permute-start(bf16[4,128,256]{2,1,0:T(8,128)(2,1)S(1)} %shard_map.68.x0), channel_id=1, source_target_pairs={{0,64},{64,128},{128,192},{192,0},{1,65},{65,129},{129,193},{193,1... | collective-permute-start | bytes 786440 | tf_op jit(solution)/shard_map/ppermute | solution.py:16
  31.3 10.8 %collective-permute-start.6 = (bf16[4,128,256]{2,1,0:T(8,128)(2,1)S(1)}, bf16[4,128,256]{2,1,0:T(8,128)(2,1)S(1)}, u32[]{:S(2)}, u32[]{:S(2)}) collective-permute-start(bf16[4,128,256]{2,1,0:T(8,128)(2,1)S(1)} %shard_map.68.x0), channel_id=1, source_target_pairs={{0,128},{64,192},{128,0},{192,64},{1,129},{65,193},{129,1},{193,65... | collective-permute-start | bytes 786440 | tf_op jit(solution)/shard_map/ppermute | solution.py:16
  32.5 12.0 %collective-permute-start.5 = (bf16[4,128,256]{2,1,0:T(8,128)(2,1)S(1)}, bf16[4,128,256]{2,1,0:T(8,128)(2,1)S(1)}, u32[]{:S(2)}, u32[]{:S(2)}) collective-permute-start(bf16[4,128,256]{2,1,0:T(8,128)(2,1)S(1)} %shard_map.68.x0), channel_id=1, source_target_pairs={{0,192},{64,0},{128,64},{192,128},{1,193},{65,1},{129,65},{193,129... | collective-permute-start | bytes 786440 | tf_op jit(solution)/shard_map/ppermute | solution.py:16
  34.6 17.8 %copy-start.13 = (bf16[2,256,256]{2,1,0:T(8,128)(2,1)}, bf16[2,256,256]{2,1,0:T(8,128)(2,1)S(1)}, u32[]{:S(2)}) copy-start(bf16[2,256,256]{2,1,0:T(8,128)(2,1)S(1)} %collective-permute-done.9.r2b) | copy-start | bytes 786436
  34.6 9.8 %collective-permute-start.11 = (bf16[1,512,256]{2,1,0:T(8,128)(2,1)S(1)}, bf16[1,512,256]{2,1,0:T(8,128)(2,1)S(1)}, u32[]{:S(2)}, u32[]{:S(2)}) collective-permute-start(bf16[1,512,256]{2,1,0:T(8,128)(2,1)S(1)} %slice.28), channel_id=1, source_target_pairs={{0,8},{8,16},{16,24},{24,0},{1,9},{9,17},{17,25},{25,1},{2,10},{10... | collective-permute-start | bytes 786440 | tf_op jit(solution)/shard_map/ppermute | solution.py:16
  36.1 16.4 %copy-start.14 = (bf16[2,256,256]{2,1,0:T(8,128)(2,1)}, bf16[2,256,256]{2,1,0:T(8,128)(2,1)S(1)}, u32[]{:S(2)}) copy-start(bf16[2,256,256]{2,1,0:T(8,128)(2,1)S(1)} %collective-permute-done.8.r2a) | copy-start | bytes 786436
  36.1 8.3 %collective-permute-start.10 = (bf16[1,512,256]{2,1,0:T(8,128)(2,1)S(1)}, bf16[1,512,256]{2,1,0:T(8,128)(2,1)S(1)}, u32[]{:S(2)}, u32[]{:S(2)}) collective-permute-start(bf16[1,512,256]{2,1,0:T(8,128)(2,1)S(1)} %slice.28), channel_id=1, source_target_pairs={{0,24},{8,0},{16,8},{24,16},{1,25},{9,1},{17,9},{25,17},{2,26},{10... | collective-permute-start | bytes 786440 | tf_op jit(solution)/shard_map/ppermute | solution.py:16
  44.5 8.0 %copy-start.9 = (bf16[1,512,256]{2,1,0:T(8,128)(2,1)}, bf16[1,512,256]{2,1,0:T(8,128)(2,1)S(1)}, u32[]{:S(2)}) copy-start(bf16[1,512,256]{2,1,0:T(8,128)(2,1)S(1)} %collective-permute-done.11.v3) | copy-start | bytes 786436
  44.5 8.0 %copy-start.10 = (bf16[1,512,256]{2,1,0:T(8,128)(2,1)}, bf16[1,512,256]{2,1,0:T(8,128)(2,1)S(1)}, u32[]{:S(2)}) copy-start(bf16[1,512,256]{2,1,0:T(8,128)(2,1)S(1)} %collective-permute-done.10.v1) | copy-start | bytes 786436
  45.1 7.4 %copy-start = (bf16[4,4,128,256]{3,2,1,0:T(8,128)(2,1)}, bf16[4,4,128,256]{3,2,1,0:T(8,128)(2,1)S(1)}, u32[]{:S(2)}) copy-start(bf16[4,4,128,256]{3,2,1,0:T(8,128)(2,1)S(1)} %shard_map.69.own) | copy-start | bytes 3145732
  45.1 7.3 %collective-permute-start.12 = (bf16[4,4,128,256]{3,2,1,0:T(8,128)(2,1)S(1)}, bf16[4,4,128,256]{3,2,1,0:T(8,128)(2,1)S(1)}, u32[]{:S(2)}, u32[]{:S(2)}) collective-permute-start(bf16[4,4,128,256]{3,2,1,0:T(8,128)(2,1)S(1)} %shard_map.69.own), channel_id=1, source_target_pairs={{0,1},{1,0},{2,3},{3,2},{4,5},{5,4},{6,7},{7,6},{8,9},{9,8},{10,11... | collective-permute-start | bytes 3145736 | tf_op jit(solution)/shard_map/ppermute | solution.py:16
  45.2 7.2 %collective-permute-start.13 = (bf16[1,256,256]{2,1,0:T(8,128)(2,1)S(1)}, bf16[1,256,256]{2,1,0:T(8,128)(2,1)S(1)}, u32[]{:S(2)}, u32[]{:S(2)}) collective-permute-start(bf16[1,256,256]{2,1,0:T(8,128)(2,1)S(1)} %slice.31), channel_id=1, source_target_pairs={{0,8},{8,16},{16,24},{24,0},{1,9},{9,17},{17,25},{25,1},{2,10},{10... | collective-permute-start | bytes 393224 | tf_op jit(solution)/shard_map/ppermute | solution.py:16
  45.6 6.8 %collective-permute-start.14 = (bf16[1,256,256]{2,1,0:T(8,128)(2,1)S(1)}, bf16[1,256,256]{2,1,0:T(8,128)(2,1)S(1)}, u32[]{:S(2)}, u32[]{:S(2)}) collective-permute-start(bf16[1,256,256]{2,1,0:T(8,128)(2,1)S(1)} %slice.32), channel_id=1, source_target_pairs={{0,24},{8,0},{16,8},{24,16},{1,25},{9,1},{17,9},{25,17},{2,26},{10... | collective-permute-start | bytes 393224 | tf_op jit(solution)/shard_map/ppermute | solution.py:16
  52.4 0.6 copy-start.15
  52.4 0.7 copy-start.16
  53.1 1.1 copy-start.3
  59.9 2.0 %collective-permute-start.15 = (bf16[3,256,256]{2,1,0:T(8,128)(2,1)}, bf16[3,256,256]{2,1,0:T(8,128)(2,1)S(1)}, u32[]{:S(2)}, u32[]{:S(2)}) collective-permute-start(bf16[3,256,256]{2,1,0:T(8,128)(2,1)} %get-tuple-element.43), channel_id=1, source_target_pairs={{0,1},{1,0},{2,3},{3,2},{4,5},{5,4},{6,7},{7,6},{8,9},{9,8},{10,11... | collective-permute-start | bytes 1179656 | tf_op jit(solution)/shard_map/ppermute | solution.py:16
  63.0 35.2 %copy-start.4 = (bf16[2,3,256,256]{3,2,1,0:T(8,128)(2,1)}, bf16[2,3,256,256]{3,2,1,0:T(8,128)(2,1)S(1)}, u32[]{:S(2)}) copy-start(bf16[2,3,256,256]{3,2,1,0:T(8,128)(2,1)S(1)} %pad_maximum_fusion.w0) | copy-start | bytes 2359300
  63.0 20.9 %collective-permute-start.17 = (bf16[2,3,256,256]{3,2,1,0:T(8,128)(2,1)S(1)}, bf16[2,3,256,256]{3,2,1,0:T(8,128)(2,1)S(1)}, u32[]{:S(2)}, u32[]{:S(2)}) collective-permute-start(bf16[2,3,256,256]{3,2,1,0:T(8,128)(2,1)S(1)} %pad_maximum_fusion.w0), channel_id=1, source_target_pairs={{0,8},{8,16},{16,24},{24,0},{1,9},{9,17},{17,25},{25,1},{2,10},{10... | collective-permute-start | bytes 2359304 | tf_op jit(solution)/shard_map/ppermute | solution.py:16
  63.7 20.3 %collective-permute-start.16 = (bf16[2,3,256,256]{3,2,1,0:T(8,128)(2,1)S(1)}, bf16[2,3,256,256]{3,2,1,0:T(8,128)(2,1)S(1)}, u32[]{:S(2)}, u32[]{:S(2)}) collective-permute-start(bf16[2,3,256,256]{3,2,1,0:T(8,128)(2,1)S(1)} %pad_maximum_fusion.w0), channel_id=1, source_target_pairs={{0,24},{8,0},{16,8},{24,16},{1,25},{9,1},{17,9},{25,17},{2,26},{10... | collective-permute-start | bytes 2359304 | tf_op jit(solution)/shard_map/ppermute | solution.py:16
  83.9 14.4 %copy-start.5 = (bf16[2,3,256,256]{3,2,1,0:T(8,128)(2,1)}, bf16[2,3,256,256]{3,2,1,0:T(8,128)(2,1)S(1)}, u32[]{:S(2)}) copy-start(bf16[2,3,256,256]{3,2,1,0:T(8,128)(2,1)S(1)} %collective-permute-done.17.w3) | copy-start | bytes 2359300
  83.9 11.7 %collective-permute-start.18 = (bf16[3,256,256]{2,1,0:T(8,128)(2,1)S(1)}, bf16[3,256,256]{2,1,0:T(8,128)(2,1)S(1)}, u32[]{:S(2)}, u32[]{:S(2)}) collective-permute-start(bf16[3,256,256]{2,1,0:T(8,128)(2,1)S(1)} %slice_bitcast_fusion.1), channel_id=1, source_target_pairs={{0,8},{8,16},{16,24},{24,0},{1,9},{9,17},{17,25},{25,1},{2,10},{10... | collective-permute-start | bytes 1179656 | tf_op jit(solution)/shard_map/ppermute | solution.py:16
  84.0 14.2 %copy-start.6 = (bf16[2,3,256,256]{3,2,1,0:T(8,128)(2,1)}, bf16[2,3,256,256]{3,2,1,0:T(8,128)(2,1)S(1)}, u32[]{:S(2)}) copy-start(bf16[2,3,256,256]{3,2,1,0:T(8,128)(2,1)S(1)} %collective-permute-done.16.w1) | copy-start | bytes 2359300
  84.0 11.6 %collective-permute-start.19 = (bf16[3,256,256]{2,1,0:T(8,128)(2,1)S(1)}, bf16[3,256,256]{2,1,0:T(8,128)(2,1)S(1)}, u32[]{:S(2)}, u32[]{:S(2)}) collective-permute-start(bf16[3,256,256]{2,1,0:T(8,128)(2,1)S(1)} %slice_bitcast_fusion), channel_id=1, source_target_pairs={{0,24},{8,0},{16,8},{24,16},{1,25},{9,1},{17,9},{25,17},{2,26},{10... | collective-permute-start | bytes 1179656 | tf_op jit(solution)/shard_map/ppermute | solution.py:16
  95.6 2.6 %copy-start.11 = (bf16[3,256,256]{2,1,0:T(8,128)(2,1)}, bf16[3,256,256]{2,1,0:T(8,128)(2,1)S(1)}, u32[]{:S(2)}) copy-start(bf16[3,256,256]{2,1,0:T(8,128)(2,1)S(1)} %collective-permute-done.18.w2a) | copy-start | bytes 1179652
  95.6 2.6 %copy-start.12 = (bf16[3,256,256]{2,1,0:T(8,128)(2,1)}, bf16[3,256,256]{2,1,0:T(8,128)(2,1)S(1)}, u32[]{:S(2)}) copy-start(bf16[3,256,256]{2,1,0:T(8,128)(2,1)S(1)} %collective-permute-done.19.w2b) | copy-start | bytes 1179652
  103.8 42.4 %copy-start.1 = (bf16[512,256]{1,0:T(8,128)(2,1)S(1)}, bf16[512,256]{1,0:T(8,128)(2,1)}, u32[]{:S(2)}) copy-start(bf16[512,256]{1,0:T(8,128)(2,1)} %psi.1) | copy-start | bytes 786436
  119.4 6.0 %collective-permute-start.20 = (f32[8,128]{1,0:T(8,128)S(1)}, f32[8,128]{1,0:T(8,128)S(1)}, u32[]{:S(2)}, u32[]{:S(2)}) collective-permute-start(f32[8,128]{1,0:T(8,128)S(1)} %get-tuple-element.45), channel_id=1, source_target_pairs={{0,0},{3,1},{2,2},{5,3},{4,4},{7,5},{6,6},{9,7},{8,8},{11,9},{10,1... | collective-permute-start | bytes 12296 | tf_op jit(solution)/shard_map/ppermute | solution.py:26
  125.3 1.3 collective-permute-start.21

commit v4 on v3

--- a/solution.py
+++ b/solution.py
@@ -14,16 +14,6 @@
 
 def shift(x, axis, n, k):
     return lax.ppermute(x, axis, [(i, (i + k) % n) for i in range(n)])
-
-
-def fetch(x):
-    pairs = []
-    for t in range(8):
-        for at in range(16):
-            for c in range(2):
-                source = (at + 2 * t + c) % 16
-                pairs.append((t * 32 + source * 2 + c, t * 32 + at * 2 + c))
-    return lax.ppermute(x, (*TERMS, "row", "zhi", "core"), pairs)
 
 
 def together(*xs):
@@ -141,31 +131,21 @@
     chunk = parts[0].astype(F32)
     for part in range(1, 16):
         chunk += parts[part].astype(F32)
-    out[...] = chunk[0:64]
+    for part in range(8):
+        out[part] = chunk[0:64]
     for i in range(2):
         one = chunk[64 + 4 * i : 68 + 4 * i].sum(0, keepdims=True).sum(1, keepdims=True)
         sums[i : i + 1] = jnp.broadcast_to(one, (1, 128))
     sums[2:8] = jnp.zeros((6, 128), F32)
 
 
-def spread_kernel(chunk, one, other, out):
-    for part in range(8):
-        out[part, 0:64] = chunk[...]
-        out[part, 64:72, 0:128] = one[...]
-        out[part, 64:72, 128:256] = other[...]
-
-
-def last_kernel(parts, psi, sigma, residual, energy):
-    tail = parts[0, 64:72]
-    for part in range(1, 8):
-        tail += parts[part, 64:72]
-    tail = tail[:, 0:128] + tail[:, 128:256]
-    ratio = jnp.broadcast_to(tail[0:1] / (tail[1:2] * 0.125), (8, 128))
-    energy[...] = ratio
+def last_kernel(parts, sums, psi, sigma, residual, energy):
+    ratio = jnp.broadcast_to(sums[0:1] / (sums[1:2] * 0.125), (8, 128))
+    energy[...] = ratio[0:1, 0:1]
     row = jnp.concatenate([ratio[0:1], ratio[0:1]], axis=1)
     for part in range(8):
         rows = slice(part * 64, (part + 1) * 64)
-        full = parts[part, 0:64]
+        full = parts[part]
         sigma[rows] = full.astype(BF16)
         residual[rows] = (full - row * psi[rows].astype(F32)).astype(BF16)
 
@@ -233,15 +213,14 @@
     )
 
     parts = lax.all_to_all(payload, (*TERMS, "core"), 0, 0, tiled=True)
-    chunk, sums = call(third_kernel, [((64, 256), F32), ((8, 128), F32)], [VMEM], parts)
-    one = fetch(sums)
-    other = shift(one, "core", 2, 1)
-    (spread,) = call(spread_kernel, [((8, 72, 256), F32)], [VMEM] * 3, chunk, one, other)
-    full = lax.all_to_all(spread, TERMS, 0, 0, tiled=True)
+    chunk, sums = call(third_kernel, [((8, 64, 256), F32), ((8, 128), F32)], [VMEM], parts)
+    full = lax.all_to_all(chunk, TERMS, 0, 0, tiled=True)
+    for axis in ("row", "zhi"):
+        sums = sums + shift(sums, axis, 4, 1) + shift(sums, axis, 4, 2) + shift(sums, axis, 4, 3)
     sigma, residual, energy = call(
-        last_kernel, [((512, 256), BF16), ((512, 256), BF16), ((8, 128), F32)], [VMEM] * 2, full, psi
-    )
-    return sigma, residual, energy[0, 0]
+        last_kernel, [((512, 256), BF16), ((512, 256), BF16), ((1, 1), F32)], [VMEM] * 3, full, sums, psi
+    )
+    return sigma, residual, energy.reshape(())
 
 
 def solution(mesh):

time: 149 us -> 146 us (0.980)
  blocking collectives: 35 us -> 15.7 us
  starting transfers between devices: 44.4 us -> 57 us
  waiting for transfers between devices: 44 us -> 47.6 us
    all_to_all x1 -> x0, blocking collectives: 19.6 us -> none  [per_device(): full = lax.all_to_all(spread, TERMS, 0, 0, tiled=True)]
    ppermute x21 -> x26, starting transfers between devices: 34.6 us -> 46.6 us  [shift(): return lax.ppermute(x, axis, [(i, (i + k) % n) for i in range(n)])]
    ppermute x21 -> x26, waiting for transfers between devices: 40.1 us -> 47.2 us  [shift(): return lax.ppermute(x, axis, [(i, (i + k) % n) for i in range(n)])]
    all_to_all x0 -> x1, starting transfers between devices: none -> 5.36 us  [per_device(): full = lax.all_to_all(chunk, TERMS, 0, 0, tiled=True)]
    ppermute x1 -> x0, starting transfers between devices: 4.67 us -> none  [fetch(): return lax.ppermute(x, (*TERMS, 'row', 'zhi', 'core'), pairs)]
    all_to_all x1, waiting for transfers between devices: 2.59 us -> 0.32 us  [per_device(): left = lax.all_to_all(left, 'zhi', 0, 0, tiled=True)]
    pallas_call x7 -> x6, Pallas kernels: 13.4 us -> 14.2 us  [call(): pl.pallas_call(kernel, out_shape=[jax.ShapeDtypeStruct(shape, dtype) for...]
  transfers between devices with their start and end apart: 23 -> 28, of which waited for: 12 -> 15; matrix products, arithmetic and copies ran while one was open for 2% -> 2% of each run, Pallas kernels for 7% -> 7%
where the time goes in v4:
time: 146 us; the launch traced here: 145 us
  starting transfers between devices  57 us (39%)
  waiting for transfers between devices  47.6 us (33%)
  Pallas kernels  17 us (12%)
  blocking collectives  15.7 us (11%)
  local copies, waits for them, and re-layouts  5.35 us (4%)
  between operations  1.57 us (1%)
    ppermute x26, waiting for transfers between devices, shift(): return lax.ppermute(x, axis, [(i, (i + k) % n) for i in range(n)])  47.2 us
    ppermute x26, starting transfers between devices, shift(): return lax.ppermute(x, axis, [(i, (i + k) % n) for i in range(n)])  46.6 us
    all_to_all x1, blocking collectives, per_device(): parts = lax.all_to_all(payload, (*TERMS, 'core'), 0, 0, tiled=True)  15.7 us
    pallas_call x6, Pallas kernels, call(): pl.pallas_call(kernel, out_shape=[jax.ShapeDtypeStruct(shape, dtype) for...  14.2 us
    all_to_all x1, starting transfers between devices, per_device(): full = lax.all_to_all(chunk, TERMS, 0, 0, tiled=True)  5.36 us
    all_to_all x1, starting transfers between devices, per_device(): left = lax.all_to_all(left, 'zhi', 0, 0, tiled=True)  5.06 us
  transfers between devices with their start and end apart: 28, of which 15 were waited for; matrix products, arithmetic and copies ran while one was open for 2% of the time, Pallas kernels for 7%

profile of v4, /device:TPU:2, one launch (start us, length us, event | category | flops | bytes accessed | tf_op | source)
XLA Modules:
  0.0 145.2 jit_solution(5892418554766882101)
XLA Ops:
  0.6 1.1 slice.24
  1.7 1.7 %collective-permute-start.4 = (bf16[2,512,256]{2,1,0:T(8,128)(2,1)S(1)}, bf16[2,512,256]{2,1,0:T(8,128)(2,1)S(1)}, u32[]{:S(2)}, u32[]{:S(2)}) collective-permute-start(bf16[2,512,256]{2,1,0:T(8,128)(2,1)S(1)} %slice.24), channel_id=1, source_target_pairs={{0,8},{8,16},{16,24},{24,0},{1,9},{9,17},{17,25},{25,1},{2,10},{10... | collective-permute-start | bytes 1572872 | tf_op jit(solution)/shard_map/ppermute | solution.py:16
  3.4 1.7 %collective-permute-start.3 = (bf16[2,512,256]{2,1,0:T(8,128)(2,1)S(1)}, bf16[2,512,256]{2,1,0:T(8,128)(2,1)S(1)}, u32[]{:S(2)}, u32[]{:S(2)}) collective-permute-start(bf16[2,512,256]{2,1,0:T(8,128)(2,1)S(1)} %slice.24), channel_id=1, source_target_pairs={{0,24},{8,0},{16,8},{24,16},{1,25},{9,1},{17,9},{25,17},{2,26},{10... | collective-permute-start | bytes 1572872 | tf_op jit(solution)/shard_map/ppermute | solution.py:16
  5.0 0.8 constant_dynamic-slice_fusion.q0
  5.9 3.3 %collective-permute-start.2 = (bf16[128,256]{1,0:T(8,128)(2,1)S(1)}, bf16[128,256]{1,0:T(8,128)(2,1)S(1)}, u32[]{:S(2)}, u32[]{:S(2)}) collective-permute-start(bf16[128,256]{1,0:T(8,128)(2,1)S(1)} %constant_dynamic-slice_fusion.q0), channel_id=1, source_target_pairs={{0,2},{2,4},{4,6},{6,0},{1,3},{3,5},{5,7},{7,1},{8,10},{10,12},{12... | collective-permute-start | bytes 196616 | tf_op jit(solution)/shard_map/ppermute | solution.py:16
  9.1 5.4 %collective-permute-start.1 = (bf16[128,256]{1,0:T(8,128)(2,1)S(1)}, bf16[128,256]{1,0:T(8,128)(2,1)S(1)}, u32[]{:S(2)}, u32[]{:S(2)}) collective-permute-start(bf16[128,256]{1,0:T(8,128)(2,1)S(1)} %constant_dynamic-slice_fusion.q0), channel_id=1, source_target_pairs={{0,4},{2,6},{4,0},{6,2},{1,5},{3,7},{5,1},{7,3},{8,12},{10,14},{12... | collective-permute-start | bytes 196616 | tf_op jit(solution)/shard_map/ppermute | solution.py:16
  14.5 2.7 %collective-permute-start = (bf16[128,256]{1,0:T(8,128)(2,1)S(1)}, bf16[128,256]{1,0:T(8,128)(2,1)S(1)}, u32[]{:S(2)}, u32[]{:S(2)}) collective-permute-start(bf16[128,256]{1,0:T(8,128)(2,1)S(1)} %constant_dynamic-slice_fusion.q0), channel_id=1, source_target_pairs={{0,6},{2,0},{4,2},{6,4},{1,7},{3,1},{5,3},{7,5},{8,14},{10,8},{12,... | collective-permute-start | bytes 196616 | tf_op jit(solution)/shard_map/ppermute | solution.py:16
  17.2 1.0 slice.25
  18.2 2.8 %shard_map.67 = bf16[4,3,512,256]{3,2,1,0:T(8,128)(2,1)} custom-call(bf16[3,512,256]{2,1,0:T(8,128)(2,1)} %x.1), custom_call_target="tpu_custom_call" | custom-call | bytes 1024 | tf_op jit(solution)/shard_map/pallas_call | solution.py:175
  21.2 5.1 %all-to-all-start = ((bf16[4,3,512,256]{3,2,1,0:T(8,128)(2,1)}), bf16[4,3,512,256]{3,2,1,0:T(8,128)(2,1)}, u32[]{:S(2)}, u32[]{:S(2)}) async-start(bf16[4,3,512,256]{3,2,1,0:T(8,128)(2,1)} %shard_map.67), calls=%async_computation | async-start | bytes 6291456 | tf_op jit(solution)/shard_map/all_to_all | solution.py:185
  26.3 2.1 %collective-permute-start.9 = (bf16[2,256,256]{2,1,0:T(8,128)(2,1)S(1)}, bf16[2,256,256]{2,1,0:T(8,128)(2,1)S(1)}, u32[]{:S(2)}, u32[]{:S(2)}) collective-permute-start(bf16[2,256,256]{2,1,0:T(8,128)(2,1)S(1)} %slice.27), channel_id=1, source_target_pairs={{0,24},{8,0},{16,8},{24,16},{1,25},{9,1},{17,9},{25,17},{2,26},{10... | collective-permute-start | bytes 786440 | tf_op jit(solution)/shard_map/ppermute | solution.py:16
  29.2 0.6 shard_map.68.x0
  29.8 1.6 %collective-permute-start.7 = (bf16[4,128,256]{2,1,0:T(8,128)(2,1)S(1)}, bf16[4,128,256]{2,1,0:T(8,128)(2,1)S(1)}, u32[]{:S(2)}, u32[]{:S(2)}) collective-permute-start(bf16[4,128,256]{2,1,0:T(8,128)(2,1)S(1)} %shard_map.68.x0), channel_id=1, source_target_pairs={{0,64},{64,128},{128,192},{192,0},{1,65},{65,129},{129,193},{193,1... | collective-permute-start | bytes 786440 | tf_op jit(solution)/shard_map/ppermute | solution.py:16
  31.3 1.1 collective-permute-start.6
  32.5 2.2 %collective-permute-start.5 = (bf16[4,128,256]{2,1,0:T(8,128)(2,1)S(1)}, bf16[4,128,256]{2,1,0:T(8,128)(2,1)S(1)}, u32[]{:S(2)}, u32[]{:S(2)}) collective-permute-start(bf16[4,128,256]{2,1,0:T(8,128)(2,1)S(1)} %shard_map.68.x0), channel_id=1, source_target_pairs={{0,192},{64,0},{128,64},{192,128},{1,193},{65,1},{129,65},{193,129... | collective-permute-start | bytes 786440 | tf_op jit(solution)/shard_map/ppermute | solution.py:16
  34.6 0.5 collective-permute-start.11
  35.2 0.9 collective-permute-done.8.r2a
  36.1 1.8 %collective-permute-start.10 = (bf16[1,512,256]{2,1,0:T(8,128)(2,1)S(1)}, bf16[1,512,256]{2,1,0:T(8,128)(2,1)S(1)}, u32[]{:S(2)}, u32[]{:S(2)}) collective-permute-start(bf16[1,512,256]{2,1,0:T(8,128)(2,1)S(1)} %slice.25), channel_id=1, source_target_pairs={{0,24},{8,0},{16,8},{24,16},{1,25},{9,1},{17,9},{25,17},{2,26},{10... | collective-permute-start | bytes 786440 | tf_op jit(solution)/shard_map/ppermute | solution.py:16
  37.9 1.2 collective-permute-done.7.x3
  39.1 3.0 %collective-permute-done.6.x2 = bf16[4,128,256]{2,1,0:T(8,128)(2,1)S(1)} collective-permute-done((bf16[4,128,256]{2,1,0:T(8,128)(2,1)S(1)}, bf16[4,128,256]{2,1,0:T(8,128)(2,1)S(1)}, u32[]{:S(2)}, u32[]{:S(2)}) %collective-permute-start.6) | collective-permute-done | bytes 262176 | tf_op jit(solution)/shard_map/ppermute | solution.py:16
  42.1 2.4 %collective-permute-done.5.x1 = bf16[4,128,256]{2,1,0:T(8,128)(2,1)S(1)} collective-permute-done((bf16[4,128,256]{2,1,0:T(8,128)(2,1)S(1)}, bf16[4,128,256]{2,1,0:T(8,128)(2,1)S(1)}, u32[]{:S(2)}, u32[]{:S(2)}) %collective-permute-start.5) | collective-permute-done | bytes 262176 | tf_op jit(solution)/shard_map/ppermute | solution.py:16
  44.5 0.6 shard_map.69.own
  45.6 2.9 %collective-permute-start.14 = (bf16[1,256,256]{2,1,0:T(8,128)(2,1)S(1)}, bf16[1,256,256]{2,1,0:T(8,128)(2,1)S(1)}, u32[]{:S(2)}, u32[]{:S(2)}) collective-permute-start(bf16[1,256,256]{2,1,0:T(8,128)(2,1)S(1)} %slice.29), channel_id=1, source_target_pairs={{0,24},{8,0},{16,8},{24,16},{1,25},{9,1},{17,9},{25,17},{2,26},{10... | collective-permute-start | bytes 393224 | tf_op jit(solution)/shard_map/ppermute | solution.py:16
  48.6 3.9 %collective-permute-done.13.v2a = bf16[1,256,256]{2,1,0:T(8,128)(2,1)S(1)} collective-permute-done((bf16[1,256,256]{2,1,0:T(8,128)(2,1)S(1)}, bf16[1,256,256]{2,1,0:T(8,128)(2,1)S(1)}, u32[]{:S(2)}, u32[]{:S(2)}) %collective-permute-start.13) | collective-permute-done | bytes 131104 | tf_op jit(solution)/shard_map/ppermute | solution.py:16
  52.5 0.6 copy-done.15
  53.1 1.0 copy-done.3
  54.2 5.7 %shard_map.70 = (bf16[3,256,256]{2,1,0:T(8,128)(2,1)}, bf16[3,256,256]{2,1,0:T(8,128)(2,1)}) custom-call(s32[5]{0:T(128)} %copy-done.2, bf16[4,4,128,256]{3,2,1,0:T(8,128)(2,1)} %copy-done, bf16[4,4,128,256]{3,2,1,0:T(8,128)(2,1)} %copy-done.3, bf16[3,512,256]{2,1,0:T(8,128)(2,1)} %r0.1, bf16[2,512,256]{2,1,0:T(8,128)(2,1)} %copy-done.8, ...), custom_call_target="tpu_custom_call" | custom-call | bytes 1024 | tf_op jit(solution)/shard_map/pallas_call | solution.py:154
  60.0 1.9 %collective-permute-done.15 = bf16[3,256,256]{2,1,0:T(8,128)(2,1)S(1)} collective-permute-done((bf16[3,256,256]{2,1,0:T(8,128)(2,1)}, bf16[3,256,256]{2,1,0:T(8,128)(2,1)S(1)}, u32[]{:S(2)}, u32[]{:S(2)}) %collective-permute-start.15) | collective-permute-done | bytes 393248 | tf_op jit(solution)/shard_map/ppermute | solution.py:16
  61.9 1.1 pad_maximum_fusion.w0
  63.0 0.7 collective-permute-start.17
  63.6 2.6 %collective-permute-start.16 = (bf16[2,3,256,256]{3,2,1,0:T(8,128)(2,1)S(1)}, bf16[2,3,256,256]{3,2,1,0:T(8,128)(2,1)S(1)}, u32[]{:S(2)}, u32[]{:S(2)}) collective-permute-start(bf16[2,3,256,256]{3,2,1,0:T(8,128)(2,1)S(1)} %pad_maximum_fusion.w0), channel_id=1, source_target_pairs={{0,24},{8,0},{16,8},{24,16},{1,25},{9,1},{17,9},{25,17},{2,26},{10... | collective-permute-start | bytes 2359304 | tf_op jit(solution)/shard_map/ppermute | solution.py:16
  66.3 17.6 %collective-permute-done.17.w3 = bf16[2,3,256,256]{3,2,1,0:T(8,128)(2,1)S(1)} collective-permute-done((bf16[2,3,256,256]{3,2,1,0:T(8,128)(2,1)S(1)}, bf16[2,3,256,256]{3,2,1,0:T(8,128)(2,1)S(1)}, u32[]{:S(2)}, u32[]{:S(2)}) %collective-permute-start.17) | collective-permute-done | bytes 786464 | tf_op jit(solution)/shard_map/ppermute | solution.py:16
  84.0 3.3 %collective-permute-start.19 = (bf16[3,256,256]{2,1,0:T(8,128)(2,1)S(1)}, bf16[3,256,256]{2,1,0:T(8,128)(2,1)S(1)}, u32[]{:S(2)}, u32[]{:S(2)}) collective-permute-start(bf16[3,256,256]{2,1,0:T(8,128)(2,1)S(1)} %slice_bitcast_fusion), channel_id=1, source_target_pairs={{0,24},{8,0},{16,8},{24,16},{1,25},{9,1},{17,9},{25,17},{2,26},{10... | collective-permute-start | bytes 1179656 | tf_op jit(solution)/shard_map/ppermute | solution.py:16
  87.3 8.3 %collective-permute-done.18.w2a = bf16[3,256,256]{2,1,0:T(8,128)(2,1)S(1)} collective-permute-done((bf16[3,256,256]{2,1,0:T(8,128)(2,1)S(1)}, bf16[3,256,256]{2,1,0:T(8,128)(2,1)S(1)}, u32[]{:S(2)}, u32[]{:S(2)}) %collective-permute-start.18) | collective-permute-done | bytes 393248 | tf_op jit(solution)/shard_map/ppermute | solution.py:16
  96.5 5.5 %shard_map.71 = bf16[16,80,256]{2,1,0:T(8,128)(2,1)} custom-call(s32[5]{0:T(128)} %copy-done.2, bf16[4,3,512,256]{3,2,1,0:T(8,128)(2,1)} %all-to-all-done.left, bf16[2,3,256,256]{3,2,1,0:T(8,128)(2,1)} %copy-done.4, bf16[2,3,256,256]{3,2,1,0:T(8,128)(2,1)} %copy-done.6, bf16[3,256,256]{2,1,0:T(8,128)(2,1)} %copy-done.11, bf16[3,256,256]{2,1,0:T(8,128)(2,1)} %copy-done.12, ...), custom_call_target="tpu_custom_call" | custom-call | bytes 1024 | tf_op jit(solution)/shard_map/pallas_call | solution.py:154
  102.0 15.7 %all_to_all.15.parts = bf16[16,80,256]{2,1,0:T(8,128)(2,1)S(1)} all-to-all(bf16[16,80,256]{2,1,0:T(8,128)(2,1)} %shard_map.71), channel_id=1, replica_groups=mesh['x'=4,'zlo'=2,'row'=4,'zhi'=4,'core'=2] {'x','zlo','core'}, dimensions={0} | all-to-all | bytes 1310720 | tf_op jit(solution)/shard_map/all_to_all | solution.py:215
  117.7 0.9 shard_map.72
  118.6 5.4 %all-to-all-start.2 = ((f32[8,64,256]{2,1,0:T(8,128)}), f32[8,64,256]{2,1,0:T(8,128)S(1)}, u32[]{:S(2)}, u32[]{:S(2)}) async-start(f32[8,64,256]{2,1,0:T(8,128)} %get-tuple-element.44), calls=%async_computation.2 | async-start | bytes 1048576 | tf_op jit(solution)/shard_map/all_to_all | solution.py:217
  124.0 4.3 %collective-permute-start.22 = (f32[8,128]{1,0:T(8,128)S(1)}, f32[8,128]{1,0:T(8,128)S(1)}, u32[]{:S(2)}, u32[]{:S(2)}) collective-permute-start(f32[8,128]{1,0:T(8,128)S(1)} %get-tuple-element.45), channel_id=1, source_target_pairs={{0,24},{8,0},{16,8},{24,16},{1,25},{9,1},{17,9},{25,17},{2,26},{10... | collective-permute-start | bytes 12296 | tf_op jit(solution)/shard_map/ppermute | solution.py:16
  128.3 0.5 collective-permute-start.21
  129.2 0.4 collective-permute-done.22
  129.7 3.8 %collective-permute-done.21 = f32[8,128]{1,0:T(8,128)S(1)} collective-permute-done((f32[8,128]{1,0:T(8,128)S(1)}, f32[8,128]{1,0:T(8,128)S(1)}, u32[]{:S(2)}, u32[]{:S(2)}) %collective-permute-start.21) | collective-permute-done | bytes 4128 | tf_op jit(solution)/shard_map/ppermute | solution.py:16
  133.6 2.4 %collective-permute-start.25 = (f32[8,128]{1,0:T(8,128)S(1)}, f32[8,128]{1,0:T(8,128)S(1)}, u32[]{:S(2)}, u32[]{:S(2)}) collective-permute-start(f32[8,128]{1,0:T(8,128)S(1)} %add_add_fusion.1), channel_id=1, source_target_pairs={{0,6},{2,0},{4,2},{6,4},{1,7},{3,1},{5,3},{7,5},{8,14},{10,8},{12,... | collective-permute-start | bytes 12296 | tf_op jit(solution)/shard_map/ppermute | solution.py:16
  136.0 2.6 %collective-permute-start.24 = (f32[8,128]{1,0:T(8,128)S(1)}, f32[8,128]{1,0:T(8,128)S(1)}, u32[]{:S(2)}, u32[]{:S(2)}) collective-permute-start(f32[8,128]{1,0:T(8,128)S(1)} %add_add_fusion.1), channel_id=1, source_target_pairs={{0,4},{2,6},{4,0},{6,2},{1,5},{3,7},{5,1},{7,3},{8,12},{10,14},{12... | collective-permute-start | bytes 12296 | tf_op jit(solution)/shard_map/ppermute | solution.py:16
  138.6 2.1 %collective-permute-start.23 = (f32[8,128]{1,0:T(8,128)S(1)}, f32[8,128]{1,0:T(8,128)S(1)}, u32[]{:S(2)}, u32[]{:S(2)}) collective-permute-start(f32[8,128]{1,0:T(8,128)S(1)} %add_add_fusion.1), channel_id=1, source_target_pairs={{0,2},{2,4},{4,6},{6,0},{1,3},{3,5},{5,7},{7,1},{8,10},{10,12},{12... | collective-permute-start | bytes 12296 | tf_op jit(solution)/shard_map/ppermute | solution.py:16
  140.7 2.8 %collective-permute-done.24 = f32[8,128]{1,0:T(8,128)S(1)} collective-permute-done((f32[8,128]{1,0:T(8,128)S(1)}, f32[8,128]{1,0:T(8,128)S(1)}, u32[]{:S(2)}, u32[]{:S(2)}) %collective-permute-start.24) | collective-permute-done | bytes 4128 | tf_op jit(solution)/shard_map/ppermute | solution.py:16
  143.5 0.8 collective-permute-done.23
  144.3 0.9 shard_map.73
  (63 shorter events, 2.7 us)
Async XLA Ops:
  1.7 19.4 %collective-permute-start.4 = (bf16[2,512,256]{2,1,0:T(8,128)(2,1)S(1)}, bf16[2,512,256]{2,1,0:T(8,128)(2,1)S(1)}, u32[]{:S(2)}, u32[]{:S(2)}) collective-permute-start(bf16[2,512,256]{2,1,0:T(8,128)(2,1)S(1)} %slice.24), channel_id=1, source_target_pairs={{0,8},{8,16},{16,24},{24,0},{1,9},{9,17},{17,25},{25,1},{2,10},{10... | collective-permute-start | bytes 1572872 | tf_op jit(solution)/shard_map/ppermute | solution.py:16
  3.4 17.8 %collective-permute-start.3 = (bf16[2,512,256]{2,1,0:T(8,128)(2,1)S(1)}, bf16[2,512,256]{2,1,0:T(8,128)(2,1)S(1)}, u32[]{:S(2)}, u32[]{:S(2)}) collective-permute-start(bf16[2,512,256]{2,1,0:T(8,128)(2,1)S(1)} %slice.24), channel_id=1, source_target_pairs={{0,24},{8,0},{16,8},{24,16},{1,25},{9,1},{17,9},{25,17},{2,26},{10... | collective-permute-start | bytes 1572872 | tf_op jit(solution)/shard_map/ppermute | solution.py:16
  5.9 15.1 %collective-permute-start.2 = (bf16[128,256]{1,0:T(8,128)(2,1)S(1)}, bf16[128,256]{1,0:T(8,128)(2,1)S(1)}, u32[]{:S(2)}, u32[]{:S(2)}) collective-permute-start(bf16[128,256]{1,0:T(8,128)(2,1)S(1)} %constant_dynamic-slice_fusion.q0), channel_id=1, source_target_pairs={{0,2},{2,4},{4,6},{6,0},{1,3},{3,5},{5,7},{7,1},{8,10},{10,12},{12... | collective-permute-start | bytes 196616 | tf_op jit(solution)/shard_map/ppermute | solution.py:16
  9.1 11.9 %collective-permute-start.1 = (bf16[128,256]{1,0:T(8,128)(2,1)S(1)}, bf16[128,256]{1,0:T(8,128)(2,1)S(1)}, u32[]{:S(2)}, u32[]{:S(2)}) collective-permute-start(bf16[128,256]{1,0:T(8,128)(2,1)S(1)} %constant_dynamic-slice_fusion.q0), channel_id=1, source_target_pairs={{0,4},{2,6},{4,0},{6,2},{1,5},{3,7},{5,1},{7,3},{8,12},{10,14},{12... | collective-permute-start | bytes 196616 | tf_op jit(solution)/shard_map/ppermute | solution.py:16
  14.5 6.6 %collective-permute-start = (bf16[128,256]{1,0:T(8,128)(2,1)S(1)}, bf16[128,256]{1,0:T(8,128)(2,1)S(1)}, u32[]{:S(2)}, u32[]{:S(2)}) collective-permute-start(bf16[128,256]{1,0:T(8,128)(2,1)S(1)} %constant_dynamic-slice_fusion.q0), channel_id=1, source_target_pairs={{0,6},{2,0},{4,2},{6,4},{1,7},{3,1},{5,3},{7,5},{8,14},{10,8},{12,... | collective-permute-start | bytes 196616 | tf_op jit(solution)/shard_map/ppermute | solution.py:16
  21.2 7.2 %copy-start.7 = (bf16[2,512,256]{2,1,0:T(8,128)(2,1)}, bf16[2,512,256]{2,1,0:T(8,128)(2,1)S(1)}, u32[]{:S(2)}) copy-start(bf16[2,512,256]{2,1,0:T(8,128)(2,1)S(1)} %collective-permute-done.4.r3) | copy-start | bytes 1572868
  21.2 5.1 %copy-start.8 = (bf16[2,512,256]{2,1,0:T(8,128)(2,1)}, bf16[2,512,256]{2,1,0:T(8,128)(2,1)S(1)}, u32[]{:S(2)}) copy-start(bf16[2,512,256]{2,1,0:T(8,128)(2,1)S(1)} %collective-permute-done.3.r1) | copy-start | bytes 1572868
  21.2 74.7 %all-to-all-start = ((bf16[4,3,512,256]{3,2,1,0:T(8,128)(2,1)}), bf16[4,3,512,256]{3,2,1,0:T(8,128)(2,1)}, u32[]{:S(2)}, u32[]{:S(2)}) async-start(bf16[4,3,512,256]{3,2,1,0:T(8,128)(2,1)} %shard_map.67), calls=%async_computation | async-start | bytes 6291456 | tf_op jit(solution)/shard_map/all_to_all | solution.py:185
  26.3 8.4 %collective-permute-start.9 = (bf16[2,256,256]{2,1,0:T(8,128)(2,1)S(1)}, bf16[2,256,256]{2,1,0:T(8,128)(2,1)S(1)}, u32[]{:S(2)}, u32[]{:S(2)}) collective-permute-start(bf16[2,256,256]{2,1,0:T(8,128)(2,1)S(1)} %slice.27), channel_id=1, source_target_pairs={{0,24},{8,0},{16,8},{24,16},{1,25},{9,1},{17,9},{25,17},{2,26},{10... | collective-permute-start | bytes 786440 | tf_op jit(solution)/shard_map/ppermute | solution.py:16
  28.4 7.7 %collective-permute-start.8 = (bf16[2,256,256]{2,1,0:T(8,128)(2,1)S(1)}, bf16[2,256,256]{2,1,0:T(8,128)(2,1)S(1)}, u32[]{:S(2)}, u32[]{:S(2)}) collective-permute-start(bf16[2,256,256]{2,1,0:T(8,128)(2,1)S(1)} %slice.26), channel_id=1, source_target_pairs={{0,8},{8,16},{16,24},{24,0},{1,9},{9,17},{17,25},{25,1},{2,10},{10... | collective-permute-start | bytes 786440 | tf_op jit(solution)/shard_map/ppermute | solution.py:16
  29.2 23.2 %copy-start.2 = (s32[5]{0:T(128)}, s32[5]{0:T(128)S(1)}, u32[]{:S(2)}) copy-start(s32[5]{0:T(128)S(1)} %stack.28.place) | copy-start | bytes 64
  29.8 9.3 %collective-permute-start.7 = (bf16[4,128,256]{2,1,0:T(8,128)(2,1)S(1)}, bf16[4,128,256]{2,1,0:T(8,128)(2,1)S(1)}, u32[]{:S(2)}, u32[]{:S(2)}) collective-permute-start(bf16[4,128,256]{2,1,0:T(8,128)(2,1)S(1)} %shard_map.68.x0), channel_id=1, source_target_pairs={{0,64},{64,128},{128,192},{192,0},{1,65},{65,129},{129,193},{193,1... | collective-permute-start | bytes 786440 | tf_op jit(solution)/shard_map/ppermute | solution.py:16
  31.3 10.8 %collective-permute-start.6 = (bf16[4,128,256]{2,1,0:T(8,128)(2,1)S(1)}, bf16[4,128,256]{2,1,0:T(8,128)(2,1)S(1)}, u32[]{:S(2)}, u32[]{:S(2)}) collective-permute-start(bf16[4,128,256]{2,1,0:T(8,128)(2,1)S(1)} %shard_map.68.x0), channel_id=1, source_target_pairs={{0,128},{64,192},{128,0},{192,64},{1,129},{65,193},{129,1},{193,65... | collective-permute-start | bytes 786440 | tf_op jit(solution)/shard_map/ppermute | solution.py:16
  32.5 12.0 %collective-permute-start.5 = (bf16[4,128,256]{2,1,0:T(8,128)(2,1)S(1)}, bf16[4,128,256]{2,1,0:T(8,128)(2,1)S(1)}, u32[]{:S(2)}, u32[]{:S(2)}) collective-permute-start(bf16[4,128,256]{2,1,0:T(8,128)(2,1)S(1)} %shard_map.68.x0), channel_id=1, source_target_pairs={{0,192},{64,0},{128,64},{192,128},{1,193},{65,1},{129,65},{193,129... | collective-permute-start | bytes 786440 | tf_op jit(solution)/shard_map/ppermute | solution.py:16
  34.6 17.8 %copy-start.13 = (bf16[2,256,256]{2,1,0:T(8,128)(2,1)}, bf16[2,256,256]{2,1,0:T(8,128)(2,1)S(1)}, u32[]{:S(2)}) copy-start(bf16[2,256,256]{2,1,0:T(8,128)(2,1)S(1)} %collective-permute-done.9.r2b) | copy-start | bytes 786436
  34.6 9.8 %collective-permute-start.11 = (bf16[1,512,256]{2,1,0:T(8,128)(2,1)S(1)}, bf16[1,512,256]{2,1,0:T(8,128)(2,1)S(1)}, u32[]{:S(2)}, u32[]{:S(2)}) collective-permute-start(bf16[1,512,256]{2,1,0:T(8,128)(2,1)S(1)} %slice.25), channel_id=1, source_target_pairs={{0,8},{8,16},{16,24},{24,0},{1,9},{9,17},{17,25},{25,1},{2,10},{10... | collective-permute-start | bytes 786440 | tf_op jit(solution)/shard_map/ppermute | solution.py:16
  36.1 16.4 %copy-start.14 = (bf16[2,256,256]{2,1,0:T(8,128)(2,1)}, bf16[2,256,256]{2,1,0:T(8,128)(2,1)S(1)}, u32[]{:S(2)}) copy-start(bf16[2,256,256]{2,1,0:T(8,128)(2,1)S(1)} %collective-permute-done.8.r2a) | copy-start | bytes 786436
  36.1 8.4 %collective-permute-start.10 = (bf16[1,512,256]{2,1,0:T(8,128)(2,1)S(1)}, bf16[1,512,256]{2,1,0:T(8,128)(2,1)S(1)}, u32[]{:S(2)}, u32[]{:S(2)}) collective-permute-start(bf16[1,512,256]{2,1,0:T(8,128)(2,1)S(1)} %slice.25), channel_id=1, source_target_pairs={{0,24},{8,0},{16,8},{24,16},{1,25},{9,1},{17,9},{25,17},{2,26},{10... | collective-permute-start | bytes 786440 | tf_op jit(solution)/shard_map/ppermute | solution.py:16
  44.5 8.0 %copy-start.9 = (bf16[1,512,256]{2,1,0:T(8,128)(2,1)}, bf16[1,512,256]{2,1,0:T(8,128)(2,1)S(1)}, u32[]{:S(2)}) copy-start(bf16[1,512,256]{2,1,0:T(8,128)(2,1)S(1)} %collective-permute-done.11.v3) | copy-start | bytes 786436
  44.5 8.0 %copy-start.10 = (bf16[1,512,256]{2,1,0:T(8,128)(2,1)}, bf16[1,512,256]{2,1,0:T(8,128)(2,1)S(1)}, u32[]{:S(2)}) copy-start(bf16[1,512,256]{2,1,0:T(8,128)(2,1)S(1)} %collective-permute-done.10.v1) | copy-start | bytes 786436
  45.1 7.4 %copy-start = (bf16[4,4,128,256]{3,2,1,0:T(8,128)(2,1)}, bf16[4,4,128,256]{3,2,1,0:T(8,128)(2,1)S(1)}, u32[]{:S(2)}) copy-start(bf16[4,4,128,256]{3,2,1,0:T(8,128)(2,1)S(1)} %shard_map.69.own) | copy-start | bytes 3145732
  45.1 7.3 %collective-permute-start.12 = (bf16[4,4,128,256]{3,2,1,0:T(8,128)(2,1)S(1)}, bf16[4,4,128,256]{3,2,1,0:T(8,128)(2,1)S(1)}, u32[]{:S(2)}, u32[]{:S(2)}) collective-permute-start(bf16[4,4,128,256]{3,2,1,0:T(8,128)(2,1)S(1)} %shard_map.69.own), channel_id=1, source_target_pairs={{0,1},{1,0},{2,3},{3,2},{4,5},{5,4},{6,7},{7,6},{8,9},{9,8},{10,11... | collective-permute-start | bytes 3145736 | tf_op jit(solution)/shard_map/ppermute | solution.py:16
  45.2 7.2 %collective-permute-start.13 = (bf16[1,256,256]{2,1,0:T(8,128)(2,1)S(1)}, bf16[1,256,256]{2,1,0:T(8,128)(2,1)S(1)}, u32[]{:S(2)}, u32[]{:S(2)}) collective-permute-start(bf16[1,256,256]{2,1,0:T(8,128)(2,1)S(1)} %slice.28), channel_id=1, source_target_pairs={{0,8},{8,16},{16,24},{24,0},{1,9},{9,17},{17,25},{25,1},{2,10},{10... | collective-permute-start | bytes 393224 | tf_op jit(solution)/shard_map/ppermute | solution.py:16
  45.6 6.8 %collective-permute-start.14 = (bf16[1,256,256]{2,1,0:T(8,128)(2,1)S(1)}, bf16[1,256,256]{2,1,0:T(8,128)(2,1)S(1)}, u32[]{:S(2)}, u32[]{:S(2)}) collective-permute-start(bf16[1,256,256]{2,1,0:T(8,128)(2,1)S(1)} %slice.29), channel_id=1, source_target_pairs={{0,24},{8,0},{16,8},{24,16},{1,25},{9,1},{17,9},{25,17},{2,26},{10... | collective-permute-start | bytes 393224 | tf_op jit(solution)/shard_map/ppermute | solution.py:16
  52.4 0.6 copy-start.15
  52.4 0.7 copy-start.16
  53.1 1.0 copy-start.3
  59.9 2.0 %collective-permute-start.15 = (bf16[3,256,256]{2,1,0:T(8,128)(2,1)}, bf16[3,256,256]{2,1,0:T(8,128)(2,1)S(1)}, u32[]{:S(2)}, u32[]{:S(2)}) collective-permute-start(bf16[3,256,256]{2,1,0:T(8,128)(2,1)} %get-tuple-element.43), channel_id=1, source_target_pairs={{0,1},{1,0},{2,3},{3,2},{4,5},{5,4},{6,7},{7,6},{8,9},{9,8},{10,11... | collective-permute-start | bytes 1179656 | tf_op jit(solution)/shard_map/ppermute | solution.py:16
  63.0 33.0 %copy-start.4 = (bf16[2,3,256,256]{3,2,1,0:T(8,128)(2,1)}, bf16[2,3,256,256]{3,2,1,0:T(8,128)(2,1)S(1)}, u32[]{:S(2)}) copy-start(bf16[2,3,256,256]{3,2,1,0:T(8,128)(2,1)S(1)} %pad_maximum_fusion.w0) | copy-start | bytes 2359300
  63.0 20.9 %collective-permute-start.17 = (bf16[2,3,256,256]{3,2,1,0:T(8,128)(2,1)S(1)}, bf16[2,3,256,256]{3,2,1,0:T(8,128)(2,1)S(1)}, u32[]{:S(2)}, u32[]{:S(2)}) collective-permute-start(bf16[2,3,256,256]{3,2,1,0:T(8,128)(2,1)S(1)} %pad_maximum_fusion.w0), channel_id=1, source_target_pairs={{0,8},{8,16},{16,24},{24,0},{1,9},{9,17},{17,25},{25,1},{2,10},{10... | collective-permute-start | bytes 2359304 | tf_op jit(solution)/shard_map/ppermute | solution.py:16
  63.6 20.3 %collective-permute-start.16 = (bf16[2,3,256,256]{3,2,1,0:T(8,128)(2,1)S(1)}, bf16[2,3,256,256]{3,2,1,0:T(8,128)(2,1)S(1)}, u32[]{:S(2)}, u32[]{:S(2)}) collective-permute-start(bf16[2,3,256,256]{3,2,1,0:T(8,128)(2,1)S(1)} %pad_maximum_fusion.w0), channel_id=1, source_target_pairs={{0,24},{8,0},{16,8},{24,16},{1,25},{9,1},{17,9},{25,17},{2,26},{10... | collective-permute-start | bytes 2359304 | tf_op jit(solution)/shard_map/ppermute | solution.py:16
  83.8 12.1 %copy-start.5 = (bf16[2,3,256,256]{3,2,1,0:T(8,128)(2,1)}, bf16[2,3,256,256]{3,2,1,0:T(8,128)(2,1)S(1)}, u32[]{:S(2)}) copy-start(bf16[2,3,256,256]{3,2,1,0:T(8,128)(2,1)S(1)} %collective-permute-done.17.w3) | copy-start | bytes 2359300
  83.9 11.7 %collective-permute-start.18 = (bf16[3,256,256]{2,1,0:T(8,128)(2,1)S(1)}, bf16[3,256,256]{2,1,0:T(8,128)(2,1)S(1)}, u32[]{:S(2)}, u32[]{:S(2)}) collective-permute-start(bf16[3,256,256]{2,1,0:T(8,128)(2,1)S(1)} %slice_bitcast_fusion.1), channel_id=1, source_target_pairs={{0,8},{8,16},{16,24},{24,0},{1,9},{9,17},{17,25},{25,1},{2,10},{10... | collective-permute-start | bytes 1179656 | tf_op jit(solution)/shard_map/ppermute | solution.py:16
  84.0 12.0 %copy-start.6 = (bf16[2,3,256,256]{3,2,1,0:T(8,128)(2,1)}, bf16[2,3,256,256]{3,2,1,0:T(8,128)(2,1)S(1)}, u32[]{:S(2)}) copy-start(bf16[2,3,256,256]{3,2,1,0:T(8,128)(2,1)S(1)} %collective-permute-done.16.w1) | copy-start | bytes 2359300
  84.0 11.6 %collective-permute-start.19 = (bf16[3,256,256]{2,1,0:T(8,128)(2,1)S(1)}, bf16[3,256,256]{2,1,0:T(8,128)(2,1)S(1)}, u32[]{:S(2)}, u32[]{:S(2)}) collective-permute-start(bf16[3,256,256]{2,1,0:T(8,128)(2,1)S(1)} %slice_bitcast_fusion), channel_id=1, source_target_pairs={{0,24},{8,0},{16,8},{24,16},{1,25},{9,1},{17,9},{25,17},{2,26},{10... | collective-permute-start | bytes 1179656 | tf_op jit(solution)/shard_map/ppermute | solution.py:16
  95.6 0.7 copy-start.11
  95.6 0.9 copy-start.12
  102.0 42.3 %copy-start.1 = (bf16[512,256]{1,0:T(8,128)(2,1)S(1)}, bf16[512,256]{1,0:T(8,128)(2,1)}, u32[]{:S(2)}) copy-start(bf16[512,256]{1,0:T(8,128)(2,1)} %psi.1) | copy-start | bytes 786436
  118.6 25.7 %all-to-all-start.2 = ((f32[8,64,256]{2,1,0:T(8,128)}), f32[8,64,256]{2,1,0:T(8,128)S(1)}, u32[]{:S(2)}, u32[]{:S(2)}) async-start(f32[8,64,256]{2,1,0:T(8,128)} %get-tuple-element.44), calls=%async_computation.2 | async-start | bytes 1048576 | tf_op jit(solution)/shard_map/all_to_all | solution.py:217
  124.0 5.7 %collective-permute-start.22 = (f32[8,128]{1,0:T(8,128)S(1)}, f32[8,128]{1,0:T(8,128)S(1)}, u32[]{:S(2)}, u32[]{:S(2)}) collective-permute-start(f32[8,128]{1,0:T(8,128)S(1)} %get-tuple-element.45), channel_id=1, source_target_pairs={{0,24},{8,0},{16,8},{24,16},{1,25},{9,1},{17,9},{25,17},{2,26},{10... | collective-permute-start | bytes 12296 | tf_op jit(solution)/shard_map/ppermute | solution.py:16
  128.3 5.1 %collective-permute-start.21 = (f32[8,128]{1,0:T(8,128)S(1)}, f32[8,128]{1,0:T(8,128)S(1)}, u32[]{:S(2)}, u32[]{:S(2)}) collective-permute-start(f32[8,128]{1,0:T(8,128)S(1)} %get-tuple-element.45), channel_id=1, source_target_pairs={{0,16},{8,24},{16,0},{24,8},{1,17},{9,25},{17,1},{25,9},{2,18},{10... | collective-permute-start | bytes 12296 | tf_op jit(solution)/shard_map/ppermute | solution.py:16
  128.8 4.8 %collective-permute-start.20 = (f32[8,128]{1,0:T(8,128)S(1)}, f32[8,128]{1,0:T(8,128)S(1)}, u32[]{:S(2)}, u32[]{:S(2)}) collective-permute-start(f32[8,128]{1,0:T(8,128)S(1)} %get-tuple-element.45), channel_id=1, source_target_pairs={{0,8},{8,16},{16,24},{24,0},{1,9},{9,17},{17,25},{25,1},{2,10},{10... | collective-permute-start | bytes 12296 | tf_op jit(solution)/shard_map/ppermute | solution.py:16
  133.6 7.1 %collective-permute-start.25 = (f32[8,128]{1,0:T(8,128)S(1)}, f32[8,128]{1,0:T(8,128)S(1)}, u32[]{:S(2)}, u32[]{:S(2)}) collective-permute-start(f32[8,128]{1,0:T(8,128)S(1)} %add_add_fusion.1), channel_id=1, source_target_pairs={{0,6},{2,0},{4,2},{6,4},{1,7},{3,1},{5,3},{7,5},{8,14},{10,8},{12,... | collective-permute-start | bytes 12296 | tf_op jit(solution)/shard_map/ppermute | solution.py:16
  136.0 7.5 %collective-permute-start.24 = (f32[8,128]{1,0:T(8,128)S(1)}, f32[8,128]{1,0:T(8,128)S(1)}, u32[]{:S(2)}, u32[]{:S(2)}) collective-permute-start(f32[8,128]{1,0:T(8,128)S(1)} %add_add_fusion.1), channel_id=1, source_target_pairs={{0,4},{2,6},{4,0},{6,2},{1,5},{3,7},{5,1},{7,3},{8,12},{10,14},{12... | collective-permute-start | bytes 12296 | tf_op jit(solution)/shard_map/ppermute | solution.py:16
  138.6 5.7 %collective-permute-start.23 = (f32[8,128]{1,0:T(8,128)S(1)}, f32[8,128]{1,0:T(8,128)S(1)}, u32[]{:S(2)}, u32[]{:S(2)}) collective-permute-start(f32[8,128]{1,0:T(8,128)S(1)} %add_add_fusion.1), channel_id=1, source_target_pairs={{0,2},{2,4},{4,6},{6,0},{1,3},{3,5},{5,7},{7,1},{8,10},{10,12},{12... | collective-permute-start | bytes 12296 | tf_op jit(solution)/shard_map/ppermute | solution.py:16

commit v5 on v4

--- a/solution.py
+++ b/solution.py
@@ -215,8 +215,9 @@
     parts = lax.all_to_all(payload, (*TERMS, "core"), 0, 0, tiled=True)
     chunk, sums = call(third_kernel, [((8, 64, 256), F32), ((8, 128), F32)], [VMEM], parts)
     full = lax.all_to_all(chunk, TERMS, 0, 0, tiled=True)
-    for axis in ("row", "zhi"):
-        sums = sums + shift(sums, axis, 4, 1) + shift(sums, axis, 4, 2) + shift(sums, axis, 4, 3)
+    sums = sums + shift(sums, "row", 4, 1) + shift(sums, "row", 4, 2) + shift(sums, "row", 4, 3)
+    for k in (1, 2):
+        sums = sums + lax.ppermute(sums, "zhi", [(i, i ^ k) for i in range(4)])
     sigma, residual, energy = call(
         last_kernel, [((512, 256), BF16), ((512, 256), BF16), ((1, 1), F32)], [VMEM] * 3, full, sums, psi
     )

time: 146 us -> 147 us (level)
  waiting for transfers between devices: 47.6 us -> 50.1 us
    ppermute x26 -> x23, starting transfers between devices: 46.6 us -> 39.9 us  [shift(): return lax.ppermute(x, axis, [(i, (i + k) % n) for i in range(n)])]
    ppermute x0 -> x2, waiting for transfers between devices: none -> 6.49 us  [per_device(): sums = sums + lax.ppermute(sums, 'zhi', [(i, i ^ k) for i in range(4)])]
    ppermute x0 -> x2, starting transfers between devices: none -> 5.53 us  [per_device(): sums = sums + lax.ppermute(sums, 'zhi', [(i, i ^ k) for i in range(4)])]
    ppermute x26 -> x23, waiting for transfers between devices: 47.2 us -> 43.3 us  [shift(): return lax.ppermute(x, axis, [(i, (i + k) % n) for i in range(n)])]
  transfers between devices with their start and end apart: 28 -> 27, of which waited for: 15 -> 14; matrix products, arithmetic and copies ran while one was open for 2% -> 2% of each run, Pallas kernels for 7% -> 7%
where the time goes in v5:
time: 147 us; the launch traced here: 146 us
  starting transfers between devices  55.8 us (38%)
  waiting for transfers between devices  50.1 us (34%)
  Pallas kernels  17 us (12%)
  blocking collectives  14.9 us (10%)
  local copies, waits for them, and re-layouts  5.37 us (4%)
  between operations  1.56 us (1%)
    ppermute x23, waiting for transfers between devices, shift(): return lax.ppermute(x, axis, [(i, (i + k) % n) for i in range(n)])  43.3 us
    ppermute x23, starting transfers between devices, shift(): return lax.ppermute(x, axis, [(i, (i + k) % n) for i in range(n)])  39.9 us
    all_to_all x1, blocking collectives, per_device(): parts = lax.all_to_all(payload, (*TERMS, 'core'), 0, 0, tiled=True)  14.9 us
    pallas_call x6, Pallas kernels, call(): pl.pallas_call(kernel, out_shape=[jax.ShapeDtypeStruct(shape, dtype) for...  14.2 us
    ppermute x2, waiting for transfers between devices, per_device(): sums = sums + lax.ppermute(sums, 'zhi', [(i, i ^ k) for i in range(4)])  6.49 us
    ppermute x2, starting transfers between devices, per_device(): sums = sums + lax.ppermute(sums, 'zhi', [(i, i ^ k) for i in range(4)])  5.53 us
    all_to_all x1, starting transfers between devices, per_device(): full = lax.all_to_all(chunk, TERMS, 0, 0, tiled=True)  5.36 us
    all_to_all x1, starting transfers between devices, per_device(): left = lax.all_to_all(left, 'zhi', 0, 0, tiled=True)  5.06 us
  transfers between devices with their start and end apart: 27, of which 14 were waited for; matrix products, arithmetic and copies ran while one was open for 2% of the time, Pallas kernels for 7%

profile of v5, /device:TPU:2, one launch (start us, length us, event | category | flops | bytes accessed | tf_op | source)
XLA Modules:
  0.0 145.8 jit_solution(17222869815664276411)
XLA Ops:
  0.6 1.1 slice.24
  1.7 1.7 %collective-permute-start.4 = (bf16[2,512,256]{2,1,0:T(8,128)(2,1)S(1)}, bf16[2,512,256]{2,1,0:T(8,128)(2,1)S(1)}, u32[]{:S(2)}, u32[]{:S(2)}) collective-permute-start(bf16[2,512,256]{2,1,0:T(8,128)(2,1)S(1)} %slice.24), channel_id=1, source_target_pairs={{0,8},{8,16},{16,24},{24,0},{1,9},{9,17},{17,25},{25,1},{2,10},{10... | collective-permute-start | bytes 1572872 | tf_op jit(solution)/shard_map/ppermute | solution.py:16
  3.4 1.7 %collective-permute-start.3 = (bf16[2,512,256]{2,1,0:T(8,128)(2,1)S(1)}, bf16[2,512,256]{2,1,0:T(8,128)(2,1)S(1)}, u32[]{:S(2)}, u32[]{:S(2)}) collective-permute-start(bf16[2,512,256]{2,1,0:T(8,128)(2,1)S(1)} %slice.24), channel_id=1, source_target_pairs={{0,24},{8,0},{16,8},{24,16},{1,25},{9,1},{17,9},{25,17},{2,26},{10... | collective-permute-start | bytes 1572872 | tf_op jit(solution)/shard_map/ppermute | solution.py:16
  5.0 0.8 constant_dynamic-slice_fusion.q0
  5.9 3.3 %collective-permute-start.2 = (bf16[128,256]{1,0:T(8,128)(2,1)S(1)}, bf16[128,256]{1,0:T(8,128)(2,1)S(1)}, u32[]{:S(2)}, u32[]{:S(2)}) collective-permute-start(bf16[128,256]{1,0:T(8,128)(2,1)S(1)} %constant_dynamic-slice_fusion.q0), channel_id=1, source_target_pairs={{0,2},{2,4},{4,6},{6,0},{1,3},{3,5},{5,7},{7,1},{8,10},{10,12},{12... | collective-permute-start | bytes 196616 | tf_op jit(solution)/shard_map/ppermute | solution.py:16
  9.1 5.4 %collective-permute-start.1 = (bf16[128,256]{1,0:T(8,128)(2,1)S(1)}, bf16[128,256]{1,0:T(8,128)(2,1)S(1)}, u32[]{:S(2)}, u32[]{:S(2)}) collective-permute-start(bf16[128,256]{1,0:T(8,128)(2,1)S(1)} %constant_dynamic-slice_fusion.q0), channel_id=1, source_target_pairs={{0,4},{2,6},{4,0},{6,2},{1,5},{3,7},{5,1},{7,3},{8,12},{10,14},{12... | collective-permute-start | bytes 196616 | tf_op jit(solution)/shard_map/ppermute | solution.py:16
  14.5 2.7 %collective-permute-start = (bf16[128,256]{1,0:T(8,128)(2,1)S(1)}, bf16[128,256]{1,0:T(8,128)(2,1)S(1)}, u32[]{:S(2)}, u32[]{:S(2)}) collective-permute-start(bf16[128,256]{1,0:T(8,128)(2,1)S(1)} %constant_dynamic-slice_fusion.q0), channel_id=1, source_target_pairs={{0,6},{2,0},{4,2},{6,4},{1,7},{3,1},{5,3},{7,5},{8,14},{10,8},{12,... | collective-permute-start | bytes 196616 | tf_op jit(solution)/shard_map/ppermute | solution.py:16
  17.2 1.0 slice.25
  18.2 2.8 %shard_map.67 = bf16[4,3,512,256]{3,2,1,0:T(8,128)(2,1)} custom-call(bf16[3,512,256]{2,1,0:T(8,128)(2,1)} %x.1), custom_call_target="tpu_custom_call" | custom-call | bytes 1024 | tf_op jit(solution)/shard_map/pallas_call | solution.py:175
  21.2 5.1 %all-to-all-start = ((bf16[4,3,512,256]{3,2,1,0:T(8,128)(2,1)}), bf16[4,3,512,256]{3,2,1,0:T(8,128)(2,1)}, u32[]{:S(2)}, u32[]{:S(2)}) async-start(bf16[4,3,512,256]{3,2,1,0:T(8,128)(2,1)} %shard_map.67), calls=%async_computation | async-start | bytes 6291456 | tf_op jit(solution)/shard_map/all_to_all | solution.py:185
  26.3 2.1 %collective-permute-start.9 = (bf16[2,256,256]{2,1,0:T(8,128)(2,1)S(1)}, bf16[2,256,256]{2,1,0:T(8,128)(2,1)S(1)}, u32[]{:S(2)}, u32[]{:S(2)}) collective-permute-start(bf16[2,256,256]{2,1,0:T(8,128)(2,1)S(1)} %slice.27), channel_id=1, source_target_pairs={{0,24},{8,0},{16,8},{24,16},{1,25},{9,1},{17,9},{25,17},{2,26},{10... | collective-permute-start | bytes 786440 | tf_op jit(solution)/shard_map/ppermute | solution.py:16
  29.2 0.6 shard_map.68.x0
  29.8 1.6 %collective-permute-start.7 = (bf16[4,128,256]{2,1,0:T(8,128)(2,1)S(1)}, bf16[4,128,256]{2,1,0:T(8,128)(2,1)S(1)}, u32[]{:S(2)}, u32[]{:S(2)}) collective-permute-start(bf16[4,128,256]{2,1,0:T(8,128)(2,1)S(1)} %shard_map.68.x0), channel_id=1, source_target_pairs={{0,64},{64,128},{128,192},{192,0},{1,65},{65,129},{129,193},{193,1... | collective-permute-start | bytes 786440 | tf_op jit(solution)/shard_map/ppermute | solution.py:16
  31.3 1.1 collective-permute-start.6
  32.5 2.2 %collective-permute-start.5 = (bf16[4,128,256]{2,1,0:T(8,128)(2,1)S(1)}, bf16[4,128,256]{2,1,0:T(8,128)(2,1)S(1)}, u32[]{:S(2)}, u32[]{:S(2)}) collective-permute-start(bf16[4,128,256]{2,1,0:T(8,128)(2,1)S(1)} %shard_map.68.x0), channel_id=1, source_target_pairs={{0,192},{64,0},{128,64},{192,128},{1,193},{65,1},{129,65},{193,129... | collective-permute-start | bytes 786440 | tf_op jit(solution)/shard_map/ppermute | solution.py:16
  34.6 0.5 collective-permute-start.11
  35.2 0.9 collective-permute-done.8.r2a
  36.1 1.8 %collective-permute-start.10 = (bf16[1,512,256]{2,1,0:T(8,128)(2,1)S(1)}, bf16[1,512,256]{2,1,0:T(8,128)(2,1)S(1)}, u32[]{:S(2)}, u32[]{:S(2)}) collective-permute-start(bf16[1,512,256]{2,1,0:T(8,128)(2,1)S(1)} %slice.25), channel_id=1, source_target_pairs={{0,24},{8,0},{16,8},{24,16},{1,25},{9,1},{17,9},{25,17},{2,26},{10... | collective-permute-start | bytes 786440 | tf_op jit(solution)/shard_map/ppermute | solution.py:16
  37.9 1.2 collective-permute-done.7.x3
  39.1 3.0 %collective-permute-done.6.x2 = bf16[4,128,256]{2,1,0:T(8,128)(2,1)S(1)} collective-permute-done((bf16[4,128,256]{2,1,0:T(8,128)(2,1)S(1)}, bf16[4,128,256]{2,1,0:T(8,128)(2,1)S(1)}, u32[]{:S(2)}, u32[]{:S(2)}) %collective-permute-start.6) | collective-permute-done | bytes 262176 | tf_op jit(solution)/shard_map/ppermute | solution.py:16
  42.1 2.4 %collective-permute-done.5.x1 = bf16[4,128,256]{2,1,0:T(8,128)(2,1)S(1)} collective-permute-done((bf16[4,128,256]{2,1,0:T(8,128)(2,1)S(1)}, bf16[4,128,256]{2,1,0:T(8,128)(2,1)S(1)}, u32[]{:S(2)}, u32[]{:S(2)}) %collective-permute-start.5) | collective-permute-done | bytes 262176 | tf_op jit(solution)/shard_map/ppermute | solution.py:16
  44.5 0.6 shard_map.69.own
  45.6 2.9 %collective-permute-start.14 = (bf16[1,256,256]{2,1,0:T(8,128)(2,1)S(1)}, bf16[1,256,256]{2,1,0:T(8,128)(2,1)S(1)}, u32[]{:S(2)}, u32[]{:S(2)}) collective-permute-start(bf16[1,256,256]{2,1,0:T(8,128)(2,1)S(1)} %slice.29), channel_id=1, source_target_pairs={{0,24},{8,0},{16,8},{24,16},{1,25},{9,1},{17,9},{25,17},{2,26},{10... | collective-permute-start | bytes 393224 | tf_op jit(solution)/shard_map/ppermute | solution.py:16
  48.6 3.9 %collective-permute-done.13.v2a = bf16[1,256,256]{2,1,0:T(8,128)(2,1)S(1)} collective-permute-done((bf16[1,256,256]{2,1,0:T(8,128)(2,1)S(1)}, bf16[1,256,256]{2,1,0:T(8,128)(2,1)S(1)}, u32[]{:S(2)}, u32[]{:S(2)}) %collective-permute-start.13) | collective-permute-done | bytes 131104 | tf_op jit(solution)/shard_map/ppermute | solution.py:16
  52.5 0.6 copy-done.15
  53.1 1.0 copy-done.3
  54.2 5.7 %shard_map.70 = (bf16[3,256,256]{2,1,0:T(8,128)(2,1)}, bf16[3,256,256]{2,1,0:T(8,128)(2,1)}) custom-call(s32[5]{0:T(128)} %copy-done.2, bf16[4,4,128,256]{3,2,1,0:T(8,128)(2,1)} %copy-done, bf16[4,4,128,256]{3,2,1,0:T(8,128)(2,1)} %copy-done.3, bf16[3,512,256]{2,1,0:T(8,128)(2,1)} %r0.1, bf16[2,512,256]{2,1,0:T(8,128)(2,1)} %copy-done.8, ...), custom_call_target="tpu_custom_call" | custom-call | bytes 1024 | tf_op jit(solution)/shard_map/pallas_call | solution.py:154
  60.0 1.9 %collective-permute-done.15 = bf16[3,256,256]{2,1,0:T(8,128)(2,1)S(1)} collective-permute-done((bf16[3,256,256]{2,1,0:T(8,128)(2,1)}, bf16[3,256,256]{2,1,0:T(8,128)(2,1)S(1)}, u32[]{:S(2)}, u32[]{:S(2)}) %collective-permute-start.15) | collective-permute-done | bytes 393248 | tf_op jit(solution)/shard_map/ppermute | solution.py:16
  61.9 1.1 pad_maximum_fusion.w0
  63.0 0.7 collective-permute-start.17
  63.6 2.7 %collective-permute-start.16 = (bf16[2,3,256,256]{3,2,1,0:T(8,128)(2,1)S(1)}, bf16[2,3,256,256]{3,2,1,0:T(8,128)(2,1)S(1)}, u32[]{:S(2)}, u32[]{:S(2)}) collective-permute-start(bf16[2,3,256,256]{3,2,1,0:T(8,128)(2,1)S(1)} %pad_maximum_fusion.w0), channel_id=1, source_target_pairs={{0,24},{8,0},{16,8},{24,16},{1,25},{9,1},{17,9},{25,17},{2,26},{10... | collective-permute-start | bytes 2359304 | tf_op jit(solution)/shard_map/ppermute | solution.py:16
  66.3 17.6 %collective-permute-done.17.w3 = bf16[2,3,256,256]{3,2,1,0:T(8,128)(2,1)S(1)} collective-permute-done((bf16[2,3,256,256]{3,2,1,0:T(8,128)(2,1)S(1)}, bf16[2,3,256,256]{3,2,1,0:T(8,128)(2,1)S(1)}, u32[]{:S(2)}, u32[]{:S(2)}) %collective-permute-start.17) | collective-permute-done | bytes 786464 | tf_op jit(solution)/shard_map/ppermute | solution.py:16
  84.0 3.3 %collective-permute-start.19 = (bf16[3,256,256]{2,1,0:T(8,128)(2,1)S(1)}, bf16[3,256,256]{2,1,0:T(8,128)(2,1)S(1)}, u32[]{:S(2)}, u32[]{:S(2)}) collective-permute-start(bf16[3,256,256]{2,1,0:T(8,128)(2,1)S(1)} %slice_bitcast_fusion), channel_id=1, source_target_pairs={{0,24},{8,0},{16,8},{24,16},{1,25},{9,1},{17,9},{25,17},{2,26},{10... | collective-permute-start | bytes 1179656 | tf_op jit(solution)/shard_map/ppermute | solution.py:16
  87.3 8.3 %collective-permute-done.18.w2a = bf16[3,256,256]{2,1,0:T(8,128)(2,1)S(1)} collective-permute-done((bf16[3,256,256]{2,1,0:T(8,128)(2,1)S(1)}, bf16[3,256,256]{2,1,0:T(8,128)(2,1)S(1)}, u32[]{:S(2)}, u32[]{:S(2)}) %collective-permute-start.18) | collective-permute-done | bytes 393248 | tf_op jit(solution)/shard_map/ppermute | solution.py:16
  95.9 0.4 copy-done.11
  96.5 5.5 %shard_map.71 = bf16[16,80,256]{2,1,0:T(8,128)(2,1)} custom-call(s32[5]{0:T(128)} %copy-done.2, bf16[4,3,512,256]{3,2,1,0:T(8,128)(2,1)} %all-to-all-done.left, bf16[2,3,256,256]{3,2,1,0:T(8,128)(2,1)} %copy-done.4, bf16[2,3,256,256]{3,2,1,0:T(8,128)(2,1)} %copy-done.6, bf16[3,256,256]{2,1,0:T(8,128)(2,1)} %copy-done.11, bf16[3,256,256]{2,1,0:T(8,128)(2,1)} %copy-done.12, ...), custom_call_target="tpu_custom_call" | custom-call | bytes 1024 | tf_op jit(solution)/shard_map/pallas_call | solution.py:154
  102.1 14.9 %all_to_all.15.parts = bf16[16,80,256]{2,1,0:T(8,128)(2,1)S(1)} all-to-all(bf16[16,80,256]{2,1,0:T(8,128)(2,1)} %shard_map.71), channel_id=1, replica_groups=mesh['x'=4,'zlo'=2,'row'=4,'zhi'=4,'core'=2] {'x','zlo','core'}, dimensions={0} | all-to-all | bytes 1310720 | tf_op jit(solution)/shard_map/all_to_all | solution.py:215
  117.0 0.9 shard_map.72
  117.9 5.4 %all-to-all-start.2 = ((f32[8,64,256]{2,1,0:T(8,128)}), f32[8,64,256]{2,1,0:T(8,128)S(1)}, u32[]{:S(2)}, u32[]{:S(2)}) async-start(f32[8,64,256]{2,1,0:T(8,128)} %get-tuple-element.44), calls=%async_computation.2 | async-start | bytes 1048576 | tf_op jit(solution)/shard_map/all_to_all | solution.py:217
  123.2 4.4 %collective-permute-start.22 = (f32[8,128]{1,0:T(8,128)S(1)}, f32[8,128]{1,0:T(8,128)S(1)}, u32[]{:S(2)}, u32[]{:S(2)}) collective-permute-start(f32[8,128]{1,0:T(8,128)S(1)} %get-tuple-element.45), channel_id=1, source_target_pairs={{0,24},{8,0},{16,8},{24,16},{1,25},{9,1},{17,9},{25,17},{2,26},{10... | collective-permute-start | bytes 12296 | tf_op jit(solution)/shard_map/ppermute | solution.py:16
  127.6 0.5 collective-permute-start.21
  128.1 0.8 collective-permute-start.20
  129.0 3.8 %collective-permute-done.21 = f32[8,128]{1,0:T(8,128)S(1)} collective-permute-done((f32[8,128]{1,0:T(8,128)S(1)}, f32[8,128]{1,0:T(8,128)S(1)}, u32[]{:S(2)}, u32[]{:S(2)}) %collective-permute-start.21) | collective-permute-done | bytes 4128 | tf_op jit(solution)/shard_map/ppermute | solution.py:16
  132.9 1.4 collective-permute-start.23
  134.3 3.1 %collective-permute-done.23 = f32[8,128]{1,0:T(8,128)S(1)} collective-permute-done((f32[8,128]{1,0:T(8,128)S(1)}, f32[8,128]{1,0:T(8,128)S(1)}, u32[]{:S(2)}, u32[]{:S(2)}) %collective-permute-start.23) | collective-permute-done | bytes 4128 | tf_op jit(solution)/shard_map/ppermute | solution.py:220
  137.4 4.2 %collective-permute-start.24 = (f32[8,128]{1,0:T(8,128)S(1)}, f32[8,128]{1,0:T(8,128)S(1)}, u32[]{:S(2)}, u32[]{:S(2)}) collective-permute-start(f32[8,128]{1,0:T(8,128)S(1)} %add.22), channel_id=1, source_target_pairs={{0,4},{2,6},{4,0},{6,2},{1,5},{3,7},{5,1},{7,3},{8,12},{10,14},{12... | collective-permute-start | bytes 12296 | tf_op jit(solution)/shard_map/ppermute | solution.py:220
  141.6 3.4 %collective-permute-done.24 = f32[8,128]{1,0:T(8,128)S(1)} collective-permute-done((f32[8,128]{1,0:T(8,128)S(1)}, f32[8,128]{1,0:T(8,128)S(1)}, u32[]{:S(2)}, u32[]{:S(2)}) %collective-permute-start.24) | collective-permute-done | bytes 4128 | tf_op jit(solution)/shard_map/ppermute | solution.py:220
  145.0 0.9 shard_map.73
  (62 shorter events, 1.9 us)
Async XLA Ops:
  1.7 19.4 %collective-permute-start.4 = (bf16[2,512,256]{2,1,0:T(8,128)(2,1)S(1)}, bf16[2,512,256]{2,1,0:T(8,128)(2,1)S(1)}, u32[]{:S(2)}, u32[]{:S(2)}) collective-permute-start(bf16[2,512,256]{2,1,0:T(8,128)(2,1)S(1)} %slice.24), channel_id=1, source_target_pairs={{0,8},{8,16},{16,24},{24,0},{1,9},{9,17},{17,25},{25,1},{2,10},{10... | collective-permute-start | bytes 1572872 | tf_op jit(solution)/shard_map/ppermute | solution.py:16
  3.4 17.8 %collective-permute-start.3 = (bf16[2,512,256]{2,1,0:T(8,128)(2,1)S(1)}, bf16[2,512,256]{2,1,0:T(8,128)(2,1)S(1)}, u32[]{:S(2)}, u32[]{:S(2)}) collective-permute-start(bf16[2,512,256]{2,1,0:T(8,128)(2,1)S(1)} %slice.24), channel_id=1, source_target_pairs={{0,24},{8,0},{16,8},{24,16},{1,25},{9,1},{17,9},{25,17},{2,26},{10... | collective-permute-start | bytes 1572872 | tf_op jit(solution)/shard_map/ppermute | solution.py:16
  5.9 15.1 %collective-permute-start.2 = (bf16[128,256]{1,0:T(8,128)(2,1)S(1)}, bf16[128,256]{1,0:T(8,128)(2,1)S(1)}, u32[]{:S(2)}, u32[]{:S(2)}) collective-permute-start(bf16[128,256]{1,0:T(8,128)(2,1)S(1)} %constant_dynamic-slice_fusion.q0), channel_id=1, source_target_pairs={{0,2},{2,4},{4,6},{6,0},{1,3},{3,5},{5,7},{7,1},{8,10},{10,12},{12... | collective-permute-start | bytes 196616 | tf_op jit(solution)/shard_map/ppermute | solution.py:16
  9.1 11.9 %collective-permute-start.1 = (bf16[128,256]{1,0:T(8,128)(2,1)S(1)}, bf16[128,256]{1,0:T(8,128)(2,1)S(1)}, u32[]{:S(2)}, u32[]{:S(2)}) collective-permute-start(bf16[128,256]{1,0:T(8,128)(2,1)S(1)} %constant_dynamic-slice_fusion.q0), channel_id=1, source_target_pairs={{0,4},{2,6},{4,0},{6,2},{1,5},{3,7},{5,1},{7,3},{8,12},{10,14},{12... | collective-permute-start | bytes 196616 | tf_op jit(solution)/shard_map/ppermute | solution.py:16
  14.5 6.6 %collective-permute-start = (bf16[128,256]{1,0:T(8,128)(2,1)S(1)}, bf16[128,256]{1,0:T(8,128)(2,1)S(1)}, u32[]{:S(2)}, u32[]{:S(2)}) collective-permute-start(bf16[128,256]{1,0:T(8,128)(2,1)S(1)} %constant_dynamic-slice_fusion.q0), channel_id=1, source_target_pairs={{0,6},{2,0},{4,2},{6,4},{1,7},{3,1},{5,3},{7,5},{8,14},{10,8},{12,... | collective-permute-start | bytes 196616 | tf_op jit(solution)/shard_map/ppermute | solution.py:16
  21.2 7.2 %copy-start.7 = (bf16[2,512,256]{2,1,0:T(8,128)(2,1)}, bf16[2,512,256]{2,1,0:T(8,128)(2,1)S(1)}, u32[]{:S(2)}) copy-start(bf16[2,512,256]{2,1,0:T(8,128)(2,1)S(1)} %collective-permute-done.4.r3) | copy-start | bytes 1572868
  21.2 5.1 %copy-start.8 = (bf16[2,512,256]{2,1,0:T(8,128)(2,1)}, bf16[2,512,256]{2,1,0:T(8,128)(2,1)S(1)}, u32[]{:S(2)}) copy-start(bf16[2,512,256]{2,1,0:T(8,128)(2,1)S(1)} %collective-permute-done.3.r1) | copy-start | bytes 1572868
  21.2 74.8 %all-to-all-start = ((bf16[4,3,512,256]{3,2,1,0:T(8,128)(2,1)}), bf16[4,3,512,256]{3,2,1,0:T(8,128)(2,1)}, u32[]{:S(2)}, u32[]{:S(2)}) async-start(bf16[4,3,512,256]{3,2,1,0:T(8,128)(2,1)} %shard_map.67), calls=%async_computation | async-start | bytes 6291456 | tf_op jit(solution)/shard_map/all_to_all | solution.py:185
  26.3 8.4 %collective-permute-start.9 = (bf16[2,256,256]{2,1,0:T(8,128)(2,1)S(1)}, bf16[2,256,256]{2,1,0:T(8,128)(2,1)S(1)}, u32[]{:S(2)}, u32[]{:S(2)}) collective-permute-start(bf16[2,256,256]{2,1,0:T(8,128)(2,1)S(1)} %slice.27), channel_id=1, source_target_pairs={{0,24},{8,0},{16,8},{24,16},{1,25},{9,1},{17,9},{25,17},{2,26},{10... | collective-permute-start | bytes 786440 | tf_op jit(solution)/shard_map/ppermute | solution.py:16
  28.4 7.7 %collective-permute-start.8 = (bf16[2,256,256]{2,1,0:T(8,128)(2,1)S(1)}, bf16[2,256,256]{2,1,0:T(8,128)(2,1)S(1)}, u32[]{:S(2)}, u32[]{:S(2)}) collective-permute-start(bf16[2,256,256]{2,1,0:T(8,128)(2,1)S(1)} %slice.26), channel_id=1, source_target_pairs={{0,8},{8,16},{16,24},{24,0},{1,9},{9,17},{17,25},{25,1},{2,10},{10... | collective-permute-start | bytes 786440 | tf_op jit(solution)/shard_map/ppermute | solution.py:16
  29.2 23.2 %copy-start.2 = (s32[5]{0:T(128)}, s32[5]{0:T(128)S(1)}, u32[]{:S(2)}) copy-start(s32[5]{0:T(128)S(1)} %stack.28.place) | copy-start | bytes 64
  29.8 9.3 %collective-permute-start.7 = (bf16[4,128,256]{2,1,0:T(8,128)(2,1)S(1)}, bf16[4,128,256]{2,1,0:T(8,128)(2,1)S(1)}, u32[]{:S(2)}, u32[]{:S(2)}) collective-permute-start(bf16[4,128,256]{2,1,0:T(8,128)(2,1)S(1)} %shard_map.68.x0), channel_id=1, source_target_pairs={{0,64},{64,128},{128,192},{192,0},{1,65},{65,129},{129,193},{193,1... | collective-permute-start | bytes 786440 | tf_op jit(solution)/shard_map/ppermute | solution.py:16
  31.3 10.8 %collective-permute-start.6 = (bf16[4,128,256]{2,1,0:T(8,128)(2,1)S(1)}, bf16[4,128,256]{2,1,0:T(8,128)(2,1)S(1)}, u32[]{:S(2)}, u32[]{:S(2)}) collective-permute-start(bf16[4,128,256]{2,1,0:T(8,128)(2,1)S(1)} %shard_map.68.x0), channel_id=1, source_target_pairs={{0,128},{64,192},{128,0},{192,64},{1,129},{65,193},{129,1},{193,65... | collective-permute-start | bytes 786440 | tf_op jit(solution)/shard_map/ppermute | solution.py:16
  32.5 12.0 %collective-permute-start.5 = (bf16[4,128,256]{2,1,0:T(8,128)(2,1)S(1)}, bf16[4,128,256]{2,1,0:T(8,128)(2,1)S(1)}, u32[]{:S(2)}, u32[]{:S(2)}) collective-permute-start(bf16[4,128,256]{2,1,0:T(8,128)(2,1)S(1)} %shard_map.68.x0), channel_id=1, source_target_pairs={{0,192},{64,0},{128,64},{192,128},{1,193},{65,1},{129,65},{193,129... | collective-permute-start | bytes 786440 | tf_op jit(solution)/shard_map/ppermute | solution.py:16
  34.6 17.8 %copy-start.13 = (bf16[2,256,256]{2,1,0:T(8,128)(2,1)}, bf16[2,256,256]{2,1,0:T(8,128)(2,1)S(1)}, u32[]{:S(2)}) copy-start(bf16[2,256,256]{2,1,0:T(8,128)(2,1)S(1)} %collective-permute-done.9.r2b) | copy-start | bytes 786436
  34.6 9.8 %collective-permute-start.11 = (bf16[1,512,256]{2,1,0:T(8,128)(2,1)S(1)}, bf16[1,512,256]{2,1,0:T(8,128)(2,1)S(1)}, u32[]{:S(2)}, u32[]{:S(2)}) collective-permute-start(bf16[1,512,256]{2,1,0:T(8,128)(2,1)S(1)} %slice.25), channel_id=1, source_target_pairs={{0,8},{8,16},{16,24},{24,0},{1,9},{9,17},{17,25},{25,1},{2,10},{10... | collective-permute-start | bytes 786440 | tf_op jit(solution)/shard_map/ppermute | solution.py:16
  36.1 16.4 %copy-start.14 = (bf16[2,256,256]{2,1,0:T(8,128)(2,1)}, bf16[2,256,256]{2,1,0:T(8,128)(2,1)S(1)}, u32[]{:S(2)}) copy-start(bf16[2,256,256]{2,1,0:T(8,128)(2,1)S(1)} %collective-permute-done.8.r2a) | copy-start | bytes 786436
  36.1 8.4 %collective-permute-start.10 = (bf16[1,512,256]{2,1,0:T(8,128)(2,1)S(1)}, bf16[1,512,256]{2,1,0:T(8,128)(2,1)S(1)}, u32[]{:S(2)}, u32[]{:S(2)}) collective-permute-start(bf16[1,512,256]{2,1,0:T(8,128)(2,1)S(1)} %slice.25), channel_id=1, source_target_pairs={{0,24},{8,0},{16,8},{24,16},{1,25},{9,1},{17,9},{25,17},{2,26},{10... | collective-permute-start | bytes 786440 | tf_op jit(solution)/shard_map/ppermute | solution.py:16
  44.5 8.0 %copy-start.9 = (bf16[1,512,256]{2,1,0:T(8,128)(2,1)}, bf16[1,512,256]{2,1,0:T(8,128)(2,1)S(1)}, u32[]{:S(2)}) copy-start(bf16[1,512,256]{2,1,0:T(8,128)(2,1)S(1)} %collective-permute-done.11.v3) | copy-start | bytes 786436
  44.5 8.0 %copy-start.10 = (bf16[1,512,256]{2,1,0:T(8,128)(2,1)}, bf16[1,512,256]{2,1,0:T(8,128)(2,1)S(1)}, u32[]{:S(2)}) copy-start(bf16[1,512,256]{2,1,0:T(8,128)(2,1)S(1)} %collective-permute-done.10.v1) | copy-start | bytes 786436
  45.1 7.4 %copy-start = (bf16[4,4,128,256]{3,2,1,0:T(8,128)(2,1)}, bf16[4,4,128,256]{3,2,1,0:T(8,128)(2,1)S(1)}, u32[]{:S(2)}) copy-start(bf16[4,4,128,256]{3,2,1,0:T(8,128)(2,1)S(1)} %shard_map.69.own) | copy-start | bytes 3145732
  45.1 7.3 %collective-permute-start.12 = (bf16[4,4,128,256]{3,2,1,0:T(8,128)(2,1)S(1)}, bf16[4,4,128,256]{3,2,1,0:T(8,128)(2,1)S(1)}, u32[]{:S(2)}, u32[]{:S(2)}) collective-permute-start(bf16[4,4,128,256]{3,2,1,0:T(8,128)(2,1)S(1)} %shard_map.69.own), channel_id=1, source_target_pairs={{0,1},{1,0},{2,3},{3,2},{4,5},{5,4},{6,7},{7,6},{8,9},{9,8},{10,11... | collective-permute-start | bytes 3145736 | tf_op jit(solution)/shard_map/ppermute | solution.py:16
  45.3 7.2 %collective-permute-start.13 = (bf16[1,256,256]{2,1,0:T(8,128)(2,1)S(1)}, bf16[1,256,256]{2,1,0:T(8,128)(2,1)S(1)}, u32[]{:S(2)}, u32[]{:S(2)}) collective-permute-start(bf16[1,256,256]{2,1,0:T(8,128)(2,1)S(1)} %slice.28), channel_id=1, source_target_pairs={{0,8},{8,16},{16,24},{24,0},{1,9},{9,17},{17,25},{25,1},{2,10},{10... | collective-permute-start | bytes 393224 | tf_op jit(solution)/shard_map/ppermute | solution.py:16
  45.6 6.8 %collective-permute-start.14 = (bf16[1,256,256]{2,1,0:T(8,128)(2,1)S(1)}, bf16[1,256,256]{2,1,0:T(8,128)(2,1)S(1)}, u32[]{:S(2)}, u32[]{:S(2)}) collective-permute-start(bf16[1,256,256]{2,1,0:T(8,128)(2,1)S(1)} %slice.29), channel_id=1, source_target_pairs={{0,24},{8,0},{16,8},{24,16},{1,25},{9,1},{17,9},{25,17},{2,26},{10... | collective-permute-start | bytes 393224 | tf_op jit(solution)/shard_map/ppermute | solution.py:16
  52.4 0.6 copy-start.15
  52.4 0.7 copy-start.16
  53.1 1.0 copy-start.3
  59.9 2.0 %collective-permute-start.15 = (bf16[3,256,256]{2,1,0:T(8,128)(2,1)}, bf16[3,256,256]{2,1,0:T(8,128)(2,1)S(1)}, u32[]{:S(2)}, u32[]{:S(2)}) collective-permute-start(bf16[3,256,256]{2,1,0:T(8,128)(2,1)} %get-tuple-element.43), channel_id=1, source_target_pairs={{0,1},{1,0},{2,3},{3,2},{4,5},{5,4},{6,7},{7,6},{8,9},{9,8},{10,11... | collective-permute-start | bytes 1179656 | tf_op jit(solution)/shard_map/ppermute | solution.py:16
  63.0 33.0 %copy-start.4 = (bf16[2,3,256,256]{3,2,1,0:T(8,128)(2,1)}, bf16[2,3,256,256]{3,2,1,0:T(8,128)(2,1)S(1)}, u32[]{:S(2)}) copy-start(bf16[2,3,256,256]{3,2,1,0:T(8,128)(2,1)S(1)} %pad_maximum_fusion.w0) | copy-start | bytes 2359300
  63.0 20.9 %collective-permute-start.17 = (bf16[2,3,256,256]{3,2,1,0:T(8,128)(2,1)S(1)}, bf16[2,3,256,256]{3,2,1,0:T(8,128)(2,1)S(1)}, u32[]{:S(2)}, u32[]{:S(2)}) collective-permute-start(bf16[2,3,256,256]{3,2,1,0:T(8,128)(2,1)S(1)} %pad_maximum_fusion.w0), channel_id=1, source_target_pairs={{0,8},{8,16},{16,24},{24,0},{1,9},{9,17},{17,25},{25,1},{2,10},{10... | collective-permute-start | bytes 2359304 | tf_op jit(solution)/shard_map/ppermute | solution.py:16
  63.6 20.3 %collective-permute-start.16 = (bf16[2,3,256,256]{3,2,1,0:T(8,128)(2,1)S(1)}, bf16[2,3,256,256]{3,2,1,0:T(8,128)(2,1)S(1)}, u32[]{:S(2)}, u32[]{:S(2)}) collective-permute-start(bf16[2,3,256,256]{3,2,1,0:T(8,128)(2,1)S(1)} %pad_maximum_fusion.w0), channel_id=1, source_target_pairs={{0,24},{8,0},{16,8},{24,16},{1,25},{9,1},{17,9},{25,17},{2,26},{10... | collective-permute-start | bytes 2359304 | tf_op jit(solution)/shard_map/ppermute | solution.py:16
  83.9 12.1 %copy-start.5 = (bf16[2,3,256,256]{3,2,1,0:T(8,128)(2,1)}, bf16[2,3,256,256]{3,2,1,0:T(8,128)(2,1)S(1)}, u32[]{:S(2)}) copy-start(bf16[2,3,256,256]{3,2,1,0:T(8,128)(2,1)S(1)} %collective-permute-done.17.w3) | copy-start | bytes 2359300
  83.9 11.7 %collective-permute-start.18 = (bf16[3,256,256]{2,1,0:T(8,128)(2,1)S(1)}, bf16[3,256,256]{2,1,0:T(8,128)(2,1)S(1)}, u32[]{:S(2)}, u32[]{:S(2)}) collective-permute-start(bf16[3,256,256]{2,1,0:T(8,128)(2,1)S(1)} %slice_bitcast_fusion.1), channel_id=1, source_target_pairs={{0,8},{8,16},{16,24},{24,0},{1,9},{9,17},{17,25},{25,1},{2,10},{10... | collective-permute-start | bytes 1179656 | tf_op jit(solution)/shard_map/ppermute | solution.py:16
  84.0 11.9 %copy-start.6 = (bf16[2,3,256,256]{3,2,1,0:T(8,128)(2,1)}, bf16[2,3,256,256]{3,2,1,0:T(8,128)(2,1)S(1)}, u32[]{:S(2)}) copy-start(bf16[2,3,256,256]{3,2,1,0:T(8,128)(2,1)S(1)} %collective-permute-done.16.w1) | copy-start | bytes 2359300
  84.0 11.6 %collective-permute-start.19 = (bf16[3,256,256]{2,1,0:T(8,128)(2,1)S(1)}, bf16[3,256,256]{2,1,0:T(8,128)(2,1)S(1)}, u32[]{:S(2)}, u32[]{:S(2)}) collective-permute-start(bf16[3,256,256]{2,1,0:T(8,128)(2,1)S(1)} %slice_bitcast_fusion), channel_id=1, source_target_pairs={{0,24},{8,0},{16,8},{24,16},{1,25},{9,1},{17,9},{25,17},{2,26},{10... | collective-permute-start | bytes 1179656 | tf_op jit(solution)/shard_map/ppermute | solution.py:16
  95.6 0.8 copy-start.11
  95.6 0.9 copy-start.12
  102.1 42.9 %copy-start.1 = (bf16[512,256]{1,0:T(8,128)(2,1)S(1)}, bf16[512,256]{1,0:T(8,128)(2,1)}, u32[]{:S(2)}) copy-start(bf16[512,256]{1,0:T(8,128)(2,1)} %psi.1) | copy-start | bytes 786436
  117.9 27.1 %all-to-all-start.2 = ((f32[8,64,256]{2,1,0:T(8,128)}), f32[8,64,256]{2,1,0:T(8,128)S(1)}, u32[]{:S(2)}, u32[]{:S(2)}) async-start(f32[8,64,256]{2,1,0:T(8,128)} %get-tuple-element.44), calls=%async_computation.2 | async-start | bytes 1048576 | tf_op jit(solution)/shard_map/all_to_all | solution.py:217
  123.2 5.7 %collective-permute-start.22 = (f32[8,128]{1,0:T(8,128)S(1)}, f32[8,128]{1,0:T(8,128)S(1)}, u32[]{:S(2)}, u32[]{:S(2)}) collective-permute-start(f32[8,128]{1,0:T(8,128)S(1)} %get-tuple-element.45), channel_id=1, source_target_pairs={{0,24},{8,0},{16,8},{24,16},{1,25},{9,1},{17,9},{25,17},{2,26},{10... | collective-permute-start | bytes 12296 | tf_op jit(solution)/shard_map/ppermute | solution.py:16
  127.6 5.1 %collective-permute-start.21 = (f32[8,128]{1,0:T(8,128)S(1)}, f32[8,128]{1,0:T(8,128)S(1)}, u32[]{:S(2)}, u32[]{:S(2)}) collective-permute-start(f32[8,128]{1,0:T(8,128)S(1)} %get-tuple-element.45), channel_id=1, source_target_pairs={{0,16},{8,24},{16,0},{24,8},{1,17},{9,25},{17,1},{25,9},{2,18},{10... | collective-permute-start | bytes 12296 | tf_op jit(solution)/shard_map/ppermute | solution.py:16
  128.1 4.8 %collective-permute-start.20 = (f32[8,128]{1,0:T(8,128)S(1)}, f32[8,128]{1,0:T(8,128)S(1)}, u32[]{:S(2)}, u32[]{:S(2)}) collective-permute-start(f32[8,128]{1,0:T(8,128)S(1)} %get-tuple-element.45), channel_id=1, source_target_pairs={{0,8},{8,16},{16,24},{24,0},{1,9},{9,17},{17,25},{25,1},{2,10},{10... | collective-permute-start | bytes 12296 | tf_op jit(solution)/shard_map/ppermute | solution.py:16
  132.9 4.5 %collective-permute-start.23 = (f32[8,128]{1,0:T(8,128)S(1)}, f32[8,128]{1,0:T(8,128)S(1)}, u32[]{:S(2)}, u32[]{:S(2)}) collective-permute-start(f32[8,128]{1,0:T(8,128)S(1)} %add_add_fusion), channel_id=1, source_target_pairs={{0,2},{2,0},{4,6},{6,4},{1,3},{3,1},{5,7},{7,5},{8,10},{10,8},{12,... | collective-permute-start | bytes 12296 | tf_op jit(solution)/shard_map/ppermute | solution.py:220
  137.4 7.5 %collective-permute-start.24 = (f32[8,128]{1,0:T(8,128)S(1)}, f32[8,128]{1,0:T(8,128)S(1)}, u32[]{:S(2)}, u32[]{:S(2)}) collective-permute-start(f32[8,128]{1,0:T(8,128)S(1)} %add.22), channel_id=1, source_target_pairs={{0,4},{2,6},{4,0},{6,2},{1,5},{3,7},{5,1},{7,3},{8,12},{10,14},{12... | collective-permute-start | bytes 12296 | tf_op jit(solution)/shard_map/ppermute | solution.py:220
